TPU v7x, 32 devices: a whole 2x2x4 slice. The times are simulated.
32 devices in a mesh: wide: 16 (over z, y, x), narrow: 2 (over core).
Axes of the slice: x: 2, y: 2, z: 4, core: 2. Of those that a mesh axis runs over, the one named last changes fastest.
Arguments:
- tokens: bfloat16 [32, 1024, 576], P('wide', 'narrow'), may hold values from -6 to 6
- doc_starts: int32 [32, 8], P('wide'), may hold values from 0 to 1023, as said below
- skip_flags: int32 [32], P('wide'), may hold values 0 or 1
- cotangent: bfloat16 [32, 1024, 576], P('wide', 'narrow'), may hold values from -6 to 6
- attn_gain: bfloat16 [576], replicated, may hold values from 0.25 to 1.75
- w_query: bfloat16 [576, 576], replicated, may hold values from -0.25 to 0.25
- w_key: bfloat16 [576, 192], replicated, may hold values from -0.25 to 0.25
- w_value: bfloat16 [576, 192], replicated, may hold values from -0.25 to 0.25
- w_out: bfloat16 [576, 576], replicated, may hold values from -1.5 to 1.5
- mlp_gain: bfloat16 [576], replicated, may hold values from 0.25 to 1.75
- w_gate: bfloat16 [576, 1536], replicated, may hold values from -0.25 to 0.25
- w_up: bfloat16 [576, 1536], replicated, may hold values from -0.25 to 0.25
- w_down: bfloat16 [1536, 576], replicated, may hold values from -0.15625 to 0.15625
Outputs:
- mixed_out: bfloat16 [32, 1024, 576], P('wide', 'narrow')
- grad_tokens: bfloat16 [32, 1024, 576], P('wide', 'narrow')
- grad_attn_gain: float32 [576], replicated
- grad_w_query: float32 [576, 576], replicated
- grad_w_key: float32 [576, 192], replicated
- grad_w_value: float32 [576, 192], replicated
- grad_w_out: float32 [576, 576], replicated
- grad_mlp_gain: float32 [576], replicated
- grad_w_gate: float32 [576, 1536], replicated
- grad_w_up: float32 [576, 1536], replicated
- grad_w_down: float32 [1536, 576], replicated
Inputs may be any that keep to these rules, and one draw needn't show every extreme that they name: `doc_starts`: each row starts with 0, rises strictly and ends with 1023; no document begins at a position from 384 to 639.
All inputs are finite; a program needn't handle non-finite values. No bound on the sum of `skip_flags` on one device may be relied on, other than what follows from the above.
Results may differ from a plain program's by a relative error of at most 0.014.
Values may be sent and summed in bfloat16 or wider, within the bound.
No kernel may reach another device: no remote copies, remote signals or barrier semaphores. Data moves between devices by JAX's collectives and lax.ppermute only.
A program may use at most 192 MiB of HBM per device.

v0:
```python
import functools

import jax
import jax.numpy as jnp
import numpy as np
from jax import lax
from jax.experimental import pallas as pl
from jax.experimental.pallas import tpu as pltpu
from jax.sharding import PartitionSpec as P

HQ = 9
KVH = 3
HD = 64
GROUPS = HQ // KVH
PER = (GROUPS + 2) * HD
theta_base = 100000.0
eps_norm = 1e-05
masked_score = -1e30
BLOCK = 256
GAIN_ROWS = 16
VMEM = 60 * 2**20
f32 = jnp.float32
bf16 = jnp.bfloat16


def cost(microseconds):
    return pl.CostEstimate(flops=int(microseconds * 1.0e9), bytes_accessed=1024, transcendentals=0)


def dot(a, b, ca=1, cb=0):
    return lax.dot_general(a, b, (((ca,), (cb,)), ((), ())), preferred_element_type=f32)


def turn(rows, cosine, sine, sign):
    half = HD // 2
    first, second = rows[:half], rows[half:]
    if sign > 0:
        return jnp.concatenate([first * cosine - second * sine, second * cosine + first * sine], 0)
    return jnp.concatenate([first * cosine + second * sine, second * cosine - first * sine], 0)


def lanes_up(count):
    return -(-count // 128) * 128


ANY = pl.BlockSpec(memory_space=pl.ANY)


def without(kernel, inputs, after):
    return lambda *refs: kernel(*refs[:inputs], *refs[inputs + len(after) :])


def full(shape):
    return pl.BlockSpec(shape, lambda *_: (0,) * len(shape))


def widen(matrix):
    extra = lanes_up(matrix.shape[1]) - matrix.shape[1]
    return jnp.concatenate([matrix, jnp.zeros((matrix.shape[0], extra), matrix.dtype)], 1)


def pack_blocks(target, spot, matrix):
    for k in range(matrix.shape[1] // 128):
        target[spot : spot + matrix.shape[0]] = matrix[:, k * 128 : (k + 1) * 128]
        spot += matrix.shape[0]
    return spot


def pack_thin(target, spot, h, matrix):
    rows = matrix.shape[0]
    quarter = rows // 4
    base = matrix.shape[1] // 128
    for k in range(h * base // 2, (h + 1) * base // 2):
        target[spot : spot + rows] = matrix[:, k * 128 : (k + 1) * 128]
        spot += rows
    left = matrix[2 * h * quarter : (2 * h + 1) * quarter, base * 128 :]
    right = matrix[(2 * h + 1) * quarter : (2 * h + 2) * quarter, base * 128 :]
    target[spot : spot + quarter] = jnp.concatenate([left, right], 1)
    return spot + quarter


def unpack_thin(target, first, second, spot):
    rows, width = target.shape
    quarter = rows // 4
    base = width // 128
    for h, source in enumerate((first, second)):
        at = spot
        for k in range(h * base // 2, (h + 1) * base // 2):
            target[:, k * 128 : (k + 1) * 128] = source[at : at + rows].astype(f32)
            at += rows
        last = source[at : at + quarter].astype(f32)
        target[2 * h * quarter : (2 * h + 1) * quarter, base * 128 :] = last[:, : width - base * 128]
        target[(2 * h + 1) * quarter : (2 * h + 2) * quarter, base * 128 :] = last[:, width - base * 128 :]


def prelude_kernel(wq_ref, wkt_ref, wvt_ref, w_out_ref, gain_one_ref, gain_two_ref, t_ref, n_ref, out_t_ref, g1_ref, g2_ref, line_ref):
    q_cols = GROUPS * HD
    wqt = wq_ref[...].T
    for g in range(KVH):
        t_ref[g * PER : g * PER + q_cols] = wqt[g * q_cols : (g + 1) * q_cols]
        t_ref[g * PER + q_cols : g * PER + q_cols + HD] = wkt_ref[g * HD : (g + 1) * HD]
        t_ref[g * PER + q_cols + HD : (g + 1) * PER] = wvt_ref[g * HD : (g + 1) * HD]
    n_ref[...] = t_ref[...].T
    out_t_ref[...] = w_out_ref[...].T
    for source, target in ((gain_one_ref, g1_ref), (gain_two_ref, g2_ref)):
        gain = source[...].astype(f32).reshape(1, source.shape[0])
        target[...] = jnp.broadcast_to(gain, (128, source.shape[0])).T
    line_ref[...] = gain_one_ref[...].astype(f32).reshape(line_ref.shape)


def prelude(wq, wkt, wvt, w_out, gain_one, gain_two):
    width = wq.shape[0]
    return pl.pallas_call(
        prelude_kernel,
        out_shape=[
            jax.ShapeDtypeStruct((KVH * PER, width), bf16),
            jax.ShapeDtypeStruct((width, KVH * PER), bf16),
            jax.ShapeDtypeStruct((width, w_out.shape[0]), bf16),
            jax.ShapeDtypeStruct((width, 128), f32),
            jax.ShapeDtypeStruct((width, 128), f32),
            jax.ShapeDtypeStruct((1, width), f32),
        ],
        compiler_params=pltpu.CompilerParams(vmem_limit_bytes=VMEM),
        name="prelude",
        cost_estimate=cost(4),
    )(wq, wkt, wvt, w_out, gain_one, gain_two)


def layer_kernel(
    place_ref, skip_ref, own_ref, other_ref, cot_own_ref, cot_other_ref,
    gain_one_ref, wqkv_ref, w_out_t_ref, gain_two_ref, cos_ref, sin_ref, start_ref,
    w_out_ref, w_gate_hbm, w_up_hbm, w_down_hbm,
    qt_ref, kt_ref, vn_ref, soft_hbm, n1_ref,
    res_own_ref, res_away_ref, gh_ref, dot_ref, delta_ref, keep_a_hbm, send_a_hbm, keep_b_hbm, send_b_hbm,
    kn_all, vt_all, mixed_sc, n2t_sc, gt_sc, inner_sc, grads_sc, in_t_sc, down_sc, ga_sc, dgain_sc,
    scale_sc, soft_sc, w_gate_ref, w_up_ref, w_down_ref, pack_sc, weight_sem, soft_sem, pack_sem,
):
    step = pl.program_id(0)
    mine = (step >= 2).astype(jnp.int32) == place_ref[0]
    width = other_ref.shape[0]
    cols = w_gate_hbm.shape[1]

    weight_copies = [
        pltpu.make_async_copy(source, target, weight_sem.at[k])
        for k, (source, target) in enumerate(
            ((w_gate_hbm, w_gate_ref), (w_up_hbm, w_up_ref), (w_down_hbm, w_down_ref))
        )
    ]

    @pl.when(step == 0)
    def _():
        for copy in weight_copies:
            copy.start()
        dgain_sc[...] = jnp.zeros_like(dgain_sc)

    low = jnp.where(mine, own_ref[0], other_ref[...])
    x = low.astype(f32)
    cot = jnp.where(mine, cot_own_ref[0], cot_other_ref[...])
    g = jnp.where(skip_ref[place_ref[0]] == 1, jnp.zeros_like(cot), cot)
    gt_sc[step] = g
    inverse = lax.rsqrt(jnp.mean(x * x, 0, keepdims=True) + eps_norm)
    n1 = (x * inverse * gain_one_ref[:, :1]).astype(bf16)
    n1_ref[...] = widen(n1.T)
    qkv = dot(wqkv_ref[...], n1)
    cosine, sine = cos_ref[...], sin_ref[...]
    here = pl.ds(pl.multiple_of(step * BLOCK, BLOCK), BLOCK)
    for group in range(KVH):
        for r in range(GROUPS):
            head = group * GROUPS + r
            base = group * PER + r * HD
            rows = (turn(qkv[base : base + HD], cosine, sine, 1) * (HD**-0.5)).astype(bf16)
            qt_ref[head * HD : (head + 1) * HD] = rows
        base = group * PER + GROUPS * HD
        rows = turn(qkv[base : base + HD], cosine, sine, 1).astype(bf16)
        kt_ref[group * HD : (group + 1) * HD] = rows
        kn_all[group, here] = rows.T
        rows = qkv[base + HD : base + 2 * HD].astype(bf16)
        vt_all[step, group] = jnp.concatenate([rows, jnp.ones((16, BLOCK), bf16)], 0)
        vn_ref[group] = rows.T

    pos = step * BLOCK + lax.broadcasted_iota(jnp.int32, (1, BLOCK), 1)
    start_row = jnp.zeros((1, BLOCK), jnp.int32)
    for k in range(start_ref.shape[1]):
        first = start_ref[place_ref[0], k]
        start_row = jnp.where(pos >= first, first, start_row)

    def soft_copy(count):
        used = pl.ds(0, count * BLOCK)
        return pltpu.make_async_copy(soft_sc.at[:, used], soft_hbm.at[count - 1, :, used], soft_sem)

    def attend(count):
        t = lax.broadcasted_iota(jnp.int32, (BLOCK, BLOCK), 0)
        s_pos = lax.broadcasted_iota(jnp.int32, (BLOCK, BLOCK), 1)
        if count > 1:
            soft_copy(count - 1).wait()

        def one_group(group, carry):
            def scores_of(r):
                rows = pl.ds(pl.multiple_of((group * GROUPS + r) * HD, HD), HD)
                q = qt_ref[rows]
                scores = []
                for kb in range(count):
                    s = dot(kn_all[group, kb * BLOCK : (kb + 1) * BLOCK], q)
                    ok = t + kb * BLOCK >= start_row
                    if kb == count - 1:
                        ok = ok & (t <= s_pos)
                    scores.append(jnp.where(ok, s, masked_score))
                return scores

            def finish(r, scores):
                head = group * GROUPS + r
                rows = pl.ds(pl.multiple_of(head * HD, HD), HD)
                peak = scores[0].max(0, keepdims=True)
                for s in scores[1:]:
                    peak = jnp.maximum(peak, s.max(0, keepdims=True))
                out = None
                for kb in range(count):
                    p = jnp.exp(scores[kb] - peak).astype(bf16)
                    soft_sc[head, kb * BLOCK : (kb + 1) * BLOCK] = p
                    term = dot(vt_all[kb, group], p)
                    out = term if out is None else out + term
                scale = 1.0 / out[HD : HD + 1]
                scale_sc[head] = jnp.broadcast_to(scale, scale_sc.shape[1:])
                mixed_sc[step, rows] = (out[:HD] * scale).astype(bf16)

            every = [scores_of(r) for r in range(GROUPS)]
            for r in range(GROUPS):
                finish(r, every[r])
            return carry

        lax.fori_loop(0, KVH, one_group, 0)
        soft_copy(count).start()

    for count in range(1, 5):
        pl.when(step == count - 1)(lambda count=count: attend(count))

    @pl.when(step == 0)
    def _():
        for copy in weight_copies:
            copy.wait()
        for k, ref in enumerate((w_gate_ref, w_up_ref)):
            in_t_sc[k * cols : (k + 1) * cols] = widen(ref[...].T)
        down_sc[...] = widen(w_down_ref[...].T)

    mixed = mixed_sc[step]
    hidden = x + dot(w_out_t_ref[...], mixed)
    inverse = lax.rsqrt(jnp.mean(hidden * hidden, 0, keepdims=True) + eps_norm)
    normed = hidden * inverse
    n2t = (normed * gain_two_ref[:, :1]).astype(bf16)
    n2t_sc[step] = n2t
    n2 = n2t.T
    gn = g.T

    def chunk(k, carry):
        work = []
        for c in range(3):
            at = pl.ds(pl.multiple_of((3 * k + c) * BLOCK, BLOCK), BLOCK)
            at_up = pl.ds(pl.multiple_of(cols + (3 * k + c) * BLOCK, BLOCK), BLOCK)
            work.append((at, at_up, dot(n2, w_gate_ref[:, at]), dot(n2, w_up_ref[:, at]), dot(gn, w_down_ref[:, at])))
        for at, at_up, gate, up, grad_inner in work:
            sig = jax.nn.sigmoid(gate)
            act = gate * sig
            inner_sc[here, at] = (act * up).astype(bf16)
            grads_sc[here, at] = (grad_inner * up * (sig + act * (1.0 - sig))).astype(bf16)
            grads_sc[here, at_up] = (grad_inner * act).astype(bf16)
        return carry

    lax.fori_loop(0, cols // BLOCK // 3, chunk, 0)
    result = hidden + dot(inner_sc[here], down_sc[...]).T[:width]
    result = jnp.where(skip_ref[place_ref[0]] == 1, low, result.astype(bf16))

    @pl.when(mine)
    def _():
        res_own_ref[0] = result

    @pl.when(jnp.logical_not(mine))
    def _():
        res_away_ref[...] = result

    gn2 = dot(grads_sc[here], in_t_sc[...]).T[:width]
    c = gn2 * gain_two_ref[:, :1]
    dgain_sc[:, :1] += jnp.sum(gn2 * normed, 1, keepdims=True)
    gh = g.astype(f32) + inverse * (c - normed * jnp.mean(c * normed, 0, keepdims=True))
    gh_ref[...] = gh
    ga = gh.astype(bf16)
    ga_sc[here] = widen(ga.T)
    back_t = dot(w_out_ref[...], ga)
    for head in range(HQ):
        rows = (back_t[head * HD : (head + 1) * HD] * scale_sc[head, 0:1]).astype(bf16)
        dot_ref[head * HD : (head + 1) * HD] = rows
        delta_ref[head // GROUPS, head % GROUPS : head % GROUPS + 1] = jnp.sum(
            rows.astype(f32) * mixed[head * HD : (head + 1) * HD].astype(f32), 0, keepdims=True
        )

    @pl.when(step == pl.num_programs(0) - 1)
    def _():
        blocks = mixed_sc.shape[0]
        whole = lambda ref: jnp.concatenate([ref[k] for k in range(blocks)], 1)
        n2t_all, gt_all = whole(n2t_sc), whole(gt_sc)
        dw_out = dot(whole(mixed_sc), ga_sc[...])[:, :width].astype(bf16)
        line = dgain_sc[...].T[0:1]
        line = jnp.concatenate([line, jnp.zeros((1, lanes_up(width) - width), f32)], 1)
        lines = [line[:, k * 128 : (k + 1) * 128] for k in range(line.shape[1] // 128)]
        lines.append(jnp.zeros((GAIN_ROWS - len(lines), 128), f32))
        gain_rows = jnp.concatenate(lines, 0).astype(bf16)
        thin = 9 * width
        for h in range(2):
            target = pack_sc.at[2 + h]
            spot = pack_thin(target, thin, h, dw_out)
            target[spot : spot + GAIN_ROWS] = gain_rows

        def one_chunk(k, carry):
            at = pl.ds(pl.multiple_of(k * BLOCK, BLOCK), BLOCK)
            at_up = pl.ds(pl.multiple_of(cols + k * BLOCK, BLOCK), BLOCK)
            chain = jnp.where(k >= 3, 1, 0)
            third = k - 3 * chain
            for m, (left, right) in enumerate(
                ((n2t_all, grads_sc[:, at]), (n2t_all, grads_sc[:, at_up]), (gt_all, inner_sc[:, at]))
            ):
                both = dot(left, right).astype(bf16)
                for b in range(2):
                    half = jnp.where(third == 2, b, third)
                    spot = (3 * m + jnp.where(third == 2, 2, b)) * width
                    pack_sc[2 * chain + half, pl.ds(pl.multiple_of(spot, 16), width)] = both[:, b * 128 : (b + 1) * 128]
            for q in range(4):
                keep, send = pack_copies[q]
                pl.when((k == 3 * (q // 2) + 2) & (place_ref[0] == q % 2))(keep.start)
                pl.when((k == 3 * (q // 2) + 2) & (place_ref[0] != q % 2))(send.start)
            return carry

        pack_copies = []
        for q in range(4):
            targets = (keep_a_hbm, send_a_hbm) if q < 2 else (keep_b_hbm, send_b_hbm)
            source = pack_sc.at[q, pl.ds(0, targets[0].shape[0])]
            pack_copies.append([pltpu.make_async_copy(source, target, pack_sem.at[q]) for target in targets])
        lax.fori_loop(0, 6, one_chunk, 0)
        for keep, _ in pack_copies:
            keep.wait()
        soft_copy(blocks).wait()


def own_specs(width, near):
    own = pl.BlockSpec((1, width, BLOCK), lambda i, c, s: (c[0], 0, jnp.where(i >= near, i - near, i)))
    oth = pl.BlockSpec((width, BLOCK), lambda i, c, s: (0, jnp.where(i >= near, i - near, i)))
    return own, oth


def out_specs_halves(width, near):
    mine = pl.BlockSpec((1, width, BLOCK), lambda i, c, s: (c[0], 0, jnp.clip(i - near * c[0], 0, near - 1)))
    away = pl.BlockSpec((width, BLOCK), lambda i, c, s: (0, jnp.clip(i - near * (1 - c[0]), 0, near - 1)))
    return mine, away


def layer(
    rows_a, rows_b, place, skip, tokens, other, cot, cot_other, gain_one, wqkv_t, w_out_t, gain_two, cos_t, sin_t,
    starts, w_out, wg, wu, wdt,
):
    rows = 2 * tokens.shape[2]
    width = tokens.shape[1]
    cols = wg.shape[1]
    wide = lanes_up(width)
    blocks = rows // BLOCK
    own, oth = own_specs(width, blocks // 2)
    col = pl.BlockSpec((width, BLOCK), lambda i, c, s: (0, i))
    row_wide = pl.BlockSpec((BLOCK, wide), lambda i, c, s: (i, 0))
    small = pl.BlockSpec((HD // 2, BLOCK), lambda i, c, s: (0, i))
    const = lambda array: pl.BlockSpec(
        array.shape, lambda *_: (0,) * array.ndim, pipeline_mode=pl.Buffered(1)
    )
    any_spec = pl.BlockSpec(memory_space=pl.ANY)
    halves = [(rows_a, 128), (rows_a, 128), (rows_b, 128), (rows_b, 128)]
    out_shape = [
        jax.ShapeDtypeStruct((HQ * HD, rows), bf16),
        jax.ShapeDtypeStruct((KVH * HD, rows), bf16),
        jax.ShapeDtypeStruct((KVH, rows, HD), bf16),
        jax.ShapeDtypeStruct((blocks, HQ, rows, BLOCK), bf16),
        jax.ShapeDtypeStruct((rows, wide), bf16),
        jax.ShapeDtypeStruct((2, width, rows // 2), bf16),
        jax.ShapeDtypeStruct((width, rows // 2), bf16),
        jax.ShapeDtypeStruct((width, rows), f32),
        jax.ShapeDtypeStruct((HQ * HD, rows), bf16),
        jax.ShapeDtypeStruct((KVH, GROUPS, rows), f32),
    ] + [jax.ShapeDtypeStruct(shape, bf16) for shape in halves]
    return pl.pallas_call(
        layer_kernel,
        grid_spec=pltpu.PrefetchScalarGridSpec(
            num_scalar_prefetch=2,
            grid=(blocks,),
            in_specs=[
                own, oth, own, oth, const(gain_one), const(wqkv_t), const(w_out_t), const(gain_two),
                small, small, pl.BlockSpec(memory_space=pltpu.SMEM),
                const(w_out), any_spec, any_spec, any_spec,
            ],
            out_specs=[
                col,
                pl.BlockSpec((KVH * HD, BLOCK), lambda i, c, s: (0, i)),
                pl.BlockSpec((KVH, BLOCK, HD), lambda i, c, s: (0, i, 0)),
                any_spec,
                row_wide,
                *out_specs_halves(width, blocks // 2),
                col, col,
                pl.BlockSpec((KVH, GROUPS, BLOCK), lambda i, c, s: (0, 0, i)),
            ] + [any_spec] * 4,
            scratch_shapes=[
                pltpu.VMEM((KVH, rows, HD), bf16),
                pltpu.VMEM((blocks, KVH, HD + 16, BLOCK), bf16),
                pltpu.VMEM((blocks, HQ * HD, BLOCK), bf16),
                pltpu.VMEM((blocks, width, BLOCK), bf16),
                pltpu.VMEM((blocks, width, BLOCK), bf16),
                pltpu.VMEM((rows, cols), bf16),
                pltpu.VMEM((rows, 2 * cols), bf16),
                pltpu.VMEM((2 * cols, wide), bf16),
                pltpu.VMEM((cols, wide), bf16),
                pltpu.VMEM((rows, wide), bf16),
                pltpu.VMEM((width, 128), f32),
                pltpu.VMEM((HQ, 8, BLOCK), f32),
                pltpu.VMEM((HQ, rows, BLOCK), bf16),
                pltpu.VMEM(wg.shape, bf16),
                pltpu.VMEM(wu.shape, bf16),
                pltpu.VMEM(wdt.shape, bf16),
                pltpu.VMEM((4, rows_b, 128), bf16),
                pltpu.SemaphoreType.DMA((3,)),
                pltpu.SemaphoreType.DMA,
                pltpu.SemaphoreType.DMA((4,)),
            ],
        ),
        out_shape=out_shape,
        compiler_params=pltpu.CompilerParams(vmem_limit_bytes=VMEM),
        name="layer_forward",
        cost_estimate=cost(50),
    )(
        place, skip, tokens, other, cot, cot_other, gain_one, wqkv_t, w_out_t, gain_two, cos_t, sin_t, starts,
        w_out, wg, wu, wdt,
    )


def back_kernel(
    g, place_ref, soft_ref, qt_ref, kt_ref, vn_ref, dot_ref, delta_ref, cos_ref, sin_ref, n1_ref,
    dqkv_ref, keep_hbm, send_hbm,
    acc, ds_sc, pack_sc, pack_sem,
):
    step = pl.program_id(0)
    blocks = pl.num_programs(0)
    cosine, sine = cos_ref[...], sin_ref[...]

    @pl.when(step == 0)
    def _():
        acc[...] = jnp.zeros_like(acc)

    def attend(count):
        used = slice(0, count * BLOCK)
        here = slice((count - 1) * BLOCK, count * BLOCK)
        ups = [dot_ref[r * HD : (r + 1) * HD] for r in range(GROUPS)]
        soft_grads = [[dot(vn_ref[0, kb * BLOCK : (kb + 1) * BLOCK], up) for kb in range(count)] for up in ups]
        for r in range(GROUPS):
            rows = slice(r * HD, (r + 1) * HD)
            delta = delta_ref[0, r : r + 1]
            pair = jnp.concatenate([qt_ref[rows], ups[r]], 0).T
            left = lax.broadcasted_iota(jnp.int32, pair.shape, 1) < HD
            zero = jnp.zeros_like(pair)
            pads = jnp.concatenate([jnp.where(left, pair, zero), jnp.where(left, zero, pair)], 0)
            for kb in range(count):
                span = slice(kb * BLOCK, (kb + 1) * BLOCK)
                p = soft_ref[0, r, span]
                ds_sc[r, span, :BLOCK] = (p.astype(f32) * (soft_grads[r][kb] - delta)).astype(bf16)
                ds_sc[r, span, BLOCK:] = p
            acc[used] += dot(ds_sc[r, used], pads)
            dq = dot(kt_ref[:, used], ds_sc[r, used, :BLOCK])
            dqkv_ref[rows, here] = turn(dq * (HD**-0.5), cosine, sine, -1).astype(bf16)
        done = acc[here].T
        base = GROUPS * HD
        dqkv_ref[base : base + HD, here] = turn(done[:HD], cosine, sine, -1).astype(bf16)
        dqkv_ref[base + HD : base + 2 * HD, here] = done[HD:].astype(bf16)

    for count in range(1, 5):
        pl.when(step == 4 - count)(lambda count=count: attend(count))

    @pl.when(step == blocks - 1)
    def _():
        width = pack_sc.shape[1] * 128 * 2 // PER
        dw = dot(dqkv_ref[...], n1_ref[...])[:, :width].astype(bf16)
        span = pl.ds(g * pack_sc.shape[1], pack_sc.shape[1])
        copies = []
        for h in range(2):
            pack_thin(pack_sc.at[h], 0, h, dw)
            copies.append([pltpu.make_async_copy(pack_sc.at[h], t.at[span], pack_sem.at[h]) for t in (keep_hbm, send_hbm)])
            pl.when(place_ref[0] == h)(copies[h][0].start)
            pl.when(place_ref[0] != h)(copies[h][1].start)
        for keep, _ in copies:
            keep.wait()


def back(g, half_rows, width, place, soft, qt, kt, vn, dot_t, delta, cos_t, sin_t, n1, packed, after=()):
    blocks, _, rows, _ = soft.shape
    last = blocks - 1
    small = pl.BlockSpec((HD // 2, BLOCK), lambda i, c: (0, last - i))
    inputs = 10
    return pl.pallas_call(
        without(functools.partial(back_kernel, g), inputs, tuple(packed) + tuple(after)),
        grid_spec=pltpu.PrefetchScalarGridSpec(
            num_scalar_prefetch=1,
            grid=(blocks,),
            in_specs=[
                pl.BlockSpec((1, GROUPS, rows, BLOCK), lambda i, c: (last - i, g, 0, 0)),
                pl.BlockSpec((GROUPS * HD, BLOCK), lambda i, c: (g, last - i)),
                pl.BlockSpec((HD, rows), lambda i, c: (g, 0)),
                pl.BlockSpec((1, rows, HD), lambda i, c: (g, 0, 0)),
                pl.BlockSpec((GROUPS * HD, BLOCK), lambda i, c: (g, last - i)),
                pl.BlockSpec((1, GROUPS, BLOCK), lambda i, c: (g, 0, last - i)),
                small, small, full(n1.shape),
            ] + [ANY] * (len(packed) + len(after)),
            out_specs=[full((PER, rows)), ANY, ANY],
            scratch_shapes=[
                pltpu.VMEM((rows, 2 * HD), f32),
                pltpu.VMEM((GROUPS, rows, 2 * BLOCK), bf16),
                pltpu.VMEM((2, PER * width // 256, 128), bf16),
                pltpu.SemaphoreType.DMA((2,)),
            ],
        ),
        out_shape=[jax.ShapeDtypeStruct((PER, rows), bf16)] + [jax.ShapeDtypeStruct((half_rows, 128), bf16)] * 2,
        input_output_aliases={inputs + k: 1 + k for k in range(len(packed))},
        compiler_params=pltpu.CompilerParams(vmem_limit_bytes=VMEM),
        name="attention_backward",
        cost_estimate=cost(9),
    )(place, soft, qt, kt, vn, dot_t, delta, cos_t, sin_t, n1, *packed, *after)


def last_kernel(
    place_ref, skip_ref, x_ref, cot_ref, gh_ref, d0_ref, d1_ref, d2_ref, wqkv_ref, gain_one_ref, grad_ref,
):
    x = x_ref[...].reshape(gh_ref.shape).astype(f32)
    skipped = skip_ref[place_ref[0]] == 1
    inverse = lax.rsqrt(jnp.mean(x * x, 0, keepdims=True) + eps_norm)
    normed = x * inverse
    dqkv = jnp.concatenate([d0_ref[...], d1_ref[...], d2_ref[...]], 0)
    c = dot(wqkv_ref[...], dqkv) * gain_one_ref[:, :1]
    gx = gh_ref[...] + inverse * (c - normed * jnp.mean(c * normed, 0, keepdims=True))
    gx = jnp.where(skipped, cot_ref[...].reshape(gh_ref.shape), gx.astype(bf16))
    grad_ref[...] = gx.reshape(grad_ref.shape)


def last(mine, place, skip, x, cot, gh, parts, wqkv_n, gain_one, after=()):
    width, rows = gh.shape
    near = rows // BLOCK // 2
    if mine:
        source = pl.BlockSpec((1, width, BLOCK), lambda i, c, s: (c[0], 0, i))
        at = lambda i, c, s: (0, near * c[0] + i)
    else:
        source = pl.BlockSpec((width, BLOCK), lambda i, c, s: (0, i))
        at = lambda i, c, s: (0, near * (1 - c[0]) + i)
    col = pl.BlockSpec((width, BLOCK), at)
    part = pl.BlockSpec((PER, BLOCK), at)
    return pl.pallas_call(
        without(last_kernel, 10, after),
        grid_spec=pltpu.PrefetchScalarGridSpec(
            num_scalar_prefetch=2,
            grid=(near,),
            in_specs=[source, source, col, part, part, part, full(wqkv_n.shape), full((width, 128))]
            + [ANY] * len(after),
            out_specs=source,
        ),
        out_shape=jax.ShapeDtypeStruct(x.shape, bf16),
        compiler_params=pltpu.CompilerParams(vmem_limit_bytes=VMEM),
        name="input_backward",
        cost_estimate=cost(4),
    )(place, skip, x, cot, gh, *parts, wqkv_n, gain_one, *after)


def rotary_rows(rows):
    frequency = theta_base ** (-2.0 * np.arange(HD // 2, dtype=np.float64) / HD)
    angles = frequency[:, None] * np.arange(rows, dtype=np.float64)[None, :]
    return np.cos(angles).astype(np.float32), np.sin(angles).astype(np.float32)


def swap_core(array):
    return lax.ppermute(array, "narrow", [(0, 1), (1, 0)])


def axis_orders(bits, turn_index):
    if bits == 4:
        return (((0, 1, 2, 3), (1, 2, 3, 0)), ((1, 0, 2, 3), (2, 3, 0, 1)), ((0, 1, 2, 3), (1, 0, 2, 3)))[turn_index]
    base = tuple(range(bits))
    shift = bits // 2
    return base, base[shift:] + base[:shift]


class Summer:
    def __init__(self, core, chips, turn_index, exchanges):
        self.core = core
        self.chips = chips
        self.bits = chips.bit_length() - 1
        self.halvings = self.bits - exchanges
        self.orders = axis_orders(self.bits, turn_index)
        self.place = lax.axis_index("wide")
        self.stage = 0

    def bit(self, step):
        by_core = [(self.place >> order[step]) & 1 for order in self.orders]
        return jnp.where(self.core == 0, by_core[0], by_core[1])

    def swap(self, array, step):
        pairs = [
            (2 * chip + c, 2 * (chip ^ (1 << self.orders[c][step])) + c) for chip in range(self.chips) for c in range(2)
        ]
        return lax.ppermute(array, ("wide", "narrow"), pairs)

    def first(self, keep, send):
        self.keep, self.got = keep, swap_core(send)

    def advance(self, line):
        if line.last is not None:
            self.keep, self.got, _ = lax.optimization_barrier((self.keep, self.got, line.last))
        if self.stage < self.halvings:
            bit = self.bit(self.stage)
            half = self.keep.shape[0] // 2

            def part(which):
                a = lax.dynamic_slice_in_dim(self.keep, which * half, half, 0).astype(f32)
                b = lax.dynamic_slice_in_dim(self.got, which * half, half, 0).astype(f32)
                return (a + b).astype(bf16)

            line.last = part(1 - bit)
            self.keep, self.got = part(bit), self.swap(line.last, self.stage)
        elif self.stage <= self.bits:
            line.last = self.keep = (self.keep.astype(f32) + self.got.astype(f32)).astype(bf16)
            axis = self.stage if self.stage < self.bits else self.halvings - 1
            self.got = self.swap(self.keep, axis)
        else:
            step = self.halvings + self.bits - self.stage
            low = self.bit(step) == 0
            line.last = self.keep = jnp.where(
                low, jnp.concatenate([self.keep, self.got], 0), jnp.concatenate([self.got, self.keep], 0)
            )
            self.got = self.swap(self.keep, step - 1) if step else swap_core(self.keep)
        self.stage += 1

    @property
    def done(self):
        return self.stage > self.bits + self.halvings


class Line:
    last = None

    def after(self):
        return () if self.last is None else (self.last,)

    def both_halves(self, core, own, got):
        own, got, _ = lax.optimization_barrier((own, got, self.last))
        result = lax.dynamic_update_slice_in_dim(own, got[None], 1 - core, 0)
        self.last = got
        return result


def unpack_kernel(chain, place_ref, own, got, *refs):
    gate_ref, up_ref, down_ref = refs[-5:-2] if chain else refs
    step = pl.program_id(0)
    width = gate_ref.shape[0]

    def take(halves):
        for third in range(3):
            blocks = ((halves[0], 2), (halves[1], 2)) if third == 2 else ((halves[third], 0), (halves[third], 1))

            @pl.when(step == third)
            def _():
                for m, target in enumerate((gate_ref, up_ref, down_ref)):
                    for b, (source, place) in enumerate(blocks):
                        spot = (3 * m + place) * width
                        target[:, b * 128 : (b + 1) * 128] = source[spot : spot + width].astype(f32)

    pl.when(place_ref[0] == 0)(lambda: take((own, got)))
    pl.when(place_ref[0] != 0)(lambda: take((got, own)))

    if chain:
        w_out_ref, gain_ref = refs[-2:]

        def take_rest(first, second):
            spot = 9 * width
            unpack_thin(w_out_ref, first, second, spot)
            spot += width // 128 // 2 * width + width // 4
            rows = first[spot : spot + GAIN_ROWS].astype(f32)
            line = jnp.concatenate([rows[k : k + 1] for k in range(lanes_up(width) // 128)], 1)
            gain_ref[...] = line[:, :width].reshape(width)

        pl.when((step == 0) & (place_ref[0] == 0))(lambda: take_rest(own, got))
        pl.when((step == 0) & (place_ref[0] != 0))(lambda: take_rest(got, own))


def unpack(chain, place, buffers, width, inner, earlier):
    spec = pl.BlockSpec((width, BLOCK), lambda i, c: (0, 3 * chain + i))
    out_specs = [spec, spec, spec]
    out_shape = [jax.ShapeDtypeStruct((width, inner), f32)] * 3
    if chain:
        out_specs += [full((HQ * HD, width)), full((width,))]
        out_shape += [jax.ShapeDtypeStruct((HQ * HD, width), f32), jax.ShapeDtypeStruct((width,), f32)]
    return pl.pallas_call(
        functools.partial(unpack_kernel, chain),
        grid_spec=pltpu.PrefetchScalarGridSpec(
            num_scalar_prefetch=1,
            grid=(3,),
            in_specs=[full(b.shape) for b in buffers] + [ANY] * len(earlier),
            out_specs=out_specs,
        ),
        out_shape=out_shape,
        input_output_aliases={3 + k: k for k in range(len(earlier))},
        compiler_params=pltpu.CompilerParams(vmem_limit_bytes=VMEM),
        name="unpack_mlp",
        cost_estimate=cost(4),
    )(place, *buffers, *earlier)


def unpack_last_kernel(place_ref, own_ref, got_ref, wqkv_ref, gain_one_ref, dq_ref, dkt_ref, dvt_ref, gain_ref, all_sc):
    q_cols = GROUPS * HD

    def take(first, second):
        for g in range(KVH):
            unpack_thin(all_sc.at[g * PER : (g + 1) * PER], first, second, g * PER * all_sc.shape[1] // 256)

    pl.when(place_ref[0] == 0)(lambda: take(own_ref, got_ref))
    pl.when(place_ref[0] != 0)(lambda: take(got_ref, own_ref))
    both = all_sc[...]
    dq = []
    for g in range(KVH):
        dq.append(both[g * PER : g * PER + q_cols])
        dkt_ref[g * HD : (g + 1) * HD] = both[g * PER + q_cols : g * PER + q_cols + HD]
        dvt_ref[g * HD : (g + 1) * HD] = both[g * PER + q_cols + HD : (g + 1) * PER]
    dq_ref[...] = jnp.concatenate(dq, 0).T
    gain = jnp.sum(both * wqkv_ref[...].astype(f32), 0, keepdims=True) / gain_one_ref[...]
    gain_ref[...] = gain.reshape(gain_ref.shape)


def unpack_last(place, own, got, wqkv_t, gain_one, after):
    width = wqkv_t.shape[1]
    shapes = [(width, HQ * HD), (KVH * HD, width), (KVH * HD, width), (width,)]
    return pl.pallas_call(
        without(unpack_last_kernel, 5, after),
        grid_spec=pltpu.PrefetchScalarGridSpec(
            num_scalar_prefetch=1,
            grid=(1,),
            in_specs=[full(own.shape)] * 2 + [full(wqkv_t.shape), full((1, width))] + [ANY] * len(after),
            out_specs=[full(shape) for shape in shapes],
            scratch_shapes=[pltpu.VMEM(wqkv_t.shape, f32)],
        ),
        out_shape=[jax.ShapeDtypeStruct(shape, f32) for shape in shapes],
        compiler_params=pltpu.CompilerParams(vmem_limit_bytes=VMEM),
        name="unpack_attention",
        cost_estimate=cost(3),
    )(place, own, got, wqkv_t, gain_one, *after)


def flip(array):
    return jnp.swapaxes(array, -1, -2)


def per_device(tokens, doc_starts, skip_flags, cotangent, attn_gain, wq, wk, wv, w_out, mlp_gain, wg, wu, wd):
    core = lax.axis_index("narrow")
    chips = lax.axis_size("wide")
    tokens, cotangent = flip(tokens), flip(cotangent)
    rows = 2 * tokens.shape[2]
    width = tokens.shape[1]
    inner = wg.shape[1]
    place = core.astype(jnp.int32).reshape(1)
    skip = skip_flags
    other = swap_core(lax.dynamic_index_in_dim(tokens, 1 - core, 0, keepdims=False))
    cot_other = swap_core(lax.dynamic_index_in_dim(cotangent, 1 - core, 0, keepdims=False))
    cos_t, sin_t = rotary_rows(rows)
    wdt = flip(wd)
    wqkv_t, wqkv_n, w_out_t, gain_one, gain_two, gain_line = prelude(wq, flip(wk), flip(wv), w_out, attn_gain, mlp_gain)
    unit = 16 * chips

    def half_rows(count):
        return -(-count // unit) * unit

    mlp_rows = 3 * width * inner // 4 // 128
    thin = width // 128 // 2
    out_rows = thin * HQ * HD + HQ * HD // 4 + GAIN_ROWS
    rest_rows = thin * KVH * PER + KVH * PER // 4

    (
        qt, kt, vn, soft, n1, res_own, res_away, gh, dot_t, delta, keep_a, send_a, keep_b, send_b,
    ) = layer(
        half_rows(mlp_rows), half_rows(mlp_rows + out_rows),
        place, skip, tokens, other, cotangent, cot_other, gain_one, wqkv_t, w_out_t, gain_two, cos_t, sin_t,
        doc_starts, w_out, wg, wu, wdt,
    )
    a_sum, b_sum, c_sum = (Summer(core, chips, k, exchanges) for k, exchanges in ((0, 0), (1, 0), (2, 2)))
    a_sum.first(keep_a, send_a)
    b_sum.first(keep_b, send_b)
    line = Line()
    parts, packed = [], ()
    for g in range(KVH):
        part, *packed = back(
            g, half_rows(rest_rows), width, place, soft, qt, kt, vn, dot_t, delta, cos_t, sin_t, n1, packed, line.after()
        )
        parts.append(part)
        line.last = part
        if g == KVH - 1:
            c_sum.first(*packed)
        a_sum.advance(line)
        b_sum.advance(line)
    grad_away = last(False, place, skip, other, cot_other, gh, parts, wqkv_n, gain_one, line.after())
    line.last = grad_away
    for chain in (c_sum, a_sum, b_sum):
        chain.advance(line)
    grad_got = swap_core(grad_away)
    for chain in (c_sum, a_sum, b_sum):
        chain.advance(line)
    result = line.both_halves(core, res_own, swap_core(res_away))
    for chain in (c_sum, a_sum, b_sum, c_sum, a_sum, b_sum, c_sum, a_sum, b_sum):
        chain.advance(line)
    c_sum.advance(line)
    c_sum.advance(line)
    grad_own = last(True, place, skip, tokens, cotangent, gh, parts, wqkv_n, gain_one, line.after())
    line.last = grad_own
    a_sum.advance(line)
    for chain in (a_sum, c_sum):
        while not chain.done:
            chain.advance(line)
    dq, dkt, dvt, dgain_one = unpack_last(place, c_sum.keep, c_sum.got, wqkv_t, gain_line, line.after())
    line.last = dgain_one
    while not b_sum.done:
        b_sum.advance(line)
    first = unpack(0, place, (a_sum.keep, a_sum.got), width, inner, ())
    dwg, dwu, dwdt, dwo, dgain_two = unpack(1, place, (b_sum.keep, b_sum.got), width, inner, first)
    grad_x = line.both_halves(core, grad_own, grad_got)
    return (
        flip(result), flip(grad_x),
        dgain_one, dq, flip(dkt), flip(dvt), dwo, dgain_two, dwg, dwu, flip(dwdt),
    )


def solution(mesh):
    split = P("wide", "narrow", None)
    in_specs = (split, P("wide", None), P("wide"), split) + (P(),) * 9
    out_specs = (split, split) + (P(),) * 9
    return jax.shard_map(per_device, mesh=mesh, in_specs=in_specs, out_specs=out_specs, check_vma=False)
```

profile of v0, /device:TPU:0, one launch (start us, length us, event | category | flops | bytes accessed | tf_op | source)
XLA Modules:
  0.0 197.2 jit_solution(2759184441447171227)
XLA Ops:
  0.7 1.2 dynamic-slice_bitcast_fusion.1
  1.9 0.5 collective-permute-start
  2.4 0.2 collective-permute-start.1
  2.7 4.0 %prelude.1 = (bf16[960,576]{1,0:T(8,128)(2,1)}, bf16[576,960]{1,0:T(8,128)(2,1)}, bf16[576,576]{1,0:T(8,128)(2,1)}, f32[576,128]{1,0:T(8,128)}, f32[576,128]{1,0:T(8,128)}, /*index=5*/f32[1,576]{1,0:T(1,128)}) custom-call(bf16[576,576]{1,0:T(8,128)(2,1)} %wq_ref.1, bf16[192,576]{1,0:T(8,128)(2,1)} %bitcast.30, bf16[192,576]{1,0:T(8,128)(2,1)} %bitcast.31, ...), custom_call_target="tpu_custom_call" | custom-call | flops 4000000000 | bytes 1024 | tf_op jit(solution)/shard_map/prelude/pallas_call | solution.py:113
  6.7 0.8 copy-done.13
  7.5 0.2 copy-done.14
  7.7 55.6 %layer_forward.1 = (bf16[576,1024]{1,0:T(8,128)(2,1)}, bf16[192,1024]{1,0:T(8,128)(2,1)}, bf16[3,1024,64]{2,1,0:T(8,128)(2,1)}, bf16[4,9,1024,256]{3,2,1,0:T(8,1...) custom-call(s32[1]{0:T(128)} %bitcast.place_ref.refs_0_, ...), custom_call_target="tpu_custom_call" | custom-call | flops 49999998976 | bytes 1024 | tf_op jit(solution)/shard_map/layer_forward/pallas_call | solution.py:384
  63.3 0.4 collective-permute-start.4
  63.7 0.2 collective-permute-start.3
  63.9 9.7 %attention_backward.3 = (bf16[320,1024]{1,0:T(8,128)(2,1)}, bf16[2304,128]{1,0:T(8,128)(2,1)}, bf16[2304,128]{1,0:T(8,128)(2,1)}) custom-call(s32[1]{0:T(128)} %bitcast.place_ref.refs_0_, bf16[4,9,1024,256]{3,2,1,0:T(8,128)(2,1)} %get-tuple-element.116.refs_1_, bf16[576,1024]{1,0:T(8,128)(2,1)} %get-tuple-element.117.refs_2_, ...), custom_call_target="tpu_custom_call" | custom-call | flops 8999999488 | bytes 1024 | tf_op jit(solution)/shard_map/attention_backward/pallas_call | solution.py:498
  73.6 1.1 copy-done.2
  74.6 3.1 %add_convert_fusion.2 = (bf16[2688,128]{1,0:T(8,128)(2,1)S(1)}, bf16[2688,128]{1,0:T(8,128)(2,1)}) fusion(bf16[5376,128]{1,0:T(8,128)(2,1)} %copy-done.2, s32[]{:T(128)S(6)} %select_n.210, bf16[5376,128]{1,0:T(8,128)(2,1)} %get-tuple-element.124, s32[]{:T(128)S(6)} %select_n.206), kind=kLoop, calls=%fused_computation.4 | loop fusion | flops 2752512 | bytes 4128776 | tf_op jit(solution)/shard_map/convert_element_type | solution.py:620
  77.8 2.8 %collective-permute-start.6 = (bf16[2688,128]{1,0:T(8,128)(2,1)}, bf16[2688,128]{1,0:T(8,128)(2,1)}, u32[]{:S(2)}, u32[]{:S(2)}) collective-permute-start(bf16[2688,128]{1,0:T(8,128)(2,1)} %get-tuple-element.204), channel_id=1, source_target_pairs={{0,2},{1,5},{2,0},{3,7},{4,6},{5,1},{6,4},{7,3},{8,10},{9,13},{10,... | collective-permute-start | bytes 2064392 | tf_op jit(solution)/shard_map/ppermute | solution.py:605
  80.6 1.3 add_convert_fusion
  81.9 1.5 collective-permute-start.5
  83.4 9.6 %attention_backward.4 = (bf16[320,1024]{1,0:T(8,128)(2,1)}, bf16[2304,128]{1,0:T(8,128)(2,1)}, bf16[2304,128]{1,0:T(8,128)(2,1)}) custom-call(s32[1]{0:T(128)} %bitcast.place_ref.refs_0_, bf16[4,9,1024,256]{3,2,1,0:T(8,128)(2,1)} %get-tuple-element.116.refs_1_, ...), custom_call_target="tpu_custom_call", output_to_operand_aliasing={{1}: (10, {}), {2}: (11, {})} | custom-call | flops 8999999488 | bytes 1024 | tf_op jit(solution)/shard_map/attention_backward/pallas_call | solution.py:498
  93.1 2.0 %add_convert_fusion.6 = (bf16[1344,128]{1,0:T(8,128)(2,1)S(1)}, bf16[1344,128]{1,0:T(8,128)(2,1)}) fusion(bf16[2688,128]{1,0:T(8,128)(2,1)} %collective-permute-done.6, s32[]{:T(128)S(6)} %select_n.215, bf16[2688,128]{1,0:T(8,128)(2,1)S(1)} %get-tuple-element.131, s32[]{:T(128)S(6)} %select_n.211), kind=kLoop, calls=%fused_computation.10 | loop fusion | flops 1376256 | bytes 2064392 | tf_op jit(solution)/shard_map/convert_element_type | solution.py:620
  95.1 0.5 collective-permute-start.8
  95.6 2.8 %collective-permute-done.5 = bf16[3328,128]{1,0:T(8,128)(2,1)S(1)} collective-permute-done((bf16[3328,128]{1,0:T(8,128)(2,1)}, bf16[3328,128]{1,0:T(8,128)(2,1)S(1)}, u32[]{:S(2)}, u32[]{:S(2)}) %collective-permute-start.5) | collective-permute-done | bytes 852000 | tf_op jit(solution)/shard_map/ppermute | solution.py:605
  98.3 0.2 add_convert_fusion.4
  98.6 1.8 collective-permute-start.7
  100.4 9.9 %attention_backward.5 = (bf16[320,1024]{1,0:T(8,128)(2,1)}, bf16[2304,128]{1,0:T(8,128)(2,1)}, bf16[2304,128]{1,0:T(8,128)(2,1)}) custom-call(s32[1]{0:T(128)} %bitcast.place_ref.refs_0_, bf16[4,9,1024,256]{3,2,1,0:T(8,128)(2,1)} %get-tuple-element.116.refs_1_, ...), custom_call_target="tpu_custom_call", output_to_operand_aliasing={{1}: (10, {}), {2}: (11, {})} | custom-call | flops 8999999488 | bytes 1024 | tf_op jit(solution)/shard_map/attention_backward/pallas_call | solution.py:498
  110.4 1.6 collective-permute-start.10
  112.2 0.5 collective-permute-start.9
  112.7 0.2 copy-done.8
  112.9 5.0 %input_backward.2 = bf16[576,512]{1,0:T(8,128)(2,1)} custom-call(s32[1]{0:T(128)} %bitcast.place_ref.refs_0_, s32[2]{0:T(128)} %refs_1_.3, bf16[576,512]{1,0:T(8,128)(2,1)} %copy-done.13, bf16[576,512]{1,0:T(8,128)(2,1)} %copy-done.14, f32[576,1024]{1,0:T(8,128)} %get-tuple-element.144.refs_4_, bf16[320,1024]{1,0:T(8,128)(2,1)} %get-tuple-element.123.refs_5_, ...), custom_call_target="tpu_custom_call" | custom-call | flops 4000000000 | bytes 1024 | tf_op jit(solution)/shard_map/input_backward/pallas_call | solution.py:553
  117.9 0.2 add_convert_fusion.8
  118.1 1.1 collective-permute-start.14
  119.2 1.4 collective-permute-start.2
  120.7 0.7 collective-permute-start.13
  121.5 2.3 %collective-permute-start.12 = (bf16[416,128]{1,0:T(8,128)(2,1)S(1)}, bf16[416,128]{1,0:T(8,128)(2,1)S(1)}, u32[]{:S(2)}, u32[]{:S(2)}) collective-permute-start(bf16[416,128]{1,0:T(8,128)(2,1)S(1)} %get-tuple-element.217), channel_id=1, source_target_pairs={{0,16},{1,5},{2,18},{3,7},{4,20},{5,1},{6,22},{7,3},{8,24},{9,13},... | collective-permute-start | bytes 319496 | tf_op jit(solution)/shard_map/ppermute | solution.py:605
  123.8 2.0 %collective-permute-done.14 = bf16[1152,128]{1,0:T(8,128)(2,1)S(1)} collective-permute-done((bf16[1152,128]{1,0:T(8,128)(2,1)S(1)}, bf16[1152,128]{1,0:T(8,128)(2,1)S(1)}, u32[]{:S(2)}, u32[]{:S(2)}) %collective-permute-start.14) | collective-permute-done | bytes 294944 | tf_op jit(solution)/shard_map/ppermute | solution.py:605
  125.9 1.6 collective-permute-start.15
  127.5 2.7 %collective-permute-start.18 = (bf16[336,128]{1,0:T(8,128)(2,1)S(1)}, bf16[336,128]{1,0:T(8,128)(2,1)S(1)}, u32[]{:S(2)}, u32[]{:S(2)}) collective-permute-start(bf16[336,128]{1,0:T(8,128)(2,1)S(1)} %add_convert_fusion.22), channel_id=1, source_target_pairs={{0,16},{1,3},{2,18},{3,1},{4,20},{5,7},{6,22},{7,5},{8,24},{9,11},... | collective-permute-start | bytes 258056 | tf_op jit(solution)/shard_map/ppermute | solution.py:605
  130.2 0.4 collective-permute-start.17
  130.6 1.6 collective-permute-done.15
  132.3 1.5 collective-permute-start.16
  133.8 2.2 %collective-permute-start.21 = (bf16[672,128]{1,0:T(8,128)(2,1)S(1)}, bf16[672,128]{1,0:T(8,128)(2,1)S(1)}, u32[]{:S(2)}, u32[]{:S(2)}) collective-permute-start(bf16[672,128]{1,0:T(8,128)(2,1)S(1)} %maximum_select_fusion.9), channel_id=1, source_target_pairs={{0,8},{1,17},{2,10},{3,19},{4,12},{5,21},{6,14},{7,23},{8,0},{9,25... | collective-permute-start | bytes 516104 | tf_op jit(solution)/shard_map/ppermute | solution.py:605
  136.1 4.0 %collective-permute-done.17 = bf16[416,128]{1,0:T(8,128)(2,1)S(1)} collective-permute-done((bf16[416,128]{1,0:T(8,128)(2,1)S(1)}, bf16[416,128]{1,0:T(8,128)(2,1)S(1)}, u32[]{:S(2)}, u32[]{:S(2)}) %collective-permute-start.17) | collective-permute-done | bytes 106528 | tf_op jit(solution)/shard_map/ppermute | solution.py:605
  140.2 1.0 collective-permute-start.20
  141.2 3.9 %collective-permute-start.19 = (bf16[576,128]{1,0:T(8,128)(2,1)S(1)}, bf16[576,128]{1,0:T(8,128)(2,1)S(1)}, u32[]{:S(2)}, u32[]{:S(2)}) collective-permute-start(bf16[576,128]{1,0:T(8,128)(2,1)S(1)} %add_convert_fusion.15), channel_id=1, source_target_pairs={{0,16},{1,17},{2,18},{3,19},{4,20},{5,21},{6,22},{7,23},{8,24},{9,... | collective-permute-start | bytes 442376 | tf_op jit(solution)/shard_map/ppermute | solution.py:605
  145.2 1.0 collective-permute-start.24
  146.2 6.1 %collective-permute-done.20 = bf16[832,128]{1,0:T(8,128)(2,1)S(1)} collective-permute-done((bf16[832,128]{1,0:T(8,128)(2,1)S(1)}, bf16[832,128]{1,0:T(8,128)(2,1)S(1)}, u32[]{:S(2)}, u32[]{:S(2)}) %collective-permute-start.20) | collective-permute-done | bytes 213024 | tf_op jit(solution)/shard_map/ppermute | solution.py:605
  152.5 2.2 %collective-permute-start.23 = (bf16[1664,128]{1,0:T(8,128)(2,1)S(1)}, bf16[1664,128]{1,0:T(8,128)(2,1)S(1)}, u32[]{:S(2)}, u32[]{:S(2)}) collective-permute-start(bf16[1664,128]{1,0:T(8,128)(2,1)S(1)} %maximum_select_fusion.5), channel_id=1, source_target_pairs={{0,2},{1,17},{2,0},{3,19},{4,6},{5,21},{6,4},{7,23},{8,10},{9,25},... | collective-permute-start | bytes 1277960 | tf_op jit(solution)/shard_map/ppermute | solution.py:605
  154.7 0.3 collective-permute-start.22
  155.0 0.2 maximum_select_fusion.3
  155.2 5.6 %collective-permute-done.23 = bf16[1664,128]{1,0:T(8,128)(2,1)S(1)} collective-permute-done((bf16[1664,128]{1,0:T(8,128)(2,1)S(1)}, bf16[1664,128]{1,0:T(8,128)(2,1)S(1)}, u32[]{:S(2)}, u32[]{:S(2)}) %collective-permute-start.23) | collective-permute-done | bytes 426016 | tf_op jit(solution)/shard_map/ppermute | solution.py:605
  160.8 0.2 maximum_select_fusion.2
  161.1 2.1 %collective-permute-start.25 = (bf16[1152,128]{1,0:T(8,128)(2,1)S(1)}, bf16[1152,128]{1,0:T(8,128)(2,1)}, u32[]{:S(2)}, u32[]{:S(2)}) collective-permute-start(bf16[1152,128]{1,0:T(8,128)(2,1)S(1)} %maximum_select_fusion.7), channel_id=1, source_target_pairs={{0,2},{1,5},{2,0},{3,7},{4,6},{5,1},{6,4},{7,3},{8,10},{9,13},{10,... | collective-permute-start | bytes 884744 | tf_op jit(solution)/shard_map/ppermute | solution.py:605
  163.3 2.0 collective-permute-start.27
  165.3 2.8 %collective-permute-done.25 = bf16[1152,128]{1,0:T(8,128)(2,1)} collective-permute-done((bf16[1152,128]{1,0:T(8,128)(2,1)S(1)}, bf16[1152,128]{1,0:T(8,128)(2,1)}, u32[]{:S(2)}, u32[]{:S(2)}) %collective-permute-start.25) | collective-permute-done | bytes 294944 | tf_op jit(solution)/shard_map/ppermute | solution.py:605
  168.0 2.0 %maximum_select_fusion.4.refs_10_.refs_1_ = bf16[2304,128]{1,0:T(8,128)(2,1)} fusion(bf16[1152,128]{1,0:T(8,128)(2,1)} %collective-permute-done.25, bf16[1152,128]{1,0:T(8,128)(2,1)S(1)} %maximum_select_fusion.7, pred[]{:T(512)S(6)} %eq.19), kind=kLoop, calls=%fused_computation.12 | loop fusion | flops 2654208 | bytes 1179649 | tf_op jit(solution)/shard_map/jit(_where)/select_n | solution.py:631
  170.1 4.9 %input_backward.3 = bf16[2,576,512]{2,1,0:T(8,128)(2,1)} custom-call(s32[1]{0:T(128)} %bitcast.place_ref.refs_0_, s32[2]{0:T(128)} %refs_1_.3, bf16[2,576,512]{2,1,0:T(8,128)(2,1)} %bitcast.24, bf16[2,576,512]{2,1,0:T(8,128)(2,1)} %bitcast.26, f32[576,1024]{1,0:T(8,128)} %get-tuple-element.144.refs_4_, bf16[320,1024]{1,0:T(8,128)(2,1)} %get-tuple-element.123.refs_5_, ...), custom_call_target="tpu_custom_call" | custom-call | flops 4000000000 | bytes 1024 | tf_op jit(solution)/shard_map/input_backward/pallas_call | solution.py:553
  174.9 0.4 collective-permute-done.29
  175.3 1.4 maximum_select_fusion.1.refs_5_.own
  176.7 1.1 collective-permute-start.31
  177.8 3.6 %unpack_attention.1 = (f32[576,576]{1,0:T(8,128)}, f32[192,576]{1,0:T(8,128)}, f32[192,576]{1,0:T(8,128)}, f32[576]{0:T(1024)}) custom-call(s32[1]{0:T(128)} %bitcast.place_ref.refs_0_, bf16[2304,128]{1,0:T(8,128)(2,1)} %maximum_select_fusion.4.refs_10_.refs_1_, bf16[2304,128]{1,0:T(8,128)(2,1)} %collective-permute-done.28.refs_2_, ...), custom_call_target="tpu_custom_call" | custom-call | flops 3000000000 | bytes 1024 | tf_op jit(solution)/shard_map/unpack_attention/pallas_call | solution.py:735
  181.5 0.4 maximum_select_fusion.own
  182.0 0.5 collective-permute-start.26
  182.5 0.5 copy-done.9
  183.0 3.2 %collective-permute-done.26 = bf16[576,512]{1,0:T(8,128)(2,1)S(1)} collective-permute-done((bf16[576,512]{1,0:T(8,128)(2,1)}, bf16[576,512]{1,0:T(8,128)(2,1)S(1)}, u32[]{:S(2)}, u32[]{:S(2)}) %collective-permute-start.26) | collective-permute-done | bytes 589856 | tf_op jit(solution)/shard_map/ppermute | solution.py:576
  186.3 1.0 copy-done.12
  187.4 4.4 %unpack_mlp.2 = (f32[576,1536]{1,0:T(8,128)}, f32[576,1536]{1,0:T(8,128)}, f32[576,1536]{1,0:T(8,128)}) custom-call(s32[1]{0:T(128)} %bitcast.place_ref.refs_0_, bf16[5376,128]{1,0:T(8,128)(2,1)} %maximum_select_fusion.1.refs_5_.own, bf16[5376,128]{1,0:T(8,128)(2,1)} %collective-permute-done.31.got), custom_call_target="tpu_custom_call" | custom-call | flops 4000000000 | bytes 1024 | tf_op jit(solution)/shard_map/unpack_mlp/pallas_call | solution.py:696
  191.8 5.3 %unpack_mlp.3 = (f32[576,1536]{1,0:T(8,128)}, f32[576,1536]{1,0:T(8,128)}, f32[576,1536]{1,0:T(8,128)}, f32[576,576]{1,0:T(8,128)}, f32[576]{0:T(1024)}) custom-call(s32[1]{0:T(128)} %bitcast.place_ref.refs_0_, bf16[6656,128]{1,0:T(8,128)(2,1)} %copy-done.1, ...), custom_call_target="tpu_custom_call", output_to_operand_aliasing={{0}: (3, {}), {1}: (4, {}), {2}: (5, {})} | custom-call | flops 4000000000 | bytes 1024 | tf_op jit(solution)/shard_map/unpack_mlp/pallas_call | solution.py:696
  (69 shorter events, 1.5 us)
Async XLA Ops:
  0.6 1.7 copy-start.7
  1.9 4.8 %collective-permute-start = (bf16[576,512]{1,0:T(8,128)(2,1)S(1)}, bf16[576,512]{1,0:T(8,128)(2,1)S(1)}, u32[]{:S(2)}, u32[]{:S(2)}) collective-permute-start(bf16[576,512]{1,0:T(8,128)(2,1)S(1)} %dynamic-slice_bitcast_fusion.1), channel_id=1, source_target_pairs={{0,1},{1,0},{2,3},{3,2},{4,5},{5,4},{6,7},{7,6},{8,9},{9,8},{10,11... | collective-permute-start | bytes 1769480 | tf_op jit(solution)/shard_map/ppermute | solution.py:576
  2.4 4.2 %collective-permute-start.1 = (bf16[576,512]{1,0:T(8,128)(2,1)S(1)}, bf16[576,512]{1,0:T(8,128)(2,1)S(1)}, u32[]{:S(2)}, u32[]{:S(2)}) collective-permute-start(bf16[576,512]{1,0:T(8,128)(2,1)S(1)} %dynamic-slice_bitcast_fusion), channel_id=1, source_target_pairs={{0,1},{1,0},{2,3},{3,2},{4,5},{5,4},{6,7},{7,6},{8,9},{9,8},{10,11... | collective-permute-start | bytes 1769480 | tf_op jit(solution)/shard_map/ppermute | solution.py:576
  6.7 0.8 copy-start.13
  6.7 1.0 copy-start.14
  63.3 10.2 %collective-permute-start.4 = (bf16[5376,128]{1,0:T(8,128)(2,1)}, bf16[5376,128]{1,0:T(8,128)(2,1)S(1)}, u32[]{:S(2)}, u32[]{:S(2)}) collective-permute-start(bf16[5376,128]{1,0:T(8,128)(2,1)} %get-tuple-element.115), channel_id=1, source_target_pairs={{0,1},{1,0},{2,3},{3,2},{4,5},{5,4},{6,7},{7,6},{8,9},{9,8},{10,11... | collective-permute-start | bytes 4128776 | tf_op jit(solution)/shard_map/ppermute | solution.py:576
  63.7 16.9 %collective-permute-start.3 = (bf16[6656,128]{1,0:T(8,128)(2,1)}, bf16[6656,128]{1,0:T(8,128)(2,1)S(1)}, u32[]{:S(2)}, u32[]{:S(2)}) collective-permute-start(bf16[6656,128]{1,0:T(8,128)(2,1)} %get-tuple-element.113), channel_id=1, source_target_pairs={{0,1},{1,0},{2,3},{3,2},{4,5},{5,4},{6,7},{7,6},{8,9},{9,8},{10,11... | collective-permute-start | bytes 5111816 | tf_op jit(solution)/shard_map/ppermute | solution.py:576
  73.6 1.1 copy-start.2
  74.6 5.9 %copy-start = (bf16[6656,128]{1,0:T(8,128)(2,1)S(1)}, bf16[6656,128]{1,0:T(8,128)(2,1)}, u32[]{:S(2)}) copy-start(bf16[6656,128]{1,0:T(8,128)(2,1)} %get-tuple-element.126) | copy-start | bytes 5111812
  77.8 15.3 %collective-permute-start.6 = (bf16[2688,128]{1,0:T(8,128)(2,1)}, bf16[2688,128]{1,0:T(8,128)(2,1)}, u32[]{:S(2)}, u32[]{:S(2)}) collective-permute-start(bf16[2688,128]{1,0:T(8,128)(2,1)} %get-tuple-element.204), channel_id=1, source_target_pairs={{0,2},{1,5},{2,0},{3,7},{4,6},{5,1},{6,4},{7,3},{8,10},{9,13},{10,... | collective-permute-start | bytes 2064392 | tf_op jit(solution)/shard_map/ppermute | solution.py:605
  81.9 16.4 %collective-permute-start.5 = (bf16[3328,128]{1,0:T(8,128)(2,1)}, bf16[3328,128]{1,0:T(8,128)(2,1)S(1)}, u32[]{:S(2)}, u32[]{:S(2)}) collective-permute-start(bf16[3328,128]{1,0:T(8,128)(2,1)} %get-tuple-element.201.refs_12_), channel_id=1, source_target_pairs={{0,4},{1,9},{2,6},{3,11},{4,0},{5,13},{6,2},{7,15},{8,12},{9,1},{1... | collective-permute-start | bytes 2555912 | tf_op jit(solution)/shard_map/ppermute | solution.py:605
  95.1 15.1 %collective-permute-start.8 = (bf16[1344,128]{1,0:T(8,128)(2,1)}, bf16[1344,128]{1,0:T(8,128)(2,1)S(1)}, u32[]{:S(2)}, u32[]{:S(2)}) collective-permute-start(bf16[1344,128]{1,0:T(8,128)(2,1)} %get-tuple-element.208), channel_id=1, source_target_pairs={{0,4},{1,9},{2,6},{3,11},{4,0},{5,13},{6,2},{7,15},{8,12},{9,1},{1... | collective-permute-start | bytes 1032200 | tf_op jit(solution)/shard_map/ppermute | solution.py:605
  98.6 1.8 copy-start.6
  98.6 13.5 %collective-permute-start.7 = (bf16[1664,128]{1,0:T(8,128)(2,1)S(1)}, bf16[1664,128]{1,0:T(8,128)(2,1)S(1)}, u32[]{:S(2)}, u32[]{:S(2)}) collective-permute-start(bf16[1664,128]{1,0:T(8,128)(2,1)S(1)} %get-tuple-element.205.refs_12_), channel_id=1, source_target_pairs={{0,2},{1,17},{2,0},{3,19},{4,6},{5,21},{6,4},{7,23},{8,10},{9,25},... | collective-permute-start | bytes 1277960 | tf_op jit(solution)/shard_map/ppermute | solution.py:605
  110.2 7.7 %collective-permute-start.11 = (bf16[2304,128]{1,0:T(8,128)(2,1)}, bf16[2304,128]{1,0:T(8,128)(2,1)S(1)}, u32[]{:S(2)}, u32[]{:S(2)}) collective-permute-start(bf16[2304,128]{1,0:T(8,128)(2,1)} %get-tuple-element.143), channel_id=1, source_target_pairs={{0,1},{1,0},{2,3},{3,2},{4,5},{5,4},{6,7},{7,6},{8,9},{9,8},{10,11... | collective-permute-start | bytes 1769480 | tf_op jit(solution)/shard_map/ppermute | solution.py:576
  110.4 10.2 %collective-permute-start.10 = (bf16[672,128]{1,0:T(8,128)(2,1)S(1)}, bf16[672,128]{1,0:T(8,128)(2,1)S(1)}, u32[]{:S(2)}, u32[]{:S(2)}) collective-permute-start(bf16[672,128]{1,0:T(8,128)(2,1)S(1)} %get-tuple-element.214), channel_id=1, source_target_pairs={{0,8},{1,17},{2,10},{3,19},{4,12},{5,21},{6,14},{7,23},{8,0},{9,25... | collective-permute-start | bytes 516104 | tf_op jit(solution)/shard_map/ppermute | solution.py:605
  112.2 0.7 copy-start.8
  112.2 9.2 %collective-permute-start.9 = (bf16[832,128]{1,0:T(8,128)(2,1)S(1)}, bf16[832,128]{1,0:T(8,128)(2,1)S(1)}, u32[]{:S(2)}, u32[]{:S(2)}) collective-permute-start(bf16[832,128]{1,0:T(8,128)(2,1)S(1)} %get-tuple-element.211.refs_10_), channel_id=1, source_target_pairs={{0,8},{1,3},{2,10},{3,1},{4,12},{5,7},{6,14},{7,5},{8,0},{9,11},{1... | collective-permute-start | bytes 638984 | tf_op jit(solution)/shard_map/ppermute | solution.py:605
  112.9 5.0 %copy-start.3 = (bf16[2304,128]{1,0:T(8,128)(2,1)S(1)}, bf16[2304,128]{1,0:T(8,128)(2,1)}, u32[]{:S(2)}) copy-start(bf16[2304,128]{1,0:T(8,128)(2,1)} %get-tuple-element.146) | copy-start | bytes 1769476
  118.1 7.7 %collective-permute-start.14 = (bf16[1152,128]{1,0:T(8,128)(2,1)S(1)}, bf16[1152,128]{1,0:T(8,128)(2,1)S(1)}, u32[]{:S(2)}, u32[]{:S(2)}) collective-permute-start(bf16[1152,128]{1,0:T(8,128)(2,1)S(1)} %get-tuple-element.210), channel_id=1, source_target_pairs={{0,2},{1,5},{2,0},{3,7},{4,6},{5,1},{6,4},{7,3},{8,10},{9,13},{10,... | collective-permute-start | bytes 884744 | tf_op jit(solution)/shard_map/ppermute | solution.py:605
  119.2 11.4 %collective-permute-start.2 = (bf16[576,512]{1,0:T(8,128)(2,1)}, bf16[576,512]{1,0:T(8,128)(2,1)S(1)}, u32[]{:S(2)}, u32[]{:S(2)}) collective-permute-start(bf16[576,512]{1,0:T(8,128)(2,1)} %get-tuple-element.111), channel_id=1, source_target_pairs={{0,1},{1,0},{2,3},{3,2},{4,5},{5,4},{6,7},{7,6},{8,9},{9,8},{10,11... | collective-permute-start | bytes 1769480 | tf_op jit(solution)/shard_map/ppermute | solution.py:576
  120.7 6.8 %collective-permute-start.13 = (bf16[336,128]{1,0:T(8,128)(2,1)S(1)}, bf16[336,128]{1,0:T(8,128)(2,1)S(1)}, u32[]{:S(2)}, u32[]{:S(2)}) collective-permute-start(bf16[336,128]{1,0:T(8,128)(2,1)S(1)} %get-tuple-element.220), channel_id=1, source_target_pairs={{0,16},{1,3},{2,18},{3,1},{4,20},{5,7},{6,22},{7,5},{8,24},{9,11},... | collective-permute-start | bytes 258056 | tf_op jit(solution)/shard_map/ppermute | solution.py:605
  121.5 8.7 %collective-permute-start.12 = (bf16[416,128]{1,0:T(8,128)(2,1)S(1)}, bf16[416,128]{1,0:T(8,128)(2,1)S(1)}, u32[]{:S(2)}, u32[]{:S(2)}) collective-permute-start(bf16[416,128]{1,0:T(8,128)(2,1)S(1)} %get-tuple-element.217), channel_id=1, source_target_pairs={{0,16},{1,5},{2,18},{3,7},{4,20},{5,1},{6,22},{7,3},{8,24},{9,13},... | collective-permute-start | bytes 319496 | tf_op jit(solution)/shard_map/ppermute | solution.py:605
  125.9 6.3 %collective-permute-start.15 = (bf16[576,128]{1,0:T(8,128)(2,1)S(1)}, bf16[576,128]{1,0:T(8,128)(2,1)S(1)}, u32[]{:S(2)}, u32[]{:S(2)}) collective-permute-start(bf16[576,128]{1,0:T(8,128)(2,1)S(1)} %get-tuple-element.216), channel_id=1, source_target_pairs={{0,4},{1,3},{2,6},{3,1},{4,0},{5,7},{6,2},{7,5},{8,12},{9,11},{10,... | collective-permute-start | bytes 442376 | tf_op jit(solution)/shard_map/ppermute | solution.py:605
  127.5 6.3 %collective-permute-start.18 = (bf16[336,128]{1,0:T(8,128)(2,1)S(1)}, bf16[336,128]{1,0:T(8,128)(2,1)S(1)}, u32[]{:S(2)}, u32[]{:S(2)}) collective-permute-start(bf16[336,128]{1,0:T(8,128)(2,1)S(1)} %add_convert_fusion.22), channel_id=1, source_target_pairs={{0,16},{1,3},{2,18},{3,1},{4,20},{5,7},{6,22},{7,5},{8,24},{9,11},... | collective-permute-start | bytes 258056 | tf_op jit(solution)/shard_map/ppermute | solution.py:605
  130.2 9.9 %collective-permute-start.17 = (bf16[416,128]{1,0:T(8,128)(2,1)S(1)}, bf16[416,128]{1,0:T(8,128)(2,1)S(1)}, u32[]{:S(2)}, u32[]{:S(2)}) collective-permute-start(bf16[416,128]{1,0:T(8,128)(2,1)S(1)} %add_convert_fusion.19), channel_id=1, source_target_pairs={{0,16},{1,5},{2,18},{3,7},{4,20},{5,1},{6,22},{7,3},{8,24},{9,13},... | collective-permute-start | bytes 319496 | tf_op jit(solution)/shard_map/ppermute | solution.py:605
  130.6 1.6 copy-start.4
  132.3 8.9 %collective-permute-start.16 = (bf16[576,128]{1,0:T(8,128)(2,1)S(1)}, bf16[576,128]{1,0:T(8,128)(2,1)S(1)}, u32[]{:S(2)}, u32[]{:S(2)}) collective-permute-start(bf16[576,128]{1,0:T(8,128)(2,1)S(1)} %add_convert_fusion.16), channel_id=1, source_target_pairs={{0,8},{1,9},{2,10},{3,11},{4,12},{5,13},{6,14},{7,15},{8,0},{9,1},... | collective-permute-start | bytes 442376 | tf_op jit(solution)/shard_map/ppermute | solution.py:605
  133.8 11.3 %collective-permute-start.21 = (bf16[672,128]{1,0:T(8,128)(2,1)S(1)}, bf16[672,128]{1,0:T(8,128)(2,1)S(1)}, u32[]{:S(2)}, u32[]{:S(2)}) collective-permute-start(bf16[672,128]{1,0:T(8,128)(2,1)S(1)} %maximum_select_fusion.9), channel_id=1, source_target_pairs={{0,8},{1,17},{2,10},{3,19},{4,12},{5,21},{6,14},{7,23},{8,0},{9,25... | collective-permute-start | bytes 516104 | tf_op jit(solution)/shard_map/ppermute | solution.py:605
  140.2 12.2 %collective-permute-start.20 = (bf16[832,128]{1,0:T(8,128)(2,1)S(1)}, bf16[832,128]{1,0:T(8,128)(2,1)S(1)}, u32[]{:S(2)}, u32[]{:S(2)}) collective-permute-start(bf16[832,128]{1,0:T(8,128)(2,1)S(1)} %maximum_select_fusion.8), channel_id=1, source_target_pairs={{0,8},{1,3},{2,10},{3,1},{4,12},{5,7},{6,14},{7,5},{8,0},{9,11},{1... | collective-permute-start | bytes 638984 | tf_op jit(solution)/shard_map/ppermute | solution.py:605
  141.2 13.5 %collective-permute-start.19 = (bf16[576,128]{1,0:T(8,128)(2,1)S(1)}, bf16[576,128]{1,0:T(8,128)(2,1)S(1)}, u32[]{:S(2)}, u32[]{:S(2)}) collective-permute-start(bf16[576,128]{1,0:T(8,128)(2,1)S(1)} %add_convert_fusion.15), channel_id=1, source_target_pairs={{0,16},{1,17},{2,18},{3,19},{4,20},{5,21},{6,22},{7,23},{8,24},{9,... | collective-permute-start | bytes 442376 | tf_op jit(solution)/shard_map/ppermute | solution.py:605
  145.2 9.8 %collective-permute-start.24 = (bf16[1344,128]{1,0:T(8,128)(2,1)S(1)}, bf16[1344,128]{1,0:T(8,128)(2,1)S(1)}, u32[]{:S(2)}, u32[]{:S(2)}) collective-permute-start(bf16[1344,128]{1,0:T(8,128)(2,1)S(1)} %maximum_select_fusion.6), channel_id=1, source_target_pairs={{0,4},{1,9},{2,6},{3,11},{4,0},{5,13},{6,2},{7,15},{8,12},{9,1},{1... | collective-permute-start | bytes 1032200 | tf_op jit(solution)/shard_map/ppermute | solution.py:605
  152.5 8.3 %collective-permute-start.23 = (bf16[1664,128]{1,0:T(8,128)(2,1)S(1)}, bf16[1664,128]{1,0:T(8,128)(2,1)S(1)}, u32[]{:S(2)}, u32[]{:S(2)}) collective-permute-start(bf16[1664,128]{1,0:T(8,128)(2,1)S(1)} %maximum_select_fusion.5), channel_id=1, source_target_pairs={{0,2},{1,17},{2,0},{3,19},{4,6},{5,21},{6,4},{7,23},{8,10},{9,25},... | collective-permute-start | bytes 1277960 | tf_op jit(solution)/shard_map/ppermute | solution.py:605
  154.7 6.3 %collective-permute-start.22 = (bf16[576,128]{1,0:T(8,128)(2,1)S(1)}, bf16[576,128]{1,0:T(8,128)(2,1)S(1)}, u32[]{:S(2)}, u32[]{:S(2)}) collective-permute-start(bf16[576,128]{1,0:T(8,128)(2,1)S(1)} %add_convert_fusion.14), channel_id=1, source_target_pairs={{0,4},{1,3},{2,6},{3,1},{4,0},{5,7},{6,2},{7,5},{8,12},{9,11},{10,... | collective-permute-start | bytes 442376 | tf_op jit(solution)/shard_map/ppermute | solution.py:605
  161.1 6.9 %collective-permute-start.25 = (bf16[1152,128]{1,0:T(8,128)(2,1)S(1)}, bf16[1152,128]{1,0:T(8,128)(2,1)}, u32[]{:S(2)}, u32[]{:S(2)}) collective-permute-start(bf16[1152,128]{1,0:T(8,128)(2,1)S(1)} %maximum_select_fusion.7), channel_id=1, source_target_pairs={{0,2},{1,5},{2,0},{3,7},{4,6},{5,1},{6,4},{7,3},{8,10},{9,13},{10,... | collective-permute-start | bytes 884744 | tf_op jit(solution)/shard_map/ppermute | solution.py:605
  163.2 12.1 %collective-permute-start.29 = (bf16[2688,128]{1,0:T(8,128)(2,1)S(1)}, bf16[2688,128]{1,0:T(8,128)(2,1)S(1)}, u32[]{:S(2)}, u32[]{:S(2)}) collective-permute-start(bf16[2688,128]{1,0:T(8,128)(2,1)S(1)} %maximum_select_fusion.3), channel_id=1, source_target_pairs={{0,2},{1,5},{2,0},{3,7},{4,6},{5,1},{6,4},{7,3},{8,10},{9,13},{10,... | collective-permute-start | bytes 2064392 | tf_op jit(solution)/shard_map/ppermute | solution.py:605
  163.3 18.1 %collective-permute-start.27 = (bf16[3328,128]{1,0:T(8,128)(2,1)S(1)}, bf16[3328,128]{1,0:T(8,128)(2,1)S(1)}, u32[]{:S(2)}, u32[]{:S(2)}) collective-permute-start(bf16[3328,128]{1,0:T(8,128)(2,1)S(1)} %maximum_select_fusion.2), channel_id=1, source_target_pairs={{0,4},{1,9},{2,6},{3,11},{4,0},{5,13},{6,2},{7,15},{8,12},{9,1},{1... | collective-permute-start | bytes 2555912 | tf_op jit(solution)/shard_map/ppermute | solution.py:605
  170.1 7.8 %collective-permute-start.28 = (bf16[2304,128]{1,0:T(8,128)(2,1)}, bf16[2304,128]{1,0:T(8,128)(2,1)}, u32[]{:S(2)}, u32[]{:S(2)}) collective-permute-start(bf16[2304,128]{1,0:T(8,128)(2,1)} %maximum_select_fusion.4.refs_10_.refs_1_), channel_id=1, source_target_pairs={{0,1},{1,0},{2,3},{3,2},{4,5},{5,4},{6,7},{7,6},{8,9},{9,8},{10,11... | collective-permute-start | bytes 1769480 | tf_op jit(solution)/shard_map/ppermute | solution.py:576
  176.7 10.6 %collective-permute-start.31 = (bf16[5376,128]{1,0:T(8,128)(2,1)}, bf16[5376,128]{1,0:T(8,128)(2,1)}, u32[]{:S(2)}, u32[]{:S(2)}) collective-permute-start(bf16[5376,128]{1,0:T(8,128)(2,1)} %maximum_select_fusion.1.refs_5_.own), channel_id=1, source_target_pairs={{0,1},{1,0},{2,3},{3,2},{4,5},{5,4},{6,7},{7,6},{8,9},{9,8},{10,11... | collective-permute-start | bytes 4128776 | tf_op jit(solution)/shard_map/ppermute | solution.py:576
  181.4 1.1 copy-start.5
  181.4 1.5 copy-start.9
  181.5 4.8 %copy-start.11 = (bf16[2,576,512]{2,1,0:T(8,128)(2,1)S(1)}, bf16[2,576,512]{2,1,0:T(8,128)(2,1)}, u32[]{:S(2)}) copy-start(bf16[2,576,512]{2,1,0:T(8,128)(2,1)} %input_backward.3) | copy-start | bytes 3538948
  181.9 9.9 %copy-start.1 = (bf16[6656,128]{1,0:T(8,128)(2,1)}, bf16[6656,128]{1,0:T(8,128)(2,1)S(1)}, u32[]{:S(2)}) copy-start(bf16[6656,128]{1,0:T(8,128)(2,1)S(1)} %maximum_select_fusion.own) | copy-start | bytes 5111812
  181.9 9.9 %collective-permute-start.30 = (bf16[6656,128]{1,0:T(8,128)(2,1)S(1)}, bf16[6656,128]{1,0:T(8,128)(2,1)}, u32[]{:S(2)}, u32[]{:S(2)}) collective-permute-start(bf16[6656,128]{1,0:T(8,128)(2,1)S(1)} %maximum_select_fusion.own), channel_id=1, source_target_pairs={{0,1},{1,0},{2,3},{3,2},{4,5},{5,4},{6,7},{7,6},{8,9},{9,8},{10,11... | collective-permute-start | bytes 5111816 | tf_op jit(solution)/shard_map/ppermute | solution.py:576
  182.0 4.3 %collective-permute-start.26 = (bf16[576,512]{1,0:T(8,128)(2,1)}, bf16[576,512]{1,0:T(8,128)(2,1)S(1)}, u32[]{:S(2)}, u32[]{:S(2)}) collective-permute-start(bf16[576,512]{1,0:T(8,128)(2,1)} %input_backward.2), channel_id=1, source_target_pairs={{0,1},{1,0},{2,3},{3,2},{4,5},{5,4},{6,7},{7,6},{8,9},{9,8},{10,11... | collective-permute-start | bytes 1769480 | tf_op jit(solution)/shard_map/ppermute | solution.py:576
  183.0 3.3 %copy-start.10 = (bf16[2,576,512]{2,1,0:T(8,128)(2,1)}, bf16[2,576,512]{2,1,0:T(8,128)(2,1)S(1)}, u32[]{:S(2)}) copy-start(bf16[2,576,512]{2,1,0:T(8,128)(2,1)S(1)} %bitcast_dynamic-update-slice_fusion.1) | copy-start | bytes 3538948
  186.3 1.0 copy-start.12
where the time goes:
time: 198 us; the launch traced here: 197 us
  Pallas kernels  112 us (57%)
  starting transfers between devices  38.3 us (19%)
  waiting for transfers between devices  28.5 us (14%)
  other arithmetic  12.2 us (6%)
  local copies, waits for them, and re-layouts  5.09 us (3%)
    pallas_call x1, Pallas kernels, layer(): pl.pallas_call(layer_kernel, grid_spec=pltpu.PrefetchScalarGridSpec(num_s...  55.6 us
    ppermute x22, starting transfers between devices, swap(): return lax.ppermute(array, ('wide', 'narrow'), pairs)  33.9 us
    pallas_call x3, Pallas kernels, back(): pl.pallas_call(without(functools.partial(back_kernel, g), inputs, tuple(p...  29.1 us
    ppermute x22, waiting for transfers between devices, swap(): return lax.ppermute(array, ('wide', 'narrow'), pairs)  25.3 us
    pallas_call x2, Pallas kernels, last(): pl.pallas_call(without(last_kernel, 10, after), grid_spec=pltpu.PrefetchS...  9.91 us
    pallas_call x2, Pallas kernels, unpack(): pl.pallas_call(functools.partial(unpack_kernel, chain), grid_spec=pltpu.P...  9.71 us
    convert_element_type x10, other arithmetic, part(): return (a + b).astype(bf16)  7.27 us
    select_n x10, other arithmetic, advance(): jnp.where(low, jnp.concatenate([self.keep, self.got], 0), jnp.concatenate...  4.72 us
  transfers between devices with their start and end apart: 32, of which 9 were waited for; matrix products, arithmetic and copies ran while one was open for 6% of the time, Pallas kernels for 26%

commit v1 on v0

--- a/solution.py
+++ b/solution.py
@@ -525,45 +525,92 @@
     )(place, soft, qt, kt, vn, dot_t, delta, cos_t, sin_t, n1, *packed, *after)
 
 
-def last_kernel(
-    place_ref, skip_ref, x_ref, cot_ref, gh_ref, d0_ref, d1_ref, d2_ref, wqkv_ref, gain_one_ref, grad_ref,
-):
+def input_grad(place_ref, skip_ref, x_ref, cot_ref, gh_ref, parts, wqkv_ref, gain_one_ref):
     x = x_ref[...].reshape(gh_ref.shape).astype(f32)
     skipped = skip_ref[place_ref[0]] == 1
     inverse = lax.rsqrt(jnp.mean(x * x, 0, keepdims=True) + eps_norm)
     normed = x * inverse
-    dqkv = jnp.concatenate([d0_ref[...], d1_ref[...], d2_ref[...]], 0)
+    dqkv = jnp.concatenate([part[...] for part in parts], 0)
     c = dot(wqkv_ref[...], dqkv) * gain_one_ref[:, :1]
     gx = gh_ref[...] + inverse * (c - normed * jnp.mean(c * normed, 0, keepdims=True))
-    gx = jnp.where(skipped, cot_ref[...].reshape(gh_ref.shape), gx.astype(bf16))
-    grad_ref[...] = gx.reshape(grad_ref.shape)
-
-
-def last(mine, place, skip, x, cot, gh, parts, wqkv_n, gain_one, after=()):
+    return jnp.where(skipped, cot_ref[...].reshape(gh_ref.shape), gx.astype(bf16))
+
+
+def away_kernel(
+    place_ref, skip_ref, x_ref, cot_ref, gh_ref, d0_ref, d1_ref, d2_ref, wqkv_ref, gain_one_ref, grad_ref
+):
+    grad_ref[...] = input_grad(
+        place_ref, skip_ref, x_ref, cot_ref, gh_ref, (d0_ref, d1_ref, d2_ref), wqkv_ref, gain_one_ref
+    )
+
+
+def own_kernel(
+    place_ref, skip_ref, x_ref, cot_ref, gh_ref, d0_ref, d1_ref, d2_ref, wqkv_ref, gain_one_ref,
+    grad_got, result_got, result_in, grad_hbm, result_hbm,
+    block_sc, sem, got_sem,
+):
+    step = pl.program_id(0)
+    steps = block_sc.shape[0]
+    own, away = place_ref[0], 1 - place_ref[0]
+    gots = [
+        pltpu.make_async_copy(source, target.at[away], got_sem.at[k])
+        for k, (source, target) in enumerate(((grad_got, grad_hbm), (result_got, result_hbm)))
+    ]
+    copies = [
+        pltpu.make_async_copy(block_sc.at[k], grad_hbm.at[own, :, pl.ds(k * BLOCK, BLOCK)], sem.at[k]) for k in range(steps)
+    ]
+
+    @pl.when(step == 0)
+    def _():
+        for copy in gots:
+            copy.start()
+
+    gx = input_grad(place_ref, skip_ref, x_ref, cot_ref, gh_ref, (d0_ref, d1_ref, d2_ref), wqkv_ref, gain_one_ref)
+    for k in range(steps):
+        @pl.when(step == k)
+        def _():
+            block_sc[k] = gx
+            copies[k].start()
+
+    @pl.when(step == steps - 1)
+    def _():
+        for copy in copies + gots:
+            copy.wait()
+
+
+def last(mine, place, skip, x, cot, gh, parts, wqkv_n, gain_one, gots=(), after=()):
     width, rows = gh.shape
     near = rows // BLOCK // 2
     if mine:
         source = pl.BlockSpec((1, width, BLOCK), lambda i, c, s: (c[0], 0, i))
         at = lambda i, c, s: (0, near * c[0] + i)
+        kernel, out_specs, aliases = own_kernel, [ANY, ANY], {12: 1}
+        out_shape = [jax.ShapeDtypeStruct(x.shape, bf16)] * 2
+        scratch = [pltpu.VMEM((near, width, BLOCK), bf16), pltpu.SemaphoreType.DMA((near,)), pltpu.SemaphoreType.DMA((2,))]
     else:
         source = pl.BlockSpec((width, BLOCK), lambda i, c, s: (0, i))
         at = lambda i, c, s: (0, near * (1 - c[0]) + i)
+        kernel, out_specs, aliases = away_kernel, source, {}
+        out_shape = jax.ShapeDtypeStruct(x.shape, bf16)
+        scratch = []
     col = pl.BlockSpec((width, BLOCK), at)
     part = pl.BlockSpec((PER, BLOCK), at)
     return pl.pallas_call(
-        without(last_kernel, 10, after),
+        without(kernel, 10 + len(gots), after),
         grid_spec=pltpu.PrefetchScalarGridSpec(
             num_scalar_prefetch=2,
             grid=(near,),
             in_specs=[source, source, col, part, part, part, full(wqkv_n.shape), full((width, 128))]
-            + [ANY] * len(after),
-            out_specs=source,
+            + [full(got.shape) for got in gots[:2]] + [ANY] * (len(gots[2:]) + len(after)),
+            out_specs=out_specs,
+            scratch_shapes=scratch,
         ),
-        out_shape=jax.ShapeDtypeStruct(x.shape, bf16),
+        out_shape=out_shape,
+        input_output_aliases=aliases,
         compiler_params=pltpu.CompilerParams(vmem_limit_bytes=VMEM),
         name="input_backward",
         cost_estimate=cost(4),
-    )(place, skip, x, cot, gh, *parts, wqkv_n, gain_one, *after)
+    )(place, skip, x, cot, gh, *parts, wqkv_n, gain_one, *gots, *after)
 
 
 def rotary_rows(rows):
@@ -578,7 +625,7 @@
 
 def axis_orders(bits, turn_index):
     if bits == 4:
-        return (((0, 1, 2, 3), (1, 2, 3, 0)), ((1, 0, 2, 3), (2, 3, 0, 1)), ((0, 1, 2, 3), (1, 0, 2, 3)))[turn_index]
+        return (((0, 1, 2, 3), (1, 2, 3, 0)), ((1, 2, 0, 3), (2, 0, 1, 3)), ((0, 1, 2, 3), (1, 0, 2, 3)))[turn_index]
     base = tuple(range(bits))
     shift = bits // 2
     return base, base[shift:] + base[:shift]
@@ -645,17 +692,22 @@
     def after(self):
         return () if self.last is None else (self.last,)
 
-    def both_halves(self, core, own, got):
-        own, got, _ = lax.optimization_barrier((own, got, self.last))
-        result = lax.dynamic_update_slice_in_dim(own, got[None], 1 - core, 0)
-        self.last = got
-        return result
-
-
-def unpack_kernel(chain, place_ref, own, got, *refs):
-    gate_ref, up_ref, down_ref = refs[-5:-2] if chain else refs
+
+def unpack_kernel(chain, place_ref, own_hbm, got_hbm, *refs):
+    own, got, sem = refs[-3:]
+    gate_ref, up_ref, down_ref = refs[-8:-5] if chain else refs[:3]
     step = pl.program_id(0)
     width = gate_ref.shape[0]
+    copies = [
+        pltpu.make_async_copy(source, target, sem.at[k]) for k, (source, target) in enumerate(((own_hbm, own), (got_hbm, got)))
+    ]
+
+    @pl.when(step == 0)
+    def _():
+        for copy in copies:
+            copy.start()
+        for copy in copies:
+            copy.wait()
 
     def take(halves):
         for third in range(3):
@@ -672,7 +724,7 @@
     pl.when(place_ref[0] != 0)(lambda: take((got, own)))
 
     if chain:
-        w_out_ref, gain_ref = refs[-2:]
+        w_out_ref, gain_ref = refs[-5:-3]
 
         def take_rest(first, second):
             spot = 9 * width
@@ -698,8 +750,9 @@
         grid_spec=pltpu.PrefetchScalarGridSpec(
             num_scalar_prefetch=1,
             grid=(3,),
-            in_specs=[full(b.shape) for b in buffers] + [ANY] * len(earlier),
+            in_specs=[pl.BlockSpec(memory_space=pltpu.HBM)] * 2 + [ANY] * len(earlier),
             out_specs=out_specs,
+            scratch_shapes=[pltpu.VMEM(b.shape, bf16) for b in buffers] + [pltpu.SemaphoreType.DMA((2,))],
         ),
         out_shape=out_shape,
         input_output_aliases={3 + k: k for k in range(len(earlier))},
@@ -798,20 +851,22 @@
             c_sum.first(*packed)
         a_sum.advance(line)
         b_sum.advance(line)
-    grad_away = last(False, place, skip, other, cot_other, gh, parts, wqkv_n, gain_one, line.after())
+    grad_away = last(False, place, skip, other, cot_other, gh, parts, wqkv_n, gain_one, (), line.after())
     line.last = grad_away
     for chain in (c_sum, a_sum, b_sum):
         chain.advance(line)
     grad_got = swap_core(grad_away)
     for chain in (c_sum, a_sum, b_sum):
         chain.advance(line)
-    result = line.both_halves(core, res_own, swap_core(res_away))
-    for chain in (c_sum, a_sum, b_sum, c_sum, a_sum, b_sum, c_sum, a_sum, b_sum):
+    line.last = grad_got
+    result_got = swap_core(res_away)
+    for chain in (c_sum, a_sum, b_sum, c_sum, a_sum, b_sum, c_sum, c_sum, a_sum, b_sum):
         chain.advance(line)
     c_sum.advance(line)
-    c_sum.advance(line)
-    grad_own = last(True, place, skip, tokens, cotangent, gh, parts, wqkv_n, gain_one, line.after())
-    line.last = grad_own
+    grad_x, result = last(
+        True, place, skip, tokens, cotangent, gh, parts, wqkv_n, gain_one, (grad_got, result_got, res_own), line.after()
+    )
+    line.last = grad_x
     a_sum.advance(line)
     for chain in (a_sum, c_sum):
         while not chain.done:
@@ -822,7 +877,6 @@
         b_sum.advance(line)
     first = unpack(0, place, (a_sum.keep, a_sum.got), width, inner, ())
     dwg, dwu, dwdt, dwo, dgain_two = unpack(1, place, (b_sum.keep, b_sum.got), width, inner, first)
-    grad_x = line.both_halves(core, grad_own, grad_got)
     return (
         flip(result), flip(grad_x),
         dgain_one, dq, flip(dkt), flip(dvt), dwo, dgain_two, dwg, dwu, flip(dwdt),

time: 198 us -> 193 us (0.975)
  starting transfers between devices: 38.3 us -> 28 us
  waiting for transfers between devices: 28.5 us -> 32.5 us
  local copies, waits for them, and re-layouts: 5.09 us -> 7.23 us
    ppermute x22, starting transfers between devices: 33.9 us -> 24.4 us  [swap(): return lax.ppermute(array, ('wide', 'narrow'), pairs)]
    ppermute x22, waiting for transfers between devices: 25.3 us -> 32.5 us  [swap(): return lax.ppermute(array, ('wide', 'narrow'), pairs)]
    ppermute x10, waiting for transfers between devices: 3.25 us -> 0.03 us  [swap_core(): return lax.ppermute(array, 'narrow', [(0, 1), (1, 0)])]
    unnamed x30 -> x24, local copies, waits for them, and re-layouts: 3.77 us -> 5.02 us
  transfers between devices with their start and end apart: 32 -> 32, of which waited for: 9 -> 13; matrix products, arithmetic and copies ran while one was open for 6% -> 6% of each run, Pallas kernels for 26% -> 27%
where the time goes in v1:
time: 193 us; the launch traced here: 192 us
  Pallas kernels  113 us (59%)
  waiting for transfers between devices  32.5 us (17%)
  starting transfers between devices  28 us (15%)
  other arithmetic  10.3 us (5%)
  local copies, waits for them, and re-layouts  7.23 us (4%)
    pallas_call x1, Pallas kernels, layer(): pl.pallas_call(layer_kernel, grid_spec=pltpu.PrefetchScalarGridSpec(num_s...  55.6 us
    ppermute x22, waiting for transfers between devices, swap(): return lax.ppermute(array, ('wide', 'narrow'), pairs)  32.5 us
    pallas_call x3, Pallas kernels, back(): pl.pallas_call(without(functools.partial(back_kernel, g), inputs, tuple(p...  29.3 us
    ppermute x22, starting transfers between devices, swap(): return lax.ppermute(array, ('wide', 'narrow'), pairs)  24.4 us
    pallas_call x2, Pallas kernels, last(): pl.pallas_call(without(kernel, 10 + len(gots), after), grid_spec=pltpu.Pr...  10.3 us
    pallas_call x2, Pallas kernels, unpack(): pl.pallas_call(functools.partial(unpack_kernel, chain), grid_spec=pltpu.P...  10.2 us
    convert_element_type x10, other arithmetic, part(): return (a + b).astype(bf16)  7.28 us
    unnamed x24, local copies, waits for them, and re-layouts  5.02 us
  transfers between devices with their start and end apart: 32, of which 13 were waited for; matrix products, arithmetic and copies ran while one was open for 6% of the time, Pallas kernels for 27%

profile of v1, /device:TPU:0, one launch (start us, length us, event | category | flops | bytes accessed | tf_op | source)
XLA Modules:
  0.0 192.3 jit_solution(4423534815277639023)
XLA Ops:
  0.6 1.1 dynamic-slice_bitcast_fusion.1
  1.8 0.5 collective-permute-start
  2.3 1.1 dynamic-slice_bitcast_fusion
  3.4 0.1 collective-permute-start.1
  3.5 4.0 %prelude.1 = (bf16[960,576]{1,0:T(8,128)(2,1)}, bf16[576,960]{1,0:T(8,128)(2,1)}, bf16[576,576]{1,0:T(8,128)(2,1)}, f32[576,128]{1,0:T(8,128)}, f32[576,128]{1,0:T(8,128)}, /*index=5*/f32[1,576]{1,0:T(1,128)}) custom-call(bf16[576,576]{1,0:T(8,128)(2,1)} %wq_ref.1, bf16[192,576]{1,0:T(8,128)(2,1)} %bitcast.24, bf16[192,576]{1,0:T(8,128)(2,1)} %bitcast.25, ...), custom_call_target="tpu_custom_call" | custom-call | flops 4000000000 | bytes 1024 | tf_op jit(solution)/shard_map/prelude/pallas_call | solution.py:113
  7.5 0.8 copy-done.8
  8.3 0.2 copy-done.9
  8.5 55.6 %layer_forward.1 = (bf16[576,1024]{1,0:T(8,128)(2,1)}, bf16[192,1024]{1,0:T(8,128)(2,1)}, bf16[3,1024,64]{2,1,0:T(8,128)(2,1)}, bf16[4,9,1024,256]{3,2,1,0:T(8,1...) custom-call(s32[1]{0:T(128)} %bitcast.place_ref.refs_0_, ...), custom_call_target="tpu_custom_call" | custom-call | flops 49999998976 | bytes 1024 | tf_op jit(solution)/shard_map/layer_forward/pallas_call | solution.py:384
  64.2 0.5 collective-permute-start.3
  64.7 9.8 %attention_backward.3 = (bf16[320,1024]{1,0:T(8,128)(2,1)}, bf16[2304,128]{1,0:T(8,128)(2,1)}, bf16[2304,128]{1,0:T(8,128)(2,1)}) custom-call(s32[1]{0:T(128)} %bitcast.place_ref.refs_0_, bf16[4,9,1024,256]{3,2,1,0:T(8,128)(2,1)} %get-tuple-element.109.refs_1_, bf16[576,1024]{1,0:T(8,128)(2,1)} %get-tuple-element.110.refs_2_, ...), custom_call_target="tpu_custom_call" | custom-call | flops 8999999488 | bytes 1024 | tf_op jit(solution)/shard_map/attention_backward/pallas_call | solution.py:498
  74.5 1.1 copy-done.2
  75.6 3.1 %add_convert_fusion.2 = (bf16[2688,128]{1,0:T(8,128)(2,1)S(1)}, bf16[2688,128]{1,0:T(8,128)(2,1)}) fusion(bf16[5376,128]{1,0:T(8,128)(2,1)} %copy-done.2, s32[]{:T(128)S(6)} %select_n.204, bf16[5376,128]{1,0:T(8,128)(2,1)} %get-tuple-element.123, s32[]{:T(128)S(6)} %select_n.200), kind=kLoop, calls=%fused_computation.4 | loop fusion | flops 2752512 | bytes 4128776 | tf_op jit(solution)/shard_map/convert_element_type | solution.py:667
  78.7 2.8 %collective-permute-start.5 = (bf16[2688,128]{1,0:T(8,128)(2,1)}, bf16[2688,128]{1,0:T(8,128)(2,1)}, u32[]{:S(2)}, u32[]{:S(2)}) collective-permute-start(bf16[2688,128]{1,0:T(8,128)(2,1)} %get-tuple-element.200), channel_id=1, source_target_pairs={{0,2},{1,5},{2,0},{3,7},{4,6},{5,1},{6,4},{7,3},{8,10},{9,13},{10,... | collective-permute-start | bytes 2064392 | tf_op jit(solution)/shard_map/ppermute | solution.py:652
  81.6 1.3 add_convert_fusion
  82.9 1.5 collective-permute-start.4
  84.4 9.7 %attention_backward.4 = (bf16[320,1024]{1,0:T(8,128)(2,1)}, bf16[2304,128]{1,0:T(8,128)(2,1)}, bf16[2304,128]{1,0:T(8,128)(2,1)}) custom-call(s32[1]{0:T(128)} %bitcast.place_ref.refs_0_, bf16[4,9,1024,256]{3,2,1,0:T(8,128)(2,1)} %get-tuple-element.109.refs_1_, ...), custom_call_target="tpu_custom_call", output_to_operand_aliasing={{1}: (10, {}), {2}: (11, {})} | custom-call | flops 8999999488 | bytes 1024 | tf_op jit(solution)/shard_map/attention_backward/pallas_call | solution.py:498
  94.1 2.0 %add_convert_fusion.6 = (bf16[1344,128]{1,0:T(8,128)(2,1)S(1)}, bf16[1344,128]{1,0:T(8,128)(2,1)}) fusion(bf16[2688,128]{1,0:T(8,128)(2,1)} %collective-permute-done.5, s32[]{:T(128)S(6)} %select_n.209, bf16[2688,128]{1,0:T(8,128)(2,1)S(1)} %get-tuple-element.130, s32[]{:T(128)S(6)} %select_n.205), kind=kLoop, calls=%fused_computation.10 | loop fusion | flops 1376256 | bytes 2064392 | tf_op jit(solution)/shard_map/convert_element_type | solution.py:667
  96.1 0.5 collective-permute-start.7
  96.6 2.7 %collective-permute-done.4 = bf16[3328,128]{1,0:T(8,128)(2,1)S(1)} collective-permute-done((bf16[3328,128]{1,0:T(8,128)(2,1)}, bf16[3328,128]{1,0:T(8,128)(2,1)S(1)}, u32[]{:S(2)}, u32[]{:S(2)}) %collective-permute-start.4) | collective-permute-done | bytes 852000 | tf_op jit(solution)/shard_map/ppermute | solution.py:652
  99.3 0.2 add_convert_fusion.4
  99.5 1.9 collective-permute-start.6
  101.4 9.9 %attention_backward.5 = (bf16[320,1024]{1,0:T(8,128)(2,1)}, bf16[2304,128]{1,0:T(8,128)(2,1)}, bf16[2304,128]{1,0:T(8,128)(2,1)}) custom-call(s32[1]{0:T(128)} %bitcast.place_ref.refs_0_, bf16[4,9,1024,256]{3,2,1,0:T(8,128)(2,1)} %get-tuple-element.109.refs_1_, ...), custom_call_target="tpu_custom_call", output_to_operand_aliasing={{1}: (10, {}), {2}: (11, {})} | custom-call | flops 8999999488 | bytes 1024 | tf_op jit(solution)/shard_map/attention_backward/pallas_call | solution.py:498
  111.5 0.5 collective-permute-start.13
  112.0 0.1 add_convert_fusion.10
  112.1 1.5 collective-permute-start.12
  113.7 5.0 %input_backward.2 = bf16[576,512]{1,0:T(8,128)(2,1)} custom-call(s32[1]{0:T(128)} %bitcast.place_ref.refs_0_, s32[2]{0:T(128)} %refs_1_.3, bf16[576,512]{1,0:T(8,128)(2,1)} %copy-done.8, bf16[576,512]{1,0:T(8,128)(2,1)} %copy-done.9, f32[576,1024]{1,0:T(8,128)} %get-tuple-element.108.refs_4_, bf16[320,1024]{1,0:T(8,128)(2,1)} %get-tuple-element.116.refs_5_, ...), custom_call_target="tpu_custom_call" | custom-call | flops 4000000000 | bytes 1024 | tf_op jit(solution)/shard_map/input_backward/pallas_call | solution.py:598
  118.7 0.2 add_convert_fusion.8
  118.8 0.7 collective-permute-start.11
  119.5 0.2 copy-done.11
  119.7 2.1 %collective-permute-start.8 = (bf16[576,512]{1,0:T(8,128)(2,1)S(1)}, bf16[576,512]{1,0:T(8,128)(2,1)S(1)}, u32[]{:S(2)}, u32[]{:S(2)}) collective-permute-start(bf16[576,512]{1,0:T(8,128)(2,1)S(1)} %copy-done.11), channel_id=1, source_target_pairs={{0,1},{1,0},{2,3},{3,2},{4,5},{5,4},{6,7},{7,6},{8,9},{9,8},{10,11... | collective-permute-start | bytes 1769480 | tf_op jit(solution)/shard_map/ppermute | solution.py:623
  121.9 0.5 collective-permute-start.17
  122.5 2.5 %collective-permute-start.16 = (bf16[416,128]{1,0:T(8,128)(2,1)S(1)}, bf16[416,128]{1,0:T(8,128)(2,1)S(1)}, u32[]{:S(2)}, u32[]{:S(2)}) collective-permute-start(bf16[416,128]{1,0:T(8,128)(2,1)S(1)} %get-tuple-element.214), channel_id=1, source_target_pairs={{0,16},{1,17},{2,18},{3,19},{4,20},{5,21},{6,22},{7,23},{8,24},{9,... | collective-permute-start | bytes 319496 | tf_op jit(solution)/shard_map/ppermute | solution.py:652
  125.0 1.5 collective-permute-done.11
  126.6 1.6 collective-permute-start.14
  128.2 3.1 %collective-permute-done.17 = bf16[336,128]{1,0:T(8,128)(2,1)S(1)} collective-permute-done((bf16[336,128]{1,0:T(8,128)(2,1)S(1)}, bf16[336,128]{1,0:T(8,128)(2,1)S(1)}, u32[]{:S(2)}, u32[]{:S(2)}) %collective-permute-start.17) | collective-permute-done | bytes 86048 | tf_op jit(solution)/shard_map/ppermute | solution.py:652
  131.4 1.3 collective-permute-done.16
  132.7 1.7 collective-permute-start.18
  134.4 0.8 copy-done.10
  135.3 0.5 collective-permute-start.15
  135.8 3.6 %collective-permute-done.19 = bf16[336,128]{1,0:T(8,128)(2,1)S(1)} collective-permute-done((bf16[336,128]{1,0:T(8,128)(2,1)S(1)}, bf16[336,128]{1,0:T(8,128)(2,1)S(1)}, u32[]{:S(2)}, u32[]{:S(2)}) %collective-permute-start.19) | collective-permute-done | bytes 86048 | tf_op jit(solution)/shard_map/ppermute | solution.py:652
  139.5 3.4 %collective-permute-done.18 = bf16[416,128]{1,0:T(8,128)(2,1)S(1)} collective-permute-done((bf16[416,128]{1,0:T(8,128)(2,1)S(1)}, bf16[416,128]{1,0:T(8,128)(2,1)S(1)}, u32[]{:S(2)}, u32[]{:S(2)}) %collective-permute-start.18) | collective-permute-done | bytes 106528 | tf_op jit(solution)/shard_map/ppermute | solution.py:652
  143.0 2.0 %collective-permute-start.21 = (bf16[832,128]{1,0:T(8,128)(2,1)S(1)}, bf16[832,128]{1,0:T(8,128)(2,1)S(1)}, u32[]{:S(2)}, u32[]{:S(2)}) collective-permute-start(bf16[832,128]{1,0:T(8,128)(2,1)S(1)} %maximum_select_fusion.8), channel_id=1, source_target_pairs={{0,2},{1,5},{2,0},{3,7},{4,6},{5,1},{6,4},{7,3},{8,10},{9,13},{10,... | collective-permute-start | bytes 638984 | tf_op jit(solution)/shard_map/ppermute | solution.py:652
  145.1 1.4 collective-permute-done.22
  146.6 2.3 %collective-permute-done.21 = bf16[832,128]{1,0:T(8,128)(2,1)S(1)} collective-permute-done((bf16[832,128]{1,0:T(8,128)(2,1)S(1)}, bf16[832,128]{1,0:T(8,128)(2,1)S(1)}, u32[]{:S(2)}, u32[]{:S(2)}) %collective-permute-start.21) | collective-permute-done | bytes 213024 | tf_op jit(solution)/shard_map/ppermute | solution.py:652
  149.0 2.5 %collective-permute-done.20 = bf16[576,128]{1,0:T(8,128)(2,1)S(1)} collective-permute-done((bf16[576,128]{1,0:T(8,128)(2,1)S(1)}, bf16[576,128]{1,0:T(8,128)(2,1)S(1)}, u32[]{:S(2)}, u32[]{:S(2)}) %collective-permute-start.20) | collective-permute-done | bytes 147488 | tf_op jit(solution)/shard_map/ppermute | solution.py:652
  151.5 1.3 collective-permute-start.23
  152.8 0.8 collective-permute-start.26
  153.6 3.1 %collective-permute-done.23 = bf16[576,128]{1,0:T(8,128)(2,1)S(1)} collective-permute-done((bf16[576,128]{1,0:T(8,128)(2,1)S(1)}, bf16[576,128]{1,0:T(8,128)(2,1)S(1)}, u32[]{:S(2)}, u32[]{:S(2)}) %collective-permute-start.23) | collective-permute-done | bytes 147488 | tf_op jit(solution)/shard_map/ppermute | solution.py:652
  156.8 1.5 collective-permute-start.24
  158.3 4.5 %collective-permute-done.26 = bf16[1344,128]{1,0:T(8,128)(2,1)S(1)} collective-permute-done((bf16[1344,128]{1,0:T(8,128)(2,1)S(1)}, bf16[1344,128]{1,0:T(8,128)(2,1)S(1)}, u32[]{:S(2)}, u32[]{:S(2)}) %collective-permute-start.26) | collective-permute-done | bytes 344096 | tf_op jit(solution)/shard_map/ppermute | solution.py:652
  162.8 0.2 maximum_select_fusion.3
  163.0 2.2 %collective-permute-start.28 = (bf16[2688,128]{1,0:T(8,128)(2,1)S(1)}, bf16[2688,128]{1,0:T(8,128)(2,1)S(1)}, u32[]{:S(2)}, u32[]{:S(2)}) collective-permute-start(bf16[2688,128]{1,0:T(8,128)(2,1)S(1)} %maximum_select_fusion.3), channel_id=1, source_target_pairs={{0,2},{1,5},{2,0},{3,7},{4,6},{5,1},{6,4},{7,3},{8,10},{9,13},{10,... | collective-permute-start | bytes 2064392 | tf_op jit(solution)/shard_map/ppermute | solution.py:652
  165.2 0.2 maximum_select_fusion.2
  165.6 0.2 maximum_select_fusion.4.refs_13_.refs_1_
  165.8 0.7 copy-done.4
  166.5 5.3 %input_backward.3 = (bf16[2,576,512]{2,1,0:T(8,128)(2,1)}, bf16[2,576,512]{2,1,0:T(8,128)(2,1)}) custom-call(s32[1]{0:T(128)} %bitcast.place_ref.refs_0_, s32[2]{0:T(128)} %refs_1_.3, bf16[2,576,512]{2,1,0:T(8,128)(2,1)} %bitcast.20, bf16[2,576,512]{2,1,0:T(8,128)(2,1)} %bitcast.22, ...), custom_call_target="tpu_custom_call", output_to_operand_aliasing={{1}: (12, {})} | custom-call | flops 4000000000 | bytes 1024 | tf_op jit(solution)/shard_map/input_backward/pallas_call | solution.py:598
  171.9 2.2 %collective-permute-done.28 = bf16[2688,128]{1,0:T(8,128)(2,1)S(1)} collective-permute-done((bf16[2688,128]{1,0:T(8,128)(2,1)S(1)}, bf16[2688,128]{1,0:T(8,128)(2,1)S(1)}, u32[]{:S(2)}, u32[]{:S(2)}) %collective-permute-start.28) | collective-permute-done | bytes 688160 | tf_op jit(solution)/shard_map/ppermute | solution.py:652
  174.1 1.4 maximum_select_fusion.1.refs_5_.own_hbm
  175.6 3.6 %unpack_attention.1 = (f32[576,576]{1,0:T(8,128)}, f32[192,576]{1,0:T(8,128)}, f32[192,576]{1,0:T(8,128)}, f32[576]{0:T(1024)}) custom-call(s32[1]{0:T(128)} %bitcast.place_ref.refs_0_, bf16[2304,128]{1,0:T(8,128)(2,1)} %copy-done.4, bf16[2304,128]{1,0:T(8,128)(2,1)} %collective-permute-done.27.refs_2_, ...), custom_call_target="tpu_custom_call" | custom-call | flops 3000000000 | bytes 1024 | tf_op jit(solution)/shard_map/unpack_attention/pallas_call | solution.py:788
  179.2 0.9 collective-permute-done.29
  180.1 0.4 maximum_select_fusion.own_hbm
  180.6 5.0 %unpack_mlp.2 = (f32[576,1536]{1,0:T(8,128)}, f32[576,1536]{1,0:T(8,128)}, f32[576,1536]{1,0:T(8,128)}) custom-call(s32[1]{0:T(128)} %bitcast.place_ref.refs_0_, bf16[5376,128]{1,0:T(8,128)(2,1)} %maximum_select_fusion.1.refs_5_.own_hbm, bf16[5376,128]{1,0:T(8,128)(2,1)} %collective-permute-done.31.got_hbm), custom_call_target="tpu_custom_call" | custom-call | flops 4000000000 | bytes 1024 | tf_op jit(solution)/shard_map/unpack_mlp/pallas_call | solution.py:748
  185.6 1.2 copy-done.7
  186.8 5.3 %unpack_mlp.3 = (f32[576,1536]{1,0:T(8,128)}, f32[576,1536]{1,0:T(8,128)}, f32[576,1536]{1,0:T(8,128)}, f32[576,576]{1,0:T(8,128)}, f32[576]{0:T(1024)}) custom-call(s32[1]{0:T(128)} %bitcast.place_ref.refs_0_, bf16[6656,128]{1,0:T(8,128)(2,1)} %copy-done.1, bf16[6656,128]{1,0:T(8,128)(2,1)} %copy-done.7, ...), custom_call_target="tpu_custom_call", output_to_operand_aliasing={{0}: (3, {}), {1}: (4, {}), {2}: (5, {})} | custom-call | flops 4000000000 | bytes 1024 | tf_op jit(solution)/shard_map/unpack_mlp/pallas_call | solution.py:748
  (61 shorter events, 1.6 us)
Async XLA Ops:
  1.8 5.8 %collective-permute-start = (bf16[576,512]{1,0:T(8,128)(2,1)S(1)}, bf16[576,512]{1,0:T(8,128)(2,1)S(1)}, u32[]{:S(2)}, u32[]{:S(2)}) collective-permute-start(bf16[576,512]{1,0:T(8,128)(2,1)S(1)} %dynamic-slice_bitcast_fusion.1), channel_id=1, source_target_pairs={{0,1},{1,0},{2,3},{3,2},{4,5},{5,4},{6,7},{7,6},{8,9},{9,8},{10,11... | collective-permute-start | bytes 1769480 | tf_op jit(solution)/shard_map/ppermute | solution.py:623
  3.4 4.1 %collective-permute-start.1 = (bf16[576,512]{1,0:T(8,128)(2,1)S(1)}, bf16[576,512]{1,0:T(8,128)(2,1)S(1)}, u32[]{:S(2)}, u32[]{:S(2)}) collective-permute-start(bf16[576,512]{1,0:T(8,128)(2,1)S(1)} %dynamic-slice_bitcast_fusion), channel_id=1, source_target_pairs={{0,1},{1,0},{2,3},{3,2},{4,5},{5,4},{6,7},{7,6},{8,9},{9,8},{10,11... | collective-permute-start | bytes 1769480 | tf_op jit(solution)/shard_map/ppermute | solution.py:623
  7.5 0.8 copy-start.8
  7.5 1.0 copy-start.9
  64.2 10.4 %collective-permute-start.3 = (bf16[5376,128]{1,0:T(8,128)(2,1)}, bf16[5376,128]{1,0:T(8,128)(2,1)S(1)}, u32[]{:S(2)}, u32[]{:S(2)}) collective-permute-start(bf16[5376,128]{1,0:T(8,128)(2,1)} %get-tuple-element.122), channel_id=1, source_target_pairs={{0,1},{1,0},{2,3},{3,2},{4,5},{5,4},{6,7},{7,6},{8,9},{9,8},{10,11... | collective-permute-start | bytes 4128776 | tf_op jit(solution)/shard_map/ppermute | solution.py:623
  64.7 16.9 %collective-permute-start.2 = (bf16[6656,128]{1,0:T(8,128)(2,1)}, bf16[6656,128]{1,0:T(8,128)(2,1)S(1)}, u32[]{:S(2)}, u32[]{:S(2)}) collective-permute-start(bf16[6656,128]{1,0:T(8,128)(2,1)} %get-tuple-element.120), channel_id=1, source_target_pairs={{0,1},{1,0},{2,3},{3,2},{4,5},{5,4},{6,7},{7,6},{8,9},{9,8},{10,11... | collective-permute-start | bytes 5111816 | tf_op jit(solution)/shard_map/ppermute | solution.py:623
  74.5 1.1 copy-start.2
  75.6 5.9 %copy-start = (bf16[6656,128]{1,0:T(8,128)(2,1)S(1)}, bf16[6656,128]{1,0:T(8,128)(2,1)}, u32[]{:S(2)}) copy-start(bf16[6656,128]{1,0:T(8,128)(2,1)} %get-tuple-element.125) | copy-start | bytes 5111812
  78.7 15.3 %collective-permute-start.5 = (bf16[2688,128]{1,0:T(8,128)(2,1)}, bf16[2688,128]{1,0:T(8,128)(2,1)}, u32[]{:S(2)}, u32[]{:S(2)}) collective-permute-start(bf16[2688,128]{1,0:T(8,128)(2,1)} %get-tuple-element.200), channel_id=1, source_target_pairs={{0,2},{1,5},{2,0},{3,7},{4,6},{5,1},{6,4},{7,3},{8,10},{9,13},{10,... | collective-permute-start | bytes 2064392 | tf_op jit(solution)/shard_map/ppermute | solution.py:652
  82.9 16.4 %collective-permute-start.4 = (bf16[3328,128]{1,0:T(8,128)(2,1)}, bf16[3328,128]{1,0:T(8,128)(2,1)S(1)}, u32[]{:S(2)}, u32[]{:S(2)}) collective-permute-start(bf16[3328,128]{1,0:T(8,128)(2,1)} %get-tuple-element.198.refs_12_), channel_id=1, source_target_pairs={{0,4},{1,9},{2,6},{3,11},{4,0},{5,13},{6,2},{7,15},{8,12},{9,1},{1... | collective-permute-start | bytes 2555912 | tf_op jit(solution)/shard_map/ppermute | solution.py:652
  96.1 15.2 %collective-permute-start.7 = (bf16[1344,128]{1,0:T(8,128)(2,1)}, bf16[1344,128]{1,0:T(8,128)(2,1)S(1)}, u32[]{:S(2)}, u32[]{:S(2)}) collective-permute-start(bf16[1344,128]{1,0:T(8,128)(2,1)} %get-tuple-element.204), channel_id=1, source_target_pairs={{0,4},{1,9},{2,6},{3,11},{4,0},{5,13},{6,2},{7,15},{8,12},{9,1},{1... | collective-permute-start | bytes 1032200 | tf_op jit(solution)/shard_map/ppermute | solution.py:652
  99.5 1.9 copy-start.5
  99.5 12.5 %collective-permute-start.6 = (bf16[1664,128]{1,0:T(8,128)(2,1)S(1)}, bf16[1664,128]{1,0:T(8,128)(2,1)S(1)}, u32[]{:S(2)}, u32[]{:S(2)}) collective-permute-start(bf16[1664,128]{1,0:T(8,128)(2,1)S(1)} %get-tuple-element.202.refs_12_), channel_id=1, source_target_pairs={{0,8},{1,3},{2,10},{3,1},{4,12},{5,7},{6,14},{7,5},{8,0},{9,11},{1... | collective-permute-start | bytes 1277960 | tf_op jit(solution)/shard_map/ppermute | solution.py:652
  111.3 7.4 %collective-permute-start.10 = (bf16[2304,128]{1,0:T(8,128)(2,1)}, bf16[2304,128]{1,0:T(8,128)(2,1)S(1)}, u32[]{:S(2)}, u32[]{:S(2)}) collective-permute-start(bf16[2304,128]{1,0:T(8,128)(2,1)} %get-tuple-element.143), channel_id=1, source_target_pairs={{0,1},{1,0},{2,3},{3,2},{4,5},{5,4},{6,7},{7,6},{8,9},{9,8},{10,11... | collective-permute-start | bytes 1769480 | tf_op jit(solution)/shard_map/ppermute | solution.py:623
  111.5 10.4 %collective-permute-start.13 = (bf16[672,128]{1,0:T(8,128)(2,1)S(1)}, bf16[672,128]{1,0:T(8,128)(2,1)S(1)}, u32[]{:S(2)}, u32[]{:S(2)}) collective-permute-start(bf16[672,128]{1,0:T(8,128)(2,1)S(1)} %get-tuple-element.210), channel_id=1, source_target_pairs={{0,8},{1,17},{2,10},{3,19},{4,12},{5,21},{6,14},{7,23},{8,0},{9,25... | collective-permute-start | bytes 516104 | tf_op jit(solution)/shard_map/ppermute | solution.py:652
  112.1 1.5 copy-start.6
  112.1 10.3 %collective-permute-start.12 = (bf16[832,128]{1,0:T(8,128)(2,1)S(1)}, bf16[832,128]{1,0:T(8,128)(2,1)S(1)}, u32[]{:S(2)}, u32[]{:S(2)}) collective-permute-start(bf16[832,128]{1,0:T(8,128)(2,1)S(1)} %get-tuple-element.208.refs_10_), channel_id=1, source_target_pairs={{0,2},{1,5},{2,0},{3,7},{4,6},{5,1},{6,4},{7,3},{8,10},{9,13},{10,... | collective-permute-start | bytes 638984 | tf_op jit(solution)/shard_map/ppermute | solution.py:652
  113.7 5.0 %copy-start.3 = (bf16[2304,128]{1,0:T(8,128)(2,1)S(1)}, bf16[2304,128]{1,0:T(8,128)(2,1)}, u32[]{:S(2)}) copy-start(bf16[2304,128]{1,0:T(8,128)(2,1)} %get-tuple-element.144) | copy-start | bytes 1769476
  118.7 1.1 copy-start.11
  118.8 7.7 %collective-permute-start.11 = (bf16[1152,128]{1,0:T(8,128)(2,1)S(1)}, bf16[1152,128]{1,0:T(8,128)(2,1)S(1)}, u32[]{:S(2)}, u32[]{:S(2)}) collective-permute-start(bf16[1152,128]{1,0:T(8,128)(2,1)S(1)} %get-tuple-element.205), channel_id=1, source_target_pairs={{0,2},{1,5},{2,0},{3,7},{4,6},{5,1},{6,4},{7,3},{8,10},{9,13},{10,... | collective-permute-start | bytes 884744 | tf_op jit(solution)/shard_map/ppermute | solution.py:652
  119.7 14.7 %collective-permute-start.8 = (bf16[576,512]{1,0:T(8,128)(2,1)S(1)}, bf16[576,512]{1,0:T(8,128)(2,1)S(1)}, u32[]{:S(2)}, u32[]{:S(2)}) collective-permute-start(bf16[576,512]{1,0:T(8,128)(2,1)S(1)} %copy-done.11), channel_id=1, source_target_pairs={{0,1},{1,0},{2,3},{3,2},{4,5},{5,4},{6,7},{7,6},{8,9},{9,8},{10,11... | collective-permute-start | bytes 1769480 | tf_op jit(solution)/shard_map/ppermute | solution.py:623
  121.9 9.4 %collective-permute-start.17 = (bf16[336,128]{1,0:T(8,128)(2,1)S(1)}, bf16[336,128]{1,0:T(8,128)(2,1)S(1)}, u32[]{:S(2)}, u32[]{:S(2)}) collective-permute-start(bf16[336,128]{1,0:T(8,128)(2,1)S(1)} %get-tuple-element.216), channel_id=1, source_target_pairs={{0,16},{1,3},{2,18},{3,1},{4,20},{5,7},{6,22},{7,5},{8,24},{9,11},... | collective-permute-start | bytes 258056 | tf_op jit(solution)/shard_map/ppermute | solution.py:652
  122.5 10.2 %collective-permute-start.16 = (bf16[416,128]{1,0:T(8,128)(2,1)S(1)}, bf16[416,128]{1,0:T(8,128)(2,1)S(1)}, u32[]{:S(2)}, u32[]{:S(2)}) collective-permute-start(bf16[416,128]{1,0:T(8,128)(2,1)S(1)} %get-tuple-element.214), channel_id=1, source_target_pairs={{0,16},{1,17},{2,18},{3,19},{4,20},{5,21},{6,22},{7,23},{8,24},{9,... | collective-permute-start | bytes 319496 | tf_op jit(solution)/shard_map/ppermute | solution.py:652
  126.6 7.8 %collective-permute-start.14 = (bf16[576,128]{1,0:T(8,128)(2,1)S(1)}, bf16[576,128]{1,0:T(8,128)(2,1)S(1)}, u32[]{:S(2)}, u32[]{:S(2)}) collective-permute-start(bf16[576,128]{1,0:T(8,128)(2,1)S(1)} %get-tuple-element.211), channel_id=1, source_target_pairs={{0,4},{1,3},{2,6},{3,1},{4,0},{5,7},{6,2},{7,5},{8,12},{9,11},{10,... | collective-permute-start | bytes 442376 | tf_op jit(solution)/shard_map/ppermute | solution.py:652
  131.3 8.1 %collective-permute-start.19 = (bf16[336,128]{1,0:T(8,128)(2,1)S(1)}, bf16[336,128]{1,0:T(8,128)(2,1)S(1)}, u32[]{:S(2)}, u32[]{:S(2)}) collective-permute-start(bf16[336,128]{1,0:T(8,128)(2,1)S(1)} %add_convert_fusion.22), channel_id=1, source_target_pairs={{0,16},{1,3},{2,18},{3,1},{4,20},{5,7},{6,22},{7,5},{8,24},{9,11},... | collective-permute-start | bytes 258056 | tf_op jit(solution)/shard_map/ppermute | solution.py:652
  132.7 10.2 %collective-permute-start.18 = (bf16[416,128]{1,0:T(8,128)(2,1)S(1)}, bf16[416,128]{1,0:T(8,128)(2,1)S(1)}, u32[]{:S(2)}, u32[]{:S(2)}) collective-permute-start(bf16[416,128]{1,0:T(8,128)(2,1)S(1)} %add_convert_fusion.19), channel_id=1, source_target_pairs={{0,16},{1,17},{2,18},{3,19},{4,20},{5,21},{6,22},{7,23},{8,24},{9,... | collective-permute-start | bytes 319496 | tf_op jit(solution)/shard_map/ppermute | solution.py:652
  134.4 0.8 copy-start.10
  135.3 9.7 %collective-permute-start.15 = (bf16[576,128]{1,0:T(8,128)(2,1)S(1)}, bf16[576,128]{1,0:T(8,128)(2,1)S(1)}, u32[]{:S(2)}, u32[]{:S(2)}) collective-permute-start(bf16[576,128]{1,0:T(8,128)(2,1)S(1)} %add_convert_fusion.16), channel_id=1, source_target_pairs={{0,8},{1,9},{2,10},{3,11},{4,12},{5,13},{6,14},{7,15},{8,0},{9,1},... | collective-permute-start | bytes 442376 | tf_op jit(solution)/shard_map/ppermute | solution.py:652
  139.5 7.1 %collective-permute-start.22 = (bf16[672,128]{1,0:T(8,128)(2,1)S(1)}, bf16[672,128]{1,0:T(8,128)(2,1)S(1)}, u32[]{:S(2)}, u32[]{:S(2)}) collective-permute-start(bf16[672,128]{1,0:T(8,128)(2,1)S(1)} %maximum_select_fusion.9), channel_id=1, source_target_pairs={{0,8},{1,17},{2,10},{3,19},{4,12},{5,21},{6,14},{7,23},{8,0},{9,25... | collective-permute-start | bytes 516104 | tf_op jit(solution)/shard_map/ppermute | solution.py:652
  143.0 5.9 %collective-permute-start.21 = (bf16[832,128]{1,0:T(8,128)(2,1)S(1)}, bf16[832,128]{1,0:T(8,128)(2,1)S(1)}, u32[]{:S(2)}, u32[]{:S(2)}) collective-permute-start(bf16[832,128]{1,0:T(8,128)(2,1)S(1)} %maximum_select_fusion.8), channel_id=1, source_target_pairs={{0,2},{1,5},{2,0},{3,7},{4,6},{5,1},{6,4},{7,3},{8,10},{9,13},{10,... | collective-permute-start | bytes 638984 | tf_op jit(solution)/shard_map/ppermute | solution.py:652
  145.1 6.4 %collective-permute-start.20 = (bf16[576,128]{1,0:T(8,128)(2,1)S(1)}, bf16[576,128]{1,0:T(8,128)(2,1)S(1)}, u32[]{:S(2)}, u32[]{:S(2)}) collective-permute-start(bf16[576,128]{1,0:T(8,128)(2,1)S(1)} %add_convert_fusion.15), channel_id=1, source_target_pairs={{0,16},{1,17},{2,18},{3,19},{4,20},{5,21},{6,22},{7,23},{8,24},{9,... | collective-permute-start | bytes 442376 | tf_op jit(solution)/shard_map/ppermute | solution.py:652
  151.5 5.2 %collective-permute-start.23 = (bf16[576,128]{1,0:T(8,128)(2,1)S(1)}, bf16[576,128]{1,0:T(8,128)(2,1)S(1)}, u32[]{:S(2)}, u32[]{:S(2)}) collective-permute-start(bf16[576,128]{1,0:T(8,128)(2,1)S(1)} %add_convert_fusion.14), channel_id=1, source_target_pairs={{0,4},{1,3},{2,6},{3,1},{4,0},{5,7},{6,2},{7,5},{8,12},{9,11},{10,... | collective-permute-start | bytes 442376 | tf_op jit(solution)/shard_map/ppermute | solution.py:652
  152.8 9.9 %collective-permute-start.26 = (bf16[1344,128]{1,0:T(8,128)(2,1)S(1)}, bf16[1344,128]{1,0:T(8,128)(2,1)S(1)}, u32[]{:S(2)}, u32[]{:S(2)}) collective-permute-start(bf16[1344,128]{1,0:T(8,128)(2,1)S(1)} %maximum_select_fusion.6), channel_id=1, source_target_pairs={{0,4},{1,9},{2,6},{3,11},{4,0},{5,13},{6,2},{7,15},{8,12},{9,1},{1... | collective-permute-start | bytes 1032200 | tf_op jit(solution)/shard_map/ppermute | solution.py:652
  153.6 12.2 %collective-permute-start.9 = (bf16[576,512]{1,0:T(8,128)(2,1)}, bf16[576,512]{1,0:T(8,128)(2,1)}, u32[]{:S(2)}, u32[]{:S(2)}) collective-permute-start(bf16[576,512]{1,0:T(8,128)(2,1)} %get-tuple-element.140), channel_id=1, source_target_pairs={{0,1},{1,0},{2,3},{3,2},{4,5},{5,4},{6,7},{7,6},{8,9},{9,8},{10,11... | collective-permute-start | bytes 1769480 | tf_op jit(solution)/shard_map/ppermute | solution.py:623
  153.6 11.6 %collective-permute-start.25 = (bf16[1664,128]{1,0:T(8,128)(2,1)S(1)}, bf16[1664,128]{1,0:T(8,128)(2,1)S(1)}, u32[]{:S(2)}, u32[]{:S(2)}) collective-permute-start(bf16[1664,128]{1,0:T(8,128)(2,1)S(1)} %maximum_select_fusion.5), channel_id=1, source_target_pairs={{0,8},{1,3},{2,10},{3,1},{4,12},{5,7},{6,14},{7,5},{8,0},{9,11},{1... | collective-permute-start | bytes 1277960 | tf_op jit(solution)/shard_map/ppermute | solution.py:652
  156.8 8.7 %collective-permute-start.24 = (bf16[1152,128]{1,0:T(8,128)(2,1)S(1)}, bf16[1152,128]{1,0:T(8,128)(2,1)S(1)}, u32[]{:S(2)}, u32[]{:S(2)}) collective-permute-start(bf16[1152,128]{1,0:T(8,128)(2,1)S(1)} %maximum_select_fusion.7), channel_id=1, source_target_pairs={{0,2},{1,5},{2,0},{3,7},{4,6},{5,1},{6,4},{7,3},{8,10},{9,13},{10,... | collective-permute-start | bytes 884744 | tf_op jit(solution)/shard_map/ppermute | solution.py:652
  163.0 11.2 %collective-permute-start.28 = (bf16[2688,128]{1,0:T(8,128)(2,1)S(1)}, bf16[2688,128]{1,0:T(8,128)(2,1)S(1)}, u32[]{:S(2)}, u32[]{:S(2)}) collective-permute-start(bf16[2688,128]{1,0:T(8,128)(2,1)S(1)} %maximum_select_fusion.3), channel_id=1, source_target_pairs={{0,2},{1,5},{2,0},{3,7},{4,6},{5,1},{6,4},{7,3},{8,10},{9,13},{10,... | collective-permute-start | bytes 2064392 | tf_op jit(solution)/shard_map/ppermute | solution.py:652
  165.5 14.6 %collective-permute-start.29 = (bf16[3328,128]{1,0:T(8,128)(2,1)S(1)}, bf16[3328,128]{1,0:T(8,128)(2,1)S(1)}, u32[]{:S(2)}, u32[]{:S(2)}) collective-permute-start(bf16[3328,128]{1,0:T(8,128)(2,1)S(1)} %maximum_select_fusion.2), channel_id=1, source_target_pairs={{0,4},{1,9},{2,6},{3,11},{4,0},{5,13},{6,2},{7,15},{8,12},{9,1},{1... | collective-permute-start | bytes 2555912 | tf_op jit(solution)/shard_map/ppermute | solution.py:652
  165.7 0.8 copy-start.4
  165.7 9.8 %collective-permute-start.27 = (bf16[2304,128]{1,0:T(8,128)(2,1)S(1)}, bf16[2304,128]{1,0:T(8,128)(2,1)}, u32[]{:S(2)}, u32[]{:S(2)}) collective-permute-start(bf16[2304,128]{1,0:T(8,128)(2,1)S(1)} %maximum_select_fusion.4.refs_13_.refs_1_), channel_id=1, source_target_pairs={{0,1},{1,0},{2,3},{3,2},{4,5},{5,4},{6,7},{7,6},{8,9},{9,8},{10,11... | collective-permute-start | bytes 1769480 | tf_op jit(solution)/shard_map/ppermute | solution.py:623
  175.6 5.1 %collective-permute-start.31 = (bf16[5376,128]{1,0:T(8,128)(2,1)}, bf16[5376,128]{1,0:T(8,128)(2,1)}, u32[]{:S(2)}, u32[]{:S(2)}) collective-permute-start(bf16[5376,128]{1,0:T(8,128)(2,1)} %maximum_select_fusion.1.refs_5_.own_hbm), channel_id=1, source_target_pairs={{0,1},{1,0},{2,3},{3,2},{4,5},{5,4},{6,7},{7,6},{8,9},{9,8},{10,11... | collective-permute-start | bytes 4128776 | tf_op jit(solution)/shard_map/ppermute | solution.py:623
  180.5 5.1 %copy-start.1 = (bf16[6656,128]{1,0:T(8,128)(2,1)}, bf16[6656,128]{1,0:T(8,128)(2,1)S(1)}, u32[]{:S(2)}) copy-start(bf16[6656,128]{1,0:T(8,128)(2,1)S(1)} %maximum_select_fusion.own_hbm) | copy-start | bytes 5111812
  180.5 5.1 %collective-permute-start.30 = (bf16[6656,128]{1,0:T(8,128)(2,1)S(1)}, bf16[6656,128]{1,0:T(8,128)(2,1)S(1)}, u32[]{:S(2)}, u32[]{:S(2)}) collective-permute-start(bf16[6656,128]{1,0:T(8,128)(2,1)S(1)} %maximum_select_fusion.own_hbm), channel_id=1, source_target_pairs={{0,1},{1,0},{2,3},{3,2},{4,5},{5,4},{6,7},{7,6},{8,9},{9,8},{10,11... | collective-permute-start | bytes 5111816 | tf_op jit(solution)/shard_map/ppermute | solution.py:623
  185.6 1.2 copy-start.7

commit v2 on v1

--- a/solution.py
+++ b/solution.py
@@ -706,8 +706,10 @@
     def _():
         for copy in copies:
             copy.start()
-        for copy in copies:
-            copy.wait()
+
+    for k in range(2):
+        pl.when((step == 0) & (place_ref[0] == k))(copies[k].wait)
+        pl.when((step == 1) & (place_ref[0] != k))(copies[k].wait)
 
     def take(halves):
         for third in range(3):
@@ -734,8 +736,8 @@
             line = jnp.concatenate([rows[k : k + 1] for k in range(lanes_up(width) // 128)], 1)
             gain_ref[...] = line[:, :width].reshape(width)
 
-        pl.when((step == 0) & (place_ref[0] == 0))(lambda: take_rest(own, got))
-        pl.when((step == 0) & (place_ref[0] != 0))(lambda: take_rest(got, own))
+        pl.when((step == 2) & (place_ref[0] == 0))(lambda: take_rest(own, got))
+        pl.when((step == 2) & (place_ref[0] != 0))(lambda: take_rest(got, own))
 
 
 def unpack(chain, place, buffers, width, inner, earlier):
@@ -750,7 +752,7 @@
         grid_spec=pltpu.PrefetchScalarGridSpec(
             num_scalar_prefetch=1,
             grid=(3,),
-            in_specs=[pl.BlockSpec(memory_space=pltpu.HBM)] * 2 + [ANY] * len(earlier),
+            in_specs=[ANY, pl.BlockSpec(memory_space=pltpu.HBM)] + [ANY] * len(earlier),
             out_specs=out_specs,
             scratch_shapes=[pltpu.VMEM(b.shape, bf16) for b in buffers] + [pltpu.SemaphoreType.DMA((2,))],
         ),
@@ -839,6 +841,7 @@
     a_sum, b_sum, c_sum = (Summer(core, chips, k, exchanges) for k, exchanges in ((0, 0), (1, 0), (2, 2)))
     a_sum.first(keep_a, send_a)
     b_sum.first(keep_b, send_b)
+    result_got = swap_core(res_away)
     line = Line()
     parts, packed = [], ()
     for g in range(KVH):
@@ -858,8 +861,6 @@
     grad_got = swap_core(grad_away)
     for chain in (c_sum, a_sum, b_sum):
         chain.advance(line)
-    line.last = grad_got
-    result_got = swap_core(res_away)
     for chain in (c_sum, a_sum, b_sum, c_sum, a_sum, b_sum, c_sum, c_sum, a_sum, b_sum):
         chain.advance(line)
     c_sum.advance(line)

time: 193 us -> 190 us (0.984); the launches traced: 192 us -> 187 us
  waiting for transfers between devices: 32.5 us -> 23.6 us
  starting transfers between devices: 28 us -> 34 us
    ppermute x22, waiting for transfers between devices: 32.5 us -> 23.6 us  [swap(): return lax.ppermute(array, ('wide', 'narrow'), pairs)]
    ppermute x22, starting transfers between devices: 24.4 us -> 32 us  [swap(): return lax.ppermute(array, ('wide', 'narrow'), pairs)]
    unnamed x24 -> x20, local copies, waits for them, and re-layouts: 5.02 us -> 4 us
  transfers between devices with their start and end apart: 32 -> 32, of which waited for: 13 -> 13; matrix products, arithmetic and copies ran while one was open for 6% -> 6% of each run, Pallas kernels for 27% -> 28%
where the time goes in v2:
time: 190 us; the launch traced here: 187 us
  Pallas kernels  112 us (59%)
  starting transfers between devices  34 us (18%)
  waiting for transfers between devices  23.6 us (12%)
  other arithmetic  10.3 us (5%)
  local copies, waits for them, and re-layouts  6.21 us (3%)
    pallas_call x1, Pallas kernels, layer(): pl.pallas_call(layer_kernel, grid_spec=pltpu.PrefetchScalarGridSpec(num_s...  55.6 us
    ppermute x22, starting transfers between devices, swap(): return lax.ppermute(array, ('wide', 'narrow'), pairs)  32 us
    pallas_call x3, Pallas kernels, back(): pl.pallas_call(without(functools.partial(back_kernel, g), inputs, tuple(p...  29.2 us
    ppermute x22, waiting for transfers between devices, swap(): return lax.ppermute(array, ('wide', 'narrow'), pairs)  23.6 us
    pallas_call x2, Pallas kernels, last(): pl.pallas_call(without(kernel, 10 + len(gots), after), grid_spec=pltpu.Pr...  10.3 us
    pallas_call x2, Pallas kernels, unpack(): pl.pallas_call(functools.partial(unpack_kernel, chain), grid_spec=pltpu.P...  9.17 us
    convert_element_type x10, other arithmetic, part(): return (a + b).astype(bf16)  7.27 us
    pallas_call x1, Pallas kernels, prelude(): pl.pallas_call(prelude_kernel, out_shape=[jax.ShapeDtypeStruct((KVH * PER...  4.01 us
  transfers between devices with their start and end apart: 32, of which 13 were waited for; matrix products, arithmetic and copies ran while one was open for 6% of the time, Pallas kernels for 28%

profile of v2, /device:TPU:0, one launch (start us, length us, event | category | flops | bytes accessed | tf_op | source)
XLA Modules:
  0.0 187.3 jit_solution(9716274142557227997)
XLA Ops:
  0.6 1.1 dynamic-slice_bitcast_fusion.1
  1.8 0.5 collective-permute-start
  2.3 1.1 dynamic-slice_bitcast_fusion
  3.5 4.0 %prelude.1 = (bf16[960,576]{1,0:T(8,128)(2,1)}, bf16[576,960]{1,0:T(8,128)(2,1)}, bf16[576,576]{1,0:T(8,128)(2,1)}, f32[576,128]{1,0:T(8,128)}, f32[576,128]{1,0:T(8,128)}, /*index=5*/f32[1,576]{1,0:T(1,128)}) custom-call(bf16[576,576]{1,0:T(8,128)(2,1)} %wq_ref.1, bf16[192,576]{1,0:T(8,128)(2,1)} %bitcast.24, bf16[192,576]{1,0:T(8,128)(2,1)} %bitcast.25, ...), custom_call_target="tpu_custom_call" | custom-call | flops 4000000000 | bytes 1024 | tf_op jit(solution)/shard_map/prelude/pallas_call | solution.py:113
  7.5 0.8 copy-done.8
  8.3 0.2 copy-done.9
  8.5 55.6 %layer_forward.1 = (bf16[576,1024]{1,0:T(8,128)(2,1)}, bf16[192,1024]{1,0:T(8,128)(2,1)}, bf16[3,1024,64]{2,1,0:T(8,128)(2,1)}, bf16[4,9,1024,256]{3,2,1,0:T(8,1...) custom-call(s32[1]{0:T(128)} %bitcast.place_ref.refs_0_, ...), custom_call_target="tpu_custom_call" | custom-call | flops 49999998976 | bytes 1024 | tf_op jit(solution)/shard_map/layer_forward/pallas_call | solution.py:384
  64.2 0.5 collective-permute-start.3
  64.8 9.7 %attention_backward.3 = (bf16[320,1024]{1,0:T(8,128)(2,1)}, bf16[2304,128]{1,0:T(8,128)(2,1)}, bf16[2304,128]{1,0:T(8,128)(2,1)}) custom-call(s32[1]{0:T(128)} %bitcast.place_ref.refs_0_, bf16[4,9,1024,256]{3,2,1,0:T(8,128)(2,1)} %get-tuple-element.109.refs_1_, bf16[576,1024]{1,0:T(8,128)(2,1)} %get-tuple-element.110.refs_2_, ...), custom_call_target="tpu_custom_call" | custom-call | flops 8999999488 | bytes 1024 | tf_op jit(solution)/shard_map/attention_backward/pallas_call | solution.py:498
  74.5 1.1 copy-done.2
  75.6 3.1 %add_convert_fusion.2 = (bf16[2688,128]{1,0:T(8,128)(2,1)S(1)}, bf16[2688,128]{1,0:T(8,128)(2,1)}) fusion(bf16[5376,128]{1,0:T(8,128)(2,1)} %copy-done.2, s32[]{:T(128)S(6)} %select_n.204, bf16[5376,128]{1,0:T(8,128)(2,1)} %get-tuple-element.123, s32[]{:T(128)S(6)} %select_n.200), kind=kLoop, calls=%fused_computation.4 | loop fusion | flops 2752512 | bytes 4128776 | tf_op jit(solution)/shard_map/convert_element_type | solution.py:667
  78.7 2.8 %collective-permute-start.5 = (bf16[2688,128]{1,0:T(8,128)(2,1)}, bf16[2688,128]{1,0:T(8,128)(2,1)}, u32[]{:S(2)}, u32[]{:S(2)}) collective-permute-start(bf16[2688,128]{1,0:T(8,128)(2,1)} %get-tuple-element.200), channel_id=1, source_target_pairs={{0,2},{1,5},{2,0},{3,7},{4,6},{5,1},{6,4},{7,3},{8,10},{9,13},{10,... | collective-permute-start | bytes 2064392 | tf_op jit(solution)/shard_map/ppermute | solution.py:652
  81.5 1.3 add_convert_fusion
  82.9 1.5 collective-permute-start.4
  84.4 9.6 %attention_backward.4 = (bf16[320,1024]{1,0:T(8,128)(2,1)}, bf16[2304,128]{1,0:T(8,128)(2,1)}, bf16[2304,128]{1,0:T(8,128)(2,1)}) custom-call(s32[1]{0:T(128)} %bitcast.place_ref.refs_0_, bf16[4,9,1024,256]{3,2,1,0:T(8,128)(2,1)} %get-tuple-element.109.refs_1_, ...), custom_call_target="tpu_custom_call", output_to_operand_aliasing={{1}: (10, {}), {2}: (11, {})} | custom-call | flops 8999999488 | bytes 1024 | tf_op jit(solution)/shard_map/attention_backward/pallas_call | solution.py:498
  94.1 2.0 %add_convert_fusion.6 = (bf16[1344,128]{1,0:T(8,128)(2,1)S(1)}, bf16[1344,128]{1,0:T(8,128)(2,1)}) fusion(bf16[2688,128]{1,0:T(8,128)(2,1)} %collective-permute-done.5, s32[]{:T(128)S(6)} %select_n.209, bf16[2688,128]{1,0:T(8,128)(2,1)S(1)} %get-tuple-element.130, s32[]{:T(128)S(6)} %select_n.205), kind=kLoop, calls=%fused_computation.10 | loop fusion | flops 1376256 | bytes 2064392 | tf_op jit(solution)/shard_map/convert_element_type | solution.py:667
  96.1 0.5 collective-permute-start.7
  96.6 2.7 %collective-permute-done.4 = bf16[3328,128]{1,0:T(8,128)(2,1)S(1)} collective-permute-done((bf16[3328,128]{1,0:T(8,128)(2,1)}, bf16[3328,128]{1,0:T(8,128)(2,1)S(1)}, u32[]{:S(2)}, u32[]{:S(2)}) %collective-permute-start.4) | collective-permute-done | bytes 852000 | tf_op jit(solution)/shard_map/ppermute | solution.py:652
  99.3 0.2 add_convert_fusion.4
  99.5 1.9 collective-permute-start.6
  101.4 9.9 %attention_backward.5 = (bf16[320,1024]{1,0:T(8,128)(2,1)}, bf16[2304,128]{1,0:T(8,128)(2,1)}, bf16[2304,128]{1,0:T(8,128)(2,1)}) custom-call(s32[1]{0:T(128)} %bitcast.place_ref.refs_0_, bf16[4,9,1024,256]{3,2,1,0:T(8,128)(2,1)} %get-tuple-element.109.refs_1_, ...), custom_call_target="tpu_custom_call", output_to_operand_aliasing={{1}: (10, {}), {2}: (11, {})} | custom-call | flops 8999999488 | bytes 1024 | tf_op jit(solution)/shard_map/attention_backward/pallas_call | solution.py:498
  111.5 0.5 collective-permute-start.13
  112.1 1.6 collective-permute-start.12
  113.7 5.0 %input_backward.2 = bf16[576,512]{1,0:T(8,128)(2,1)} custom-call(s32[1]{0:T(128)} %bitcast.place_ref.refs_0_, s32[2]{0:T(128)} %refs_1_.3, bf16[576,512]{1,0:T(8,128)(2,1)} %copy-done.8, bf16[576,512]{1,0:T(8,128)(2,1)} %copy-done.9, f32[576,1024]{1,0:T(8,128)} %get-tuple-element.108.refs_4_, bf16[320,1024]{1,0:T(8,128)(2,1)} %get-tuple-element.116.refs_5_, ...), custom_call_target="tpu_custom_call" | custom-call | flops 4000000000 | bytes 1024 | tf_op jit(solution)/shard_map/input_backward/pallas_call | solution.py:598
  118.7 0.2 add_convert_fusion.8
  118.9 0.7 collective-permute-start.11
  119.6 2.7 %collective-permute-start.16 = (bf16[336,128]{1,0:T(8,128)(2,1)S(1)}, bf16[336,128]{1,0:T(8,128)(2,1)S(1)}, u32[]{:S(2)}, u32[]{:S(2)}) collective-permute-start(bf16[336,128]{1,0:T(8,128)(2,1)S(1)} %get-tuple-element.216), channel_id=1, source_target_pairs={{0,16},{1,3},{2,18},{3,1},{4,20},{5,7},{6,22},{7,5},{8,24},{9,11},... | collective-permute-start | bytes 258056 | tf_op jit(solution)/shard_map/ppermute | solution.py:652
  122.3 0.4 collective-permute-start.15
  122.7 3.9 %collective-permute-done.11 = bf16[1152,128]{1,0:T(8,128)(2,1)S(1)} collective-permute-done((bf16[1152,128]{1,0:T(8,128)(2,1)S(1)}, bf16[1152,128]{1,0:T(8,128)(2,1)S(1)}, u32[]{:S(2)}, u32[]{:S(2)}) %collective-permute-start.11) | collective-permute-done | bytes 294944 | tf_op jit(solution)/shard_map/ppermute | solution.py:652
  126.7 1.6 collective-permute-start.14
  128.3 1.9 collective-permute-start.19
  130.2 0.9 collective-permute-done.15
  131.1 0.3 collective-permute-start.18
  131.4 0.5 collective-permute-done.14
  131.9 2.1 %collective-permute-start.17 = (bf16[576,128]{1,0:T(8,128)(2,1)S(1)}, bf16[576,128]{1,0:T(8,128)(2,1)S(1)}, u32[]{:S(2)}, u32[]{:S(2)}) collective-permute-start(bf16[576,128]{1,0:T(8,128)(2,1)S(1)} %add_convert_fusion.16), channel_id=1, source_target_pairs={{0,8},{1,9},{2,10},{3,11},{4,12},{5,13},{6,14},{7,15},{8,0},{9,1},... | collective-permute-start | bytes 442376 | tf_op jit(solution)/shard_map/ppermute | solution.py:652
  134.0 2.3 %collective-permute-done.19 = bf16[336,128]{1,0:T(8,128)(2,1)S(1)} collective-permute-done((bf16[336,128]{1,0:T(8,128)(2,1)S(1)}, bf16[336,128]{1,0:T(8,128)(2,1)S(1)}, u32[]{:S(2)}, u32[]{:S(2)}) %collective-permute-start.19) | collective-permute-done | bytes 86048 | tf_op jit(solution)/shard_map/ppermute | solution.py:652
  136.4 1.7 collective-permute-start.22
  138.1 2.8 %collective-permute-done.18 = bf16[416,128]{1,0:T(8,128)(2,1)S(1)} collective-permute-done((bf16[416,128]{1,0:T(8,128)(2,1)S(1)}, bf16[416,128]{1,0:T(8,128)(2,1)S(1)}, u32[]{:S(2)}, u32[]{:S(2)}) %collective-permute-start.18) | collective-permute-done | bytes 106528 | tf_op jit(solution)/shard_map/ppermute | solution.py:652
  141.0 1.8 collective-permute-start.20
  142.8 2.1 %collective-permute-done.22 = bf16[672,128]{1,0:T(8,128)(2,1)S(1)} collective-permute-done((bf16[672,128]{1,0:T(8,128)(2,1)S(1)}, bf16[672,128]{1,0:T(8,128)(2,1)S(1)}, u32[]{:S(2)}, u32[]{:S(2)}) %collective-permute-start.22) | collective-permute-done | bytes 172064 | tf_op jit(solution)/shard_map/ppermute | solution.py:652
  145.0 1.8 collective-permute-done.21
  146.9 0.5 collective-permute-done.20
  147.5 0.8 collective-permute-start.23
  148.3 1.2 collective-permute-start.26
  149.6 0.5 collective-permute-start.8
  150.1 2.2 %collective-permute-start.25 = (bf16[1664,128]{1,0:T(8,128)(2,1)S(1)}, bf16[1664,128]{1,0:T(8,128)(2,1)S(1)}, u32[]{:S(2)}, u32[]{:S(2)}) collective-permute-start(bf16[1664,128]{1,0:T(8,128)(2,1)S(1)} %maximum_select_fusion.5), channel_id=1, source_target_pairs={{0,8},{1,3},{2,10},{3,1},{4,12},{5,7},{6,14},{7,5},{8,0},{9,11},{1... | collective-permute-start | bytes 1277960 | tf_op jit(solution)/shard_map/ppermute | solution.py:652
  152.3 0.4 collective-permute-done.23
  152.8 1.7 collective-permute-start.24
  154.6 3.9 %collective-permute-done.26 = bf16[1344,128]{1,0:T(8,128)(2,1)S(1)} collective-permute-done((bf16[1344,128]{1,0:T(8,128)(2,1)S(1)}, bf16[1344,128]{1,0:T(8,128)(2,1)S(1)}, u32[]{:S(2)}, u32[]{:S(2)}) %collective-permute-start.26) | collective-permute-done | bytes 344096 | tf_op jit(solution)/shard_map/ppermute | solution.py:652
  158.5 0.2 maximum_select_fusion.3
  158.6 3.1 %collective-permute-start.28 = (bf16[2688,128]{1,0:T(8,128)(2,1)S(1)}, bf16[2688,128]{1,0:T(8,128)(2,1)S(1)}, u32[]{:S(2)}, u32[]{:S(2)}) collective-permute-start(bf16[2688,128]{1,0:T(8,128)(2,1)S(1)} %maximum_select_fusion.3), channel_id=1, source_target_pairs={{0,2},{1,5},{2,0},{3,7},{4,6},{5,1},{6,4},{7,3},{8,10},{9,13},{10,... | collective-permute-start | bytes 2064392 | tf_op jit(solution)/shard_map/ppermute | solution.py:652
  161.7 0.2 maximum_select_fusion.2
  162.0 0.9 collective-permute-start.29
  163.2 0.7 copy-done.4
  163.9 5.3 %input_backward.3 = (bf16[2,576,512]{2,1,0:T(8,128)(2,1)}, bf16[2,576,512]{2,1,0:T(8,128)(2,1)}) custom-call(s32[1]{0:T(128)} %bitcast.place_ref.refs_0_, s32[2]{0:T(128)} %refs_1_.3, bf16[2,576,512]{2,1,0:T(8,128)(2,1)} %bitcast.20, bf16[2,576,512]{2,1,0:T(8,128)(2,1)} %bitcast.22, ...), custom_call_target="tpu_custom_call", output_to_operand_aliasing={{1}: (12, {})} | custom-call | flops 4000000000 | bytes 1024 | tf_op jit(solution)/shard_map/input_backward/pallas_call | solution.py:598
  169.2 1.4 collective-permute-done.28
  170.6 1.4 maximum_select_fusion.1.refs_5_.own_hbm
  172.1 3.6 %unpack_attention.1 = (f32[576,576]{1,0:T(8,128)}, f32[192,576]{1,0:T(8,128)}, f32[192,576]{1,0:T(8,128)}, f32[576]{0:T(1024)}) custom-call(s32[1]{0:T(128)} %bitcast.place_ref.refs_0_, bf16[2304,128]{1,0:T(8,128)(2,1)} %copy-done.4, bf16[2304,128]{1,0:T(8,128)(2,1)} %collective-permute-done.27.refs_2_, ...), custom_call_target="tpu_custom_call" | custom-call | flops 3000000000 | bytes 1024 | tf_op jit(solution)/shard_map/unpack_attention/pallas_call | solution.py:790
  175.7 0.4 collective-permute-done.29
  176.1 0.4 maximum_select_fusion.own_hbm
  176.5 0.2 collective-permute-start.30
  176.7 4.4 %unpack_mlp.2 = (f32[576,1536]{1,0:T(8,128)}, f32[576,1536]{1,0:T(8,128)}, f32[576,1536]{1,0:T(8,128)}) custom-call(s32[1]{0:T(128)} %bitcast.place_ref.refs_0_, bf16[5376,128]{1,0:T(8,128)(2,1)} %maximum_select_fusion.1.refs_5_.own_hbm, bf16[5376,128]{1,0:T(8,128)(2,1)} %collective-permute-done.31.got_hbm), custom_call_target="tpu_custom_call" | custom-call | flops 4000000000 | bytes 1024 | tf_op jit(solution)/shard_map/unpack_mlp/pallas_call | solution.py:750
  181.2 1.2 copy-done.7
  182.4 4.8 %unpack_mlp.3 = (f32[576,1536]{1,0:T(8,128)}, f32[576,1536]{1,0:T(8,128)}, f32[576,1536]{1,0:T(8,128)}, f32[576,576]{1,0:T(8,128)}, f32[576]{0:T(1024)}) custom-call(s32[1]{0:T(128)} %bitcast.place_ref.refs_0_, bf16[6656,128]{1,0:T(8,128)(2,1)} %copy-done.1, bf16[6656,128]{1,0:T(8,128)(2,1)} %copy-done.7, ...), custom_call_target="tpu_custom_call", output_to_operand_aliasing={{0}: (3, {}), {1}: (4, {}), {2}: (5, {})} | custom-call | flops 4000000000 | bytes 1024 | tf_op jit(solution)/shard_map/unpack_mlp/pallas_call | solution.py:750
  (57 shorter events, 1.7 us)
Async XLA Ops:
  1.8 5.8 %collective-permute-start = (bf16[576,512]{1,0:T(8,128)(2,1)S(1)}, bf16[576,512]{1,0:T(8,128)(2,1)S(1)}, u32[]{:S(2)}, u32[]{:S(2)}) collective-permute-start(bf16[576,512]{1,0:T(8,128)(2,1)S(1)} %dynamic-slice_bitcast_fusion.1), channel_id=1, source_target_pairs={{0,1},{1,0},{2,3},{3,2},{4,5},{5,4},{6,7},{7,6},{8,9},{9,8},{10,11... | collective-permute-start | bytes 1769480 | tf_op jit(solution)/shard_map/ppermute | solution.py:623
  3.4 4.1 %collective-permute-start.1 = (bf16[576,512]{1,0:T(8,128)(2,1)S(1)}, bf16[576,512]{1,0:T(8,128)(2,1)S(1)}, u32[]{:S(2)}, u32[]{:S(2)}) collective-permute-start(bf16[576,512]{1,0:T(8,128)(2,1)S(1)} %dynamic-slice_bitcast_fusion), channel_id=1, source_target_pairs={{0,1},{1,0},{2,3},{3,2},{4,5},{5,4},{6,7},{7,6},{8,9},{9,8},{10,11... | collective-permute-start | bytes 1769480 | tf_op jit(solution)/shard_map/ppermute | solution.py:623
  7.5 0.8 copy-start.8
  7.5 1.0 copy-start.9
  64.2 10.3 %collective-permute-start.3 = (bf16[5376,128]{1,0:T(8,128)(2,1)}, bf16[5376,128]{1,0:T(8,128)(2,1)S(1)}, u32[]{:S(2)}, u32[]{:S(2)}) collective-permute-start(bf16[5376,128]{1,0:T(8,128)(2,1)} %get-tuple-element.122), channel_id=1, source_target_pairs={{0,1},{1,0},{2,3},{3,2},{4,5},{5,4},{6,7},{7,6},{8,9},{9,8},{10,11... | collective-permute-start | bytes 4128776 | tf_op jit(solution)/shard_map/ppermute | solution.py:623
  64.7 16.9 %collective-permute-start.2 = (bf16[6656,128]{1,0:T(8,128)(2,1)}, bf16[6656,128]{1,0:T(8,128)(2,1)S(1)}, u32[]{:S(2)}, u32[]{:S(2)}) collective-permute-start(bf16[6656,128]{1,0:T(8,128)(2,1)} %get-tuple-element.120), channel_id=1, source_target_pairs={{0,1},{1,0},{2,3},{3,2},{4,5},{5,4},{6,7},{7,6},{8,9},{9,8},{10,11... | collective-permute-start | bytes 5111816 | tf_op jit(solution)/shard_map/ppermute | solution.py:623
  74.5 1.1 copy-start.2
  75.6 5.9 %copy-start = (bf16[6656,128]{1,0:T(8,128)(2,1)S(1)}, bf16[6656,128]{1,0:T(8,128)(2,1)}, u32[]{:S(2)}) copy-start(bf16[6656,128]{1,0:T(8,128)(2,1)} %get-tuple-element.125) | copy-start | bytes 5111812
  78.7 15.3 %collective-permute-start.5 = (bf16[2688,128]{1,0:T(8,128)(2,1)}, bf16[2688,128]{1,0:T(8,128)(2,1)}, u32[]{:S(2)}, u32[]{:S(2)}) collective-permute-start(bf16[2688,128]{1,0:T(8,128)(2,1)} %get-tuple-element.200), channel_id=1, source_target_pairs={{0,2},{1,5},{2,0},{3,7},{4,6},{5,1},{6,4},{7,3},{8,10},{9,13},{10,... | collective-permute-start | bytes 2064392 | tf_op jit(solution)/shard_map/ppermute | solution.py:652
  82.9 16.4 %collective-permute-start.4 = (bf16[3328,128]{1,0:T(8,128)(2,1)}, bf16[3328,128]{1,0:T(8,128)(2,1)S(1)}, u32[]{:S(2)}, u32[]{:S(2)}) collective-permute-start(bf16[3328,128]{1,0:T(8,128)(2,1)} %get-tuple-element.198.refs_12_), channel_id=1, source_target_pairs={{0,4},{1,9},{2,6},{3,11},{4,0},{5,13},{6,2},{7,15},{8,12},{9,1},{1... | collective-permute-start | bytes 2555912 | tf_op jit(solution)/shard_map/ppermute | solution.py:652
  96.1 15.2 %collective-permute-start.7 = (bf16[1344,128]{1,0:T(8,128)(2,1)}, bf16[1344,128]{1,0:T(8,128)(2,1)S(1)}, u32[]{:S(2)}, u32[]{:S(2)}) collective-permute-start(bf16[1344,128]{1,0:T(8,128)(2,1)} %get-tuple-element.204), channel_id=1, source_target_pairs={{0,4},{1,9},{2,6},{3,11},{4,0},{5,13},{6,2},{7,15},{8,12},{9,1},{1... | collective-permute-start | bytes 1032200 | tf_op jit(solution)/shard_map/ppermute | solution.py:652
  99.5 1.9 %copy-start.5 = (bf16[1664,128]{1,0:T(8,128)(2,1)}, bf16[1664,128]{1,0:T(8,128)(2,1)S(1)}, u32[]{:S(2)}) copy-start(bf16[1664,128]{1,0:T(8,128)(2,1)S(1)} %get-tuple-element.202.refs_12_) | copy-start | bytes 1277956
  99.5 12.5 %collective-permute-start.6 = (bf16[1664,128]{1,0:T(8,128)(2,1)S(1)}, bf16[1664,128]{1,0:T(8,128)(2,1)S(1)}, u32[]{:S(2)}, u32[]{:S(2)}) collective-permute-start(bf16[1664,128]{1,0:T(8,128)(2,1)S(1)} %get-tuple-element.202.refs_12_), channel_id=1, source_target_pairs={{0,8},{1,3},{2,10},{3,1},{4,12},{5,7},{6,14},{7,5},{8,0},{9,11},{1... | collective-permute-start | bytes 1277960 | tf_op jit(solution)/shard_map/ppermute | solution.py:652
  111.3 7.4 %collective-permute-start.10 = (bf16[2304,128]{1,0:T(8,128)(2,1)}, bf16[2304,128]{1,0:T(8,128)(2,1)S(1)}, u32[]{:S(2)}, u32[]{:S(2)}) collective-permute-start(bf16[2304,128]{1,0:T(8,128)(2,1)} %get-tuple-element.143), channel_id=1, source_target_pairs={{0,1},{1,0},{2,3},{3,2},{4,5},{5,4},{6,7},{7,6},{8,9},{9,8},{10,11... | collective-permute-start | bytes 1769480 | tf_op jit(solution)/shard_map/ppermute | solution.py:623
  111.5 8.1 %collective-permute-start.13 = (bf16[672,128]{1,0:T(8,128)(2,1)S(1)}, bf16[672,128]{1,0:T(8,128)(2,1)S(1)}, u32[]{:S(2)}, u32[]{:S(2)}) collective-permute-start(bf16[672,128]{1,0:T(8,128)(2,1)S(1)} %get-tuple-element.210), channel_id=1, source_target_pairs={{0,8},{1,17},{2,10},{3,19},{4,12},{5,21},{6,14},{7,23},{8,0},{9,25... | collective-permute-start | bytes 516104 | tf_op jit(solution)/shard_map/ppermute | solution.py:652
  112.1 1.6 copy-start.6
  112.1 10.1 %collective-permute-start.12 = (bf16[832,128]{1,0:T(8,128)(2,1)S(1)}, bf16[832,128]{1,0:T(8,128)(2,1)S(1)}, u32[]{:S(2)}, u32[]{:S(2)}) collective-permute-start(bf16[832,128]{1,0:T(8,128)(2,1)S(1)} %get-tuple-element.208.refs_10_), channel_id=1, source_target_pairs={{0,2},{1,5},{2,0},{3,7},{4,6},{5,1},{6,4},{7,3},{8,10},{9,13},{10,... | collective-permute-start | bytes 638984 | tf_op jit(solution)/shard_map/ppermute | solution.py:652
  113.7 5.0 %copy-start.3 = (bf16[2304,128]{1,0:T(8,128)(2,1)S(1)}, bf16[2304,128]{1,0:T(8,128)(2,1)}, u32[]{:S(2)}) copy-start(bf16[2304,128]{1,0:T(8,128)(2,1)} %get-tuple-element.144) | copy-start | bytes 1769476
  118.9 7.7 %collective-permute-start.11 = (bf16[1152,128]{1,0:T(8,128)(2,1)S(1)}, bf16[1152,128]{1,0:T(8,128)(2,1)S(1)}, u32[]{:S(2)}, u32[]{:S(2)}) collective-permute-start(bf16[1152,128]{1,0:T(8,128)(2,1)S(1)} %get-tuple-element.205), channel_id=1, source_target_pairs={{0,2},{1,5},{2,0},{3,7},{4,6},{5,1},{6,4},{7,3},{8,10},{9,13},{10,... | collective-permute-start | bytes 884744 | tf_op jit(solution)/shard_map/ppermute | solution.py:652
  119.6 8.7 %collective-permute-start.16 = (bf16[336,128]{1,0:T(8,128)(2,1)S(1)}, bf16[336,128]{1,0:T(8,128)(2,1)S(1)}, u32[]{:S(2)}, u32[]{:S(2)}) collective-permute-start(bf16[336,128]{1,0:T(8,128)(2,1)S(1)} %get-tuple-element.216), channel_id=1, source_target_pairs={{0,16},{1,3},{2,18},{3,1},{4,20},{5,7},{6,22},{7,5},{8,24},{9,11},... | collective-permute-start | bytes 258056 | tf_op jit(solution)/shard_map/ppermute | solution.py:652
  122.3 8.7 %collective-permute-start.15 = (bf16[416,128]{1,0:T(8,128)(2,1)S(1)}, bf16[416,128]{1,0:T(8,128)(2,1)S(1)}, u32[]{:S(2)}, u32[]{:S(2)}) collective-permute-start(bf16[416,128]{1,0:T(8,128)(2,1)S(1)} %get-tuple-element.214), channel_id=1, source_target_pairs={{0,16},{1,17},{2,18},{3,19},{4,20},{5,21},{6,22},{7,23},{8,24},{9,... | collective-permute-start | bytes 319496 | tf_op jit(solution)/shard_map/ppermute | solution.py:652
  126.7 5.2 %collective-permute-start.14 = (bf16[576,128]{1,0:T(8,128)(2,1)S(1)}, bf16[576,128]{1,0:T(8,128)(2,1)S(1)}, u32[]{:S(2)}, u32[]{:S(2)}) collective-permute-start(bf16[576,128]{1,0:T(8,128)(2,1)S(1)} %get-tuple-element.211), channel_id=1, source_target_pairs={{0,4},{1,3},{2,6},{3,1},{4,0},{5,7},{6,2},{7,5},{8,12},{9,11},{10,... | collective-permute-start | bytes 442376 | tf_op jit(solution)/shard_map/ppermute | solution.py:652
  128.3 8.0 %collective-permute-start.19 = (bf16[336,128]{1,0:T(8,128)(2,1)S(1)}, bf16[336,128]{1,0:T(8,128)(2,1)S(1)}, u32[]{:S(2)}, u32[]{:S(2)}) collective-permute-start(bf16[336,128]{1,0:T(8,128)(2,1)S(1)} %add_convert_fusion.22), channel_id=1, source_target_pairs={{0,16},{1,3},{2,18},{3,1},{4,20},{5,7},{6,22},{7,5},{8,24},{9,11},... | collective-permute-start | bytes 258056 | tf_op jit(solution)/shard_map/ppermute | solution.py:652
  131.1 9.7 %collective-permute-start.18 = (bf16[416,128]{1,0:T(8,128)(2,1)S(1)}, bf16[416,128]{1,0:T(8,128)(2,1)S(1)}, u32[]{:S(2)}, u32[]{:S(2)}) collective-permute-start(bf16[416,128]{1,0:T(8,128)(2,1)S(1)} %add_convert_fusion.19), channel_id=1, source_target_pairs={{0,16},{1,17},{2,18},{3,19},{4,20},{5,21},{6,22},{7,23},{8,24},{9,... | collective-permute-start | bytes 319496 | tf_op jit(solution)/shard_map/ppermute | solution.py:652
  131.9 9.0 %collective-permute-start.17 = (bf16[576,128]{1,0:T(8,128)(2,1)S(1)}, bf16[576,128]{1,0:T(8,128)(2,1)S(1)}, u32[]{:S(2)}, u32[]{:S(2)}) collective-permute-start(bf16[576,128]{1,0:T(8,128)(2,1)S(1)} %add_convert_fusion.16), channel_id=1, source_target_pairs={{0,8},{1,9},{2,10},{3,11},{4,12},{5,13},{6,14},{7,15},{8,0},{9,1},... | collective-permute-start | bytes 442376 | tf_op jit(solution)/shard_map/ppermute | solution.py:652
  136.4 8.5 %collective-permute-start.22 = (bf16[672,128]{1,0:T(8,128)(2,1)S(1)}, bf16[672,128]{1,0:T(8,128)(2,1)S(1)}, u32[]{:S(2)}, u32[]{:S(2)}) collective-permute-start(bf16[672,128]{1,0:T(8,128)(2,1)S(1)} %maximum_select_fusion.9), channel_id=1, source_target_pairs={{0,8},{1,17},{2,10},{3,19},{4,12},{5,21},{6,14},{7,23},{8,0},{9,25... | collective-permute-start | bytes 516104 | tf_op jit(solution)/shard_map/ppermute | solution.py:652
  140.9 5.9 %collective-permute-start.21 = (bf16[832,128]{1,0:T(8,128)(2,1)S(1)}, bf16[832,128]{1,0:T(8,128)(2,1)S(1)}, u32[]{:S(2)}, u32[]{:S(2)}) collective-permute-start(bf16[832,128]{1,0:T(8,128)(2,1)S(1)} %maximum_select_fusion.8), channel_id=1, source_target_pairs={{0,2},{1,5},{2,0},{3,7},{4,6},{5,1},{6,4},{7,3},{8,10},{9,13},{10,... | collective-permute-start | bytes 638984 | tf_op jit(solution)/shard_map/ppermute | solution.py:652
  141.0 6.4 %collective-permute-start.20 = (bf16[576,128]{1,0:T(8,128)(2,1)S(1)}, bf16[576,128]{1,0:T(8,128)(2,1)S(1)}, u32[]{:S(2)}, u32[]{:S(2)}) collective-permute-start(bf16[576,128]{1,0:T(8,128)(2,1)S(1)} %add_convert_fusion.15), channel_id=1, source_target_pairs={{0,16},{1,17},{2,18},{3,19},{4,20},{5,21},{6,22},{7,23},{8,24},{9,... | collective-permute-start | bytes 442376 | tf_op jit(solution)/shard_map/ppermute | solution.py:652
  147.5 5.2 %collective-permute-start.23 = (bf16[576,128]{1,0:T(8,128)(2,1)S(1)}, bf16[576,128]{1,0:T(8,128)(2,1)S(1)}, u32[]{:S(2)}, u32[]{:S(2)}) collective-permute-start(bf16[576,128]{1,0:T(8,128)(2,1)S(1)} %add_convert_fusion.14), channel_id=1, source_target_pairs={{0,4},{1,3},{2,6},{3,1},{4,0},{5,7},{6,2},{7,5},{8,12},{9,11},{10,... | collective-permute-start | bytes 442376 | tf_op jit(solution)/shard_map/ppermute | solution.py:652
  148.3 10.1 %collective-permute-start.26 = (bf16[1344,128]{1,0:T(8,128)(2,1)S(1)}, bf16[1344,128]{1,0:T(8,128)(2,1)S(1)}, u32[]{:S(2)}, u32[]{:S(2)}) collective-permute-start(bf16[1344,128]{1,0:T(8,128)(2,1)S(1)} %maximum_select_fusion.6), channel_id=1, source_target_pairs={{0,4},{1,9},{2,6},{3,11},{4,0},{5,13},{6,2},{7,15},{8,12},{9,1},{1... | collective-permute-start | bytes 1032200 | tf_op jit(solution)/shard_map/ppermute | solution.py:652
  149.6 13.6 %collective-permute-start.9 = (bf16[576,512]{1,0:T(8,128)(2,1)}, bf16[576,512]{1,0:T(8,128)(2,1)}, u32[]{:S(2)}, u32[]{:S(2)}) collective-permute-start(bf16[576,512]{1,0:T(8,128)(2,1)} %get-tuple-element.140), channel_id=1, source_target_pairs={{0,1},{1,0},{2,3},{3,2},{4,5},{5,4},{6,7},{7,6},{8,9},{9,8},{10,11... | collective-permute-start | bytes 1769480 | tf_op jit(solution)/shard_map/ppermute | solution.py:623
  149.6 13.6 %collective-permute-start.8 = (bf16[576,512]{1,0:T(8,128)(2,1)}, bf16[576,512]{1,0:T(8,128)(2,1)}, u32[]{:S(2)}, u32[]{:S(2)}) collective-permute-start(bf16[576,512]{1,0:T(8,128)(2,1)} %input_backward.2), channel_id=1, source_target_pairs={{0,1},{1,0},{2,3},{3,2},{4,5},{5,4},{6,7},{7,6},{8,9},{9,8},{10,11... | collective-permute-start | bytes 1769480 | tf_op jit(solution)/shard_map/ppermute | solution.py:623
  150.1 11.6 %collective-permute-start.25 = (bf16[1664,128]{1,0:T(8,128)(2,1)S(1)}, bf16[1664,128]{1,0:T(8,128)(2,1)S(1)}, u32[]{:S(2)}, u32[]{:S(2)}) collective-permute-start(bf16[1664,128]{1,0:T(8,128)(2,1)S(1)} %maximum_select_fusion.5), channel_id=1, source_target_pairs={{0,8},{1,3},{2,10},{3,1},{4,12},{5,7},{6,14},{7,5},{8,0},{9,11},{1... | collective-permute-start | bytes 1277960 | tf_op jit(solution)/shard_map/ppermute | solution.py:652
  152.8 10.1 %collective-permute-start.24 = (bf16[1152,128]{1,0:T(8,128)(2,1)S(1)}, bf16[1152,128]{1,0:T(8,128)(2,1)S(1)}, u32[]{:S(2)}, u32[]{:S(2)}) collective-permute-start(bf16[1152,128]{1,0:T(8,128)(2,1)S(1)} %maximum_select_fusion.7), channel_id=1, source_target_pairs={{0,2},{1,5},{2,0},{3,7},{4,6},{5,1},{6,4},{7,3},{8,10},{9,13},{10,... | collective-permute-start | bytes 884744 | tf_op jit(solution)/shard_map/ppermute | solution.py:652
  158.6 12.0 %collective-permute-start.28 = (bf16[2688,128]{1,0:T(8,128)(2,1)S(1)}, bf16[2688,128]{1,0:T(8,128)(2,1)S(1)}, u32[]{:S(2)}, u32[]{:S(2)}) collective-permute-start(bf16[2688,128]{1,0:T(8,128)(2,1)S(1)} %maximum_select_fusion.3), channel_id=1, source_target_pairs={{0,2},{1,5},{2,0},{3,7},{4,6},{5,1},{6,4},{7,3},{8,10},{9,13},{10,... | collective-permute-start | bytes 2064392 | tf_op jit(solution)/shard_map/ppermute | solution.py:652
  162.0 14.1 %collective-permute-start.29 = (bf16[3328,128]{1,0:T(8,128)(2,1)S(1)}, bf16[3328,128]{1,0:T(8,128)(2,1)S(1)}, u32[]{:S(2)}, u32[]{:S(2)}) collective-permute-start(bf16[3328,128]{1,0:T(8,128)(2,1)S(1)} %maximum_select_fusion.2), channel_id=1, source_target_pairs={{0,4},{1,9},{2,6},{3,11},{4,0},{5,13},{6,2},{7,15},{8,12},{9,1},{1... | collective-permute-start | bytes 2555912 | tf_op jit(solution)/shard_map/ppermute | solution.py:652
  163.1 0.8 copy-start.4
  163.1 9.0 %collective-permute-start.27 = (bf16[2304,128]{1,0:T(8,128)(2,1)S(1)}, bf16[2304,128]{1,0:T(8,128)(2,1)}, u32[]{:S(2)}, u32[]{:S(2)}) collective-permute-start(bf16[2304,128]{1,0:T(8,128)(2,1)S(1)} %maximum_select_fusion.4.refs_13_.refs_1_), channel_id=1, source_target_pairs={{0,1},{1,0},{2,3},{3,2},{4,5},{5,4},{6,7},{7,6},{8,9},{9,8},{10,11... | collective-permute-start | bytes 1769480 | tf_op jit(solution)/shard_map/ppermute | solution.py:623
  172.1 4.6 %collective-permute-start.31 = (bf16[5376,128]{1,0:T(8,128)(2,1)}, bf16[5376,128]{1,0:T(8,128)(2,1)}, u32[]{:S(2)}, u32[]{:S(2)}) collective-permute-start(bf16[5376,128]{1,0:T(8,128)(2,1)} %maximum_select_fusion.1.refs_5_.own_hbm), channel_id=1, source_target_pairs={{0,1},{1,0},{2,3},{3,2},{4,5},{5,4},{6,7},{7,6},{8,9},{9,8},{10,11... | collective-permute-start | bytes 4128776 | tf_op jit(solution)/shard_map/ppermute | solution.py:623
  176.5 4.6 %copy-start.1 = (bf16[6656,128]{1,0:T(8,128)(2,1)}, bf16[6656,128]{1,0:T(8,128)(2,1)S(1)}, u32[]{:S(2)}) copy-start(bf16[6656,128]{1,0:T(8,128)(2,1)S(1)} %maximum_select_fusion.own_hbm) | copy-start | bytes 5111812
  176.5 4.6 %collective-permute-start.30 = (bf16[6656,128]{1,0:T(8,128)(2,1)S(1)}, bf16[6656,128]{1,0:T(8,128)(2,1)S(1)}, u32[]{:S(2)}, u32[]{:S(2)}) collective-permute-start(bf16[6656,128]{1,0:T(8,128)(2,1)S(1)} %maximum_select_fusion.own_hbm), channel_id=1, source_target_pairs={{0,1},{1,0},{2,3},{3,2},{4,5},{5,4},{6,7},{7,6},{8,9},{9,8},{10,11... | collective-permute-start | bytes 5111816 | tf_op jit(solution)/shard_map/ppermute | solution.py:623
  181.2 1.2 copy-start.7

commit v3 on v2

--- a/solution.py
+++ b/solution.py
@@ -868,8 +868,7 @@
         True, place, skip, tokens, cotangent, gh, parts, wqkv_n, gain_one, (grad_got, result_got, res_own), line.after()
     )
     line.last = grad_x
-    a_sum.advance(line)
-    for chain in (a_sum, c_sum):
+    for chain in (c_sum, a_sum):
         while not chain.done:
             chain.advance(line)
     dq, dkt, dvt, dgain_one = unpack_last(place, c_sum.keep, c_sum.got, wqkv_t, gain_line, line.after())

time: 190 us -> 190 us (level)
  no operation moved by 1% of the time
where the time goes in v3:
time: 190 us; the launch traced here: 187 us
  Pallas kernels  112 us (59%)
  starting transfers between devices  34 us (18%)
  waiting for transfers between devices  23.6 us (12%)
  other arithmetic  10.3 us (5%)
  local copies, waits for them, and re-layouts  6.21 us (3%)
    pallas_call x1, Pallas kernels, layer(): pl.pallas_call(layer_kernel, grid_spec=pltpu.PrefetchScalarGridSpec(num_s...  55.6 us
    ppermute x22, starting transfers between devices, swap(): return lax.ppermute(array, ('wide', 'narrow'), pairs)  32 us
    pallas_call x3, Pallas kernels, back(): pl.pallas_call(without(functools.partial(back_kernel, g), inputs, tuple(p...  29.2 us
    ppermute x22, waiting for transfers between devices, swap(): return lax.ppermute(array, ('wide', 'narrow'), pairs)  23.6 us
    pallas_call x2, Pallas kernels, last(): pl.pallas_call(without(kernel, 10 + len(gots), after), grid_spec=pltpu.Pr...  10.3 us
    pallas_call x2, Pallas kernels, unpack(): pl.pallas_call(functools.partial(unpack_kernel, chain), grid_spec=pltpu.P...  9.17 us
    convert_element_type x10, other arithmetic, part(): return (a + b).astype(bf16)  7.27 us
    pallas_call x1, Pallas kernels, prelude(): pl.pallas_call(prelude_kernel, out_shape=[jax.ShapeDtypeStruct((KVH * PER...  4.01 us
  transfers between devices with their start and end apart: 32, of which 13 were waited for; matrix products, arithmetic and copies ran while one was open for 6% of the time, Pallas kernels for 28%

profile of v3, /device:TPU:0, one launch (start us, length us, event | category | flops | bytes accessed | tf_op | source)
XLA Modules:
  0.0 187.3 jit_solution(9716274142557227997)
XLA Ops:
  0.6 1.1 dynamic-slice_bitcast_fusion.1
  1.8 0.5 collective-permute-start
  2.3 1.1 dynamic-slice_bitcast_fusion
  3.5 4.0 %prelude.1 = (bf16[960,576]{1,0:T(8,128)(2,1)}, bf16[576,960]{1,0:T(8,128)(2,1)}, bf16[576,576]{1,0:T(8,128)(2,1)}, f32[576,128]{1,0:T(8,128)}, f32[576,128]{1,0:T(8,128)}, /*index=5*/f32[1,576]{1,0:T(1,128)}) custom-call(bf16[576,576]{1,0:T(8,128)(2,1)} %wq_ref.1, bf16[192,576]{1,0:T(8,128)(2,1)} %bitcast.24, bf16[192,576]{1,0:T(8,128)(2,1)} %bitcast.25, ...), custom_call_target="tpu_custom_call" | custom-call | flops 4000000000 | bytes 1024 | tf_op jit(solution)/shard_map/prelude/pallas_call | solution.py:113
  7.5 0.8 copy-done.8
  8.3 0.2 copy-done.9
  8.5 55.6 %layer_forward.1 = (bf16[576,1024]{1,0:T(8,128)(2,1)}, bf16[192,1024]{1,0:T(8,128)(2,1)}, bf16[3,1024,64]{2,1,0:T(8,128)(2,1)}, bf16[4,9,1024,256]{3,2,1,0:T(8,1...) custom-call(s32[1]{0:T(128)} %bitcast.place_ref.refs_0_, ...), custom_call_target="tpu_custom_call" | custom-call | flops 49999998976 | bytes 1024 | tf_op jit(solution)/shard_map/layer_forward/pallas_call | solution.py:384
  64.2 0.5 collective-permute-start.3
  64.8 9.7 %attention_backward.3 = (bf16[320,1024]{1,0:T(8,128)(2,1)}, bf16[2304,128]{1,0:T(8,128)(2,1)}, bf16[2304,128]{1,0:T(8,128)(2,1)}) custom-call(s32[1]{0:T(128)} %bitcast.place_ref.refs_0_, bf16[4,9,1024,256]{3,2,1,0:T(8,128)(2,1)} %get-tuple-element.109.refs_1_, bf16[576,1024]{1,0:T(8,128)(2,1)} %get-tuple-element.110.refs_2_, ...), custom_call_target="tpu_custom_call" | custom-call | flops 8999999488 | bytes 1024 | tf_op jit(solution)/shard_map/attention_backward/pallas_call | solution.py:498
  74.5 1.1 copy-done.2
  75.6 3.1 %add_convert_fusion.2 = (bf16[2688,128]{1,0:T(8,128)(2,1)S(1)}, bf16[2688,128]{1,0:T(8,128)(2,1)}) fusion(bf16[5376,128]{1,0:T(8,128)(2,1)} %copy-done.2, s32[]{:T(128)S(6)} %select_n.204, bf16[5376,128]{1,0:T(8,128)(2,1)} %get-tuple-element.123, s32[]{:T(128)S(6)} %select_n.200), kind=kLoop, calls=%fused_computation.4 | loop fusion | flops 2752512 | bytes 4128776 | tf_op jit(solution)/shard_map/convert_element_type | solution.py:667
  78.7 2.8 %collective-permute-start.5 = (bf16[2688,128]{1,0:T(8,128)(2,1)}, bf16[2688,128]{1,0:T(8,128)(2,1)}, u32[]{:S(2)}, u32[]{:S(2)}) collective-permute-start(bf16[2688,128]{1,0:T(8,128)(2,1)} %get-tuple-element.200), channel_id=1, source_target_pairs={{0,2},{1,5},{2,0},{3,7},{4,6},{5,1},{6,4},{7,3},{8,10},{9,13},{10,... | collective-permute-start | bytes 2064392 | tf_op jit(solution)/shard_map/ppermute | solution.py:652
  81.5 1.3 add_convert_fusion
  82.9 1.5 collective-permute-start.4
  84.4 9.6 %attention_backward.4 = (bf16[320,1024]{1,0:T(8,128)(2,1)}, bf16[2304,128]{1,0:T(8,128)(2,1)}, bf16[2304,128]{1,0:T(8,128)(2,1)}) custom-call(s32[1]{0:T(128)} %bitcast.place_ref.refs_0_, bf16[4,9,1024,256]{3,2,1,0:T(8,128)(2,1)} %get-tuple-element.109.refs_1_, ...), custom_call_target="tpu_custom_call", output_to_operand_aliasing={{1}: (10, {}), {2}: (11, {})} | custom-call | flops 8999999488 | bytes 1024 | tf_op jit(solution)/shard_map/attention_backward/pallas_call | solution.py:498
  94.1 2.0 %add_convert_fusion.6 = (bf16[1344,128]{1,0:T(8,128)(2,1)S(1)}, bf16[1344,128]{1,0:T(8,128)(2,1)}) fusion(bf16[2688,128]{1,0:T(8,128)(2,1)} %collective-permute-done.5, s32[]{:T(128)S(6)} %select_n.209, bf16[2688,128]{1,0:T(8,128)(2,1)S(1)} %get-tuple-element.130, s32[]{:T(128)S(6)} %select_n.205), kind=kLoop, calls=%fused_computation.10 | loop fusion | flops 1376256 | bytes 2064392 | tf_op jit(solution)/shard_map/convert_element_type | solution.py:667
  96.1 0.5 collective-permute-start.7
  96.6 2.7 %collective-permute-done.4 = bf16[3328,128]{1,0:T(8,128)(2,1)S(1)} collective-permute-done((bf16[3328,128]{1,0:T(8,128)(2,1)}, bf16[3328,128]{1,0:T(8,128)(2,1)S(1)}, u32[]{:S(2)}, u32[]{:S(2)}) %collective-permute-start.4) | collective-permute-done | bytes 852000 | tf_op jit(solution)/shard_map/ppermute | solution.py:652
  99.3 0.2 add_convert_fusion.4
  99.5 1.9 collective-permute-start.6
  101.4 9.9 %attention_backward.5 = (bf16[320,1024]{1,0:T(8,128)(2,1)}, bf16[2304,128]{1,0:T(8,128)(2,1)}, bf16[2304,128]{1,0:T(8,128)(2,1)}) custom-call(s32[1]{0:T(128)} %bitcast.place_ref.refs_0_, bf16[4,9,1024,256]{3,2,1,0:T(8,128)(2,1)} %get-tuple-element.109.refs_1_, ...), custom_call_target="tpu_custom_call", output_to_operand_aliasing={{1}: (10, {}), {2}: (11, {})} | custom-call | flops 8999999488 | bytes 1024 | tf_op jit(solution)/shard_map/attention_backward/pallas_call | solution.py:498
  111.5 0.5 collective-permute-start.13
  112.1 1.6 collective-permute-start.12
  113.7 5.0 %input_backward.2 = bf16[576,512]{1,0:T(8,128)(2,1)} custom-call(s32[1]{0:T(128)} %bitcast.place_ref.refs_0_, s32[2]{0:T(128)} %refs_1_.3, bf16[576,512]{1,0:T(8,128)(2,1)} %copy-done.8, bf16[576,512]{1,0:T(8,128)(2,1)} %copy-done.9, f32[576,1024]{1,0:T(8,128)} %get-tuple-element.108.refs_4_, bf16[320,1024]{1,0:T(8,128)(2,1)} %get-tuple-element.116.refs_5_, ...), custom_call_target="tpu_custom_call" | custom-call | flops 4000000000 | bytes 1024 | tf_op jit(solution)/shard_map/input_backward/pallas_call | solution.py:598
  118.7 0.2 add_convert_fusion.8
  118.9 0.7 collective-permute-start.11
  119.6 2.7 %collective-permute-start.16 = (bf16[336,128]{1,0:T(8,128)(2,1)S(1)}, bf16[336,128]{1,0:T(8,128)(2,1)S(1)}, u32[]{:S(2)}, u32[]{:S(2)}) collective-permute-start(bf16[336,128]{1,0:T(8,128)(2,1)S(1)} %get-tuple-element.216), channel_id=1, source_target_pairs={{0,16},{1,3},{2,18},{3,1},{4,20},{5,7},{6,22},{7,5},{8,24},{9,11},... | collective-permute-start | bytes 258056 | tf_op jit(solution)/shard_map/ppermute | solution.py:652
  122.3 0.4 collective-permute-start.15
  122.7 3.9 %collective-permute-done.11 = bf16[1152,128]{1,0:T(8,128)(2,1)S(1)} collective-permute-done((bf16[1152,128]{1,0:T(8,128)(2,1)S(1)}, bf16[1152,128]{1,0:T(8,128)(2,1)S(1)}, u32[]{:S(2)}, u32[]{:S(2)}) %collective-permute-start.11) | collective-permute-done | bytes 294944 | tf_op jit(solution)/shard_map/ppermute | solution.py:652
  126.7 1.6 collective-permute-start.14
  128.3 1.9 collective-permute-start.19
  130.2 0.9 collective-permute-done.15
  131.1 0.3 collective-permute-start.18
  131.4 0.5 collective-permute-done.14
  131.9 2.1 %collective-permute-start.17 = (bf16[576,128]{1,0:T(8,128)(2,1)S(1)}, bf16[576,128]{1,0:T(8,128)(2,1)S(1)}, u32[]{:S(2)}, u32[]{:S(2)}) collective-permute-start(bf16[576,128]{1,0:T(8,128)(2,1)S(1)} %add_convert_fusion.16), channel_id=1, source_target_pairs={{0,8},{1,9},{2,10},{3,11},{4,12},{5,13},{6,14},{7,15},{8,0},{9,1},... | collective-permute-start | bytes 442376 | tf_op jit(solution)/shard_map/ppermute | solution.py:652
  134.0 2.3 %collective-permute-done.19 = bf16[336,128]{1,0:T(8,128)(2,1)S(1)} collective-permute-done((bf16[336,128]{1,0:T(8,128)(2,1)S(1)}, bf16[336,128]{1,0:T(8,128)(2,1)S(1)}, u32[]{:S(2)}, u32[]{:S(2)}) %collective-permute-start.19) | collective-permute-done | bytes 86048 | tf_op jit(solution)/shard_map/ppermute | solution.py:652
  136.4 1.7 collective-permute-start.22
  138.1 2.8 %collective-permute-done.18 = bf16[416,128]{1,0:T(8,128)(2,1)S(1)} collective-permute-done((bf16[416,128]{1,0:T(8,128)(2,1)S(1)}, bf16[416,128]{1,0:T(8,128)(2,1)S(1)}, u32[]{:S(2)}, u32[]{:S(2)}) %collective-permute-start.18) | collective-permute-done | bytes 106528 | tf_op jit(solution)/shard_map/ppermute | solution.py:652
  141.0 1.8 collective-permute-start.20
  142.8 2.1 %collective-permute-done.22 = bf16[672,128]{1,0:T(8,128)(2,1)S(1)} collective-permute-done((bf16[672,128]{1,0:T(8,128)(2,1)S(1)}, bf16[672,128]{1,0:T(8,128)(2,1)S(1)}, u32[]{:S(2)}, u32[]{:S(2)}) %collective-permute-start.22) | collective-permute-done | bytes 172064 | tf_op jit(solution)/shard_map/ppermute | solution.py:652
  145.0 1.8 collective-permute-done.21
  146.9 0.5 collective-permute-done.20
  147.5 0.8 collective-permute-start.23
  148.3 1.2 collective-permute-start.26
  149.6 0.5 collective-permute-start.8
  150.1 2.2 %collective-permute-start.25 = (bf16[1664,128]{1,0:T(8,128)(2,1)S(1)}, bf16[1664,128]{1,0:T(8,128)(2,1)S(1)}, u32[]{:S(2)}, u32[]{:S(2)}) collective-permute-start(bf16[1664,128]{1,0:T(8,128)(2,1)S(1)} %maximum_select_fusion.5), channel_id=1, source_target_pairs={{0,8},{1,3},{2,10},{3,1},{4,12},{5,7},{6,14},{7,5},{8,0},{9,11},{1... | collective-permute-start | bytes 1277960 | tf_op jit(solution)/shard_map/ppermute | solution.py:652
  152.3 0.4 collective-permute-done.23
  152.8 1.7 collective-permute-start.24
  154.6 3.9 %collective-permute-done.26 = bf16[1344,128]{1,0:T(8,128)(2,1)S(1)} collective-permute-done((bf16[1344,128]{1,0:T(8,128)(2,1)S(1)}, bf16[1344,128]{1,0:T(8,128)(2,1)S(1)}, u32[]{:S(2)}, u32[]{:S(2)}) %collective-permute-start.26) | collective-permute-done | bytes 344096 | tf_op jit(solution)/shard_map/ppermute | solution.py:652
  158.5 0.2 maximum_select_fusion.3
  158.6 3.1 %collective-permute-start.28 = (bf16[2688,128]{1,0:T(8,128)(2,1)S(1)}, bf16[2688,128]{1,0:T(8,128)(2,1)S(1)}, u32[]{:S(2)}, u32[]{:S(2)}) collective-permute-start(bf16[2688,128]{1,0:T(8,128)(2,1)S(1)} %maximum_select_fusion.3), channel_id=1, source_target_pairs={{0,2},{1,5},{2,0},{3,7},{4,6},{5,1},{6,4},{7,3},{8,10},{9,13},{10,... | collective-permute-start | bytes 2064392 | tf_op jit(solution)/shard_map/ppermute | solution.py:652
  161.7 0.2 maximum_select_fusion.2
  162.0 0.9 collective-permute-start.29
  163.2 0.7 copy-done.4
  163.9 5.3 %input_backward.3 = (bf16[2,576,512]{2,1,0:T(8,128)(2,1)}, bf16[2,576,512]{2,1,0:T(8,128)(2,1)}) custom-call(s32[1]{0:T(128)} %bitcast.place_ref.refs_0_, s32[2]{0:T(128)} %refs_1_.3, bf16[2,576,512]{2,1,0:T(8,128)(2,1)} %bitcast.20, bf16[2,576,512]{2,1,0:T(8,128)(2,1)} %bitcast.22, ...), custom_call_target="tpu_custom_call", output_to_operand_aliasing={{1}: (12, {})} | custom-call | flops 4000000000 | bytes 1024 | tf_op jit(solution)/shard_map/input_backward/pallas_call | solution.py:598
  169.2 1.4 collective-permute-done.28
  170.6 1.4 maximum_select_fusion.1.refs_5_.own_hbm
  172.1 3.6 %unpack_attention.1 = (f32[576,576]{1,0:T(8,128)}, f32[192,576]{1,0:T(8,128)}, f32[192,576]{1,0:T(8,128)}, f32[576]{0:T(1024)}) custom-call(s32[1]{0:T(128)} %bitcast.place_ref.refs_0_, bf16[2304,128]{1,0:T(8,128)(2,1)} %copy-done.4, bf16[2304,128]{1,0:T(8,128)(2,1)} %collective-permute-done.27.refs_2_, ...), custom_call_target="tpu_custom_call" | custom-call | flops 3000000000 | bytes 1024 | tf_op jit(solution)/shard_map/unpack_attention/pallas_call | solution.py:790
  175.7 0.4 collective-permute-done.29
  176.1 0.4 maximum_select_fusion.own_hbm
  176.5 0.2 collective-permute-start.30
  176.7 4.4 %unpack_mlp.2 = (f32[576,1536]{1,0:T(8,128)}, f32[576,1536]{1,0:T(8,128)}, f32[576,1536]{1,0:T(8,128)}) custom-call(s32[1]{0:T(128)} %bitcast.place_ref.refs_0_, bf16[5376,128]{1,0:T(8,128)(2,1)} %maximum_select_fusion.1.refs_5_.own_hbm, bf16[5376,128]{1,0:T(8,128)(2,1)} %collective-permute-done.31.got_hbm), custom_call_target="tpu_custom_call" | custom-call | flops 4000000000 | bytes 1024 | tf_op jit(solution)/shard_map/unpack_mlp/pallas_call | solution.py:750
  181.2 1.2 copy-done.7
  182.4 4.8 %unpack_mlp.3 = (f32[576,1536]{1,0:T(8,128)}, f32[576,1536]{1,0:T(8,128)}, f32[576,1536]{1,0:T(8,128)}, f32[576,576]{1,0:T(8,128)}, f32[576]{0:T(1024)}) custom-call(s32[1]{0:T(128)} %bitcast.place_ref.refs_0_, bf16[6656,128]{1,0:T(8,128)(2,1)} %copy-done.1, bf16[6656,128]{1,0:T(8,128)(2,1)} %copy-done.7, ...), custom_call_target="tpu_custom_call", output_to_operand_aliasing={{0}: (3, {}), {1}: (4, {}), {2}: (5, {})} | custom-call | flops 4000000000 | bytes 1024 | tf_op jit(solution)/shard_map/unpack_mlp/pallas_call | solution.py:750
  (57 shorter events, 1.7 us)
Async XLA Ops:
  1.8 5.8 %collective-permute-start = (bf16[576,512]{1,0:T(8,128)(2,1)S(1)}, bf16[576,512]{1,0:T(8,128)(2,1)S(1)}, u32[]{:S(2)}, u32[]{:S(2)}) collective-permute-start(bf16[576,512]{1,0:T(8,128)(2,1)S(1)} %dynamic-slice_bitcast_fusion.1), channel_id=1, source_target_pairs={{0,1},{1,0},{2,3},{3,2},{4,5},{5,4},{6,7},{7,6},{8,9},{9,8},{10,11... | collective-permute-start | bytes 1769480 | tf_op jit(solution)/shard_map/ppermute | solution.py:623
  3.4 4.1 %collective-permute-start.1 = (bf16[576,512]{1,0:T(8,128)(2,1)S(1)}, bf16[576,512]{1,0:T(8,128)(2,1)S(1)}, u32[]{:S(2)}, u32[]{:S(2)}) collective-permute-start(bf16[576,512]{1,0:T(8,128)(2,1)S(1)} %dynamic-slice_bitcast_fusion), channel_id=1, source_target_pairs={{0,1},{1,0},{2,3},{3,2},{4,5},{5,4},{6,7},{7,6},{8,9},{9,8},{10,11... | collective-permute-start | bytes 1769480 | tf_op jit(solution)/shard_map/ppermute | solution.py:623
  7.5 0.8 copy-start.8
  7.5 1.0 copy-start.9
  64.2 10.3 %collective-permute-start.3 = (bf16[5376,128]{1,0:T(8,128)(2,1)}, bf16[5376,128]{1,0:T(8,128)(2,1)S(1)}, u32[]{:S(2)}, u32[]{:S(2)}) collective-permute-start(bf16[5376,128]{1,0:T(8,128)(2,1)} %get-tuple-element.122), channel_id=1, source_target_pairs={{0,1},{1,0},{2,3},{3,2},{4,5},{5,4},{6,7},{7,6},{8,9},{9,8},{10,11... | collective-permute-start | bytes 4128776 | tf_op jit(solution)/shard_map/ppermute | solution.py:623
  64.7 16.9 %collective-permute-start.2 = (bf16[6656,128]{1,0:T(8,128)(2,1)}, bf16[6656,128]{1,0:T(8,128)(2,1)S(1)}, u32[]{:S(2)}, u32[]{:S(2)}) collective-permute-start(bf16[6656,128]{1,0:T(8,128)(2,1)} %get-tuple-element.120), channel_id=1, source_target_pairs={{0,1},{1,0},{2,3},{3,2},{4,5},{5,4},{6,7},{7,6},{8,9},{9,8},{10,11... | collective-permute-start | bytes 5111816 | tf_op jit(solution)/shard_map/ppermute | solution.py:623
  74.5 1.1 copy-start.2
  75.6 5.9 %copy-start = (bf16[6656,128]{1,0:T(8,128)(2,1)S(1)}, bf16[6656,128]{1,0:T(8,128)(2,1)}, u32[]{:S(2)}) copy-start(bf16[6656,128]{1,0:T(8,128)(2,1)} %get-tuple-element.125) | copy-start | bytes 5111812
  78.7 15.3 %collective-permute-start.5 = (bf16[2688,128]{1,0:T(8,128)(2,1)}, bf16[2688,128]{1,0:T(8,128)(2,1)}, u32[]{:S(2)}, u32[]{:S(2)}) collective-permute-start(bf16[2688,128]{1,0:T(8,128)(2,1)} %get-tuple-element.200), channel_id=1, source_target_pairs={{0,2},{1,5},{2,0},{3,7},{4,6},{5,1},{6,4},{7,3},{8,10},{9,13},{10,... | collective-permute-start | bytes 2064392 | tf_op jit(solution)/shard_map/ppermute | solution.py:652
  82.9 16.4 %collective-permute-start.4 = (bf16[3328,128]{1,0:T(8,128)(2,1)}, bf16[3328,128]{1,0:T(8,128)(2,1)S(1)}, u32[]{:S(2)}, u32[]{:S(2)}) collective-permute-start(bf16[3328,128]{1,0:T(8,128)(2,1)} %get-tuple-element.198.refs_12_), channel_id=1, source_target_pairs={{0,4},{1,9},{2,6},{3,11},{4,0},{5,13},{6,2},{7,15},{8,12},{9,1},{1... | collective-permute-start | bytes 2555912 | tf_op jit(solution)/shard_map/ppermute | solution.py:652
  96.1 15.2 %collective-permute-start.7 = (bf16[1344,128]{1,0:T(8,128)(2,1)}, bf16[1344,128]{1,0:T(8,128)(2,1)S(1)}, u32[]{:S(2)}, u32[]{:S(2)}) collective-permute-start(bf16[1344,128]{1,0:T(8,128)(2,1)} %get-tuple-element.204), channel_id=1, source_target_pairs={{0,4},{1,9},{2,6},{3,11},{4,0},{5,13},{6,2},{7,15},{8,12},{9,1},{1... | collective-permute-start | bytes 1032200 | tf_op jit(solution)/shard_map/ppermute | solution.py:652
  99.5 1.9 %copy-start.5 = (bf16[1664,128]{1,0:T(8,128)(2,1)}, bf16[1664,128]{1,0:T(8,128)(2,1)S(1)}, u32[]{:S(2)}) copy-start(bf16[1664,128]{1,0:T(8,128)(2,1)S(1)} %get-tuple-element.202.refs_12_) | copy-start | bytes 1277956
  99.5 12.5 %collective-permute-start.6 = (bf16[1664,128]{1,0:T(8,128)(2,1)S(1)}, bf16[1664,128]{1,0:T(8,128)(2,1)S(1)}, u32[]{:S(2)}, u32[]{:S(2)}) collective-permute-start(bf16[1664,128]{1,0:T(8,128)(2,1)S(1)} %get-tuple-element.202.refs_12_), channel_id=1, source_target_pairs={{0,8},{1,3},{2,10},{3,1},{4,12},{5,7},{6,14},{7,5},{8,0},{9,11},{1... | collective-permute-start | bytes 1277960 | tf_op jit(solution)/shard_map/ppermute | solution.py:652
  111.3 7.4 %collective-permute-start.10 = (bf16[2304,128]{1,0:T(8,128)(2,1)}, bf16[2304,128]{1,0:T(8,128)(2,1)S(1)}, u32[]{:S(2)}, u32[]{:S(2)}) collective-permute-start(bf16[2304,128]{1,0:T(8,128)(2,1)} %get-tuple-element.143), channel_id=1, source_target_pairs={{0,1},{1,0},{2,3},{3,2},{4,5},{5,4},{6,7},{7,6},{8,9},{9,8},{10,11... | collective-permute-start | bytes 1769480 | tf_op jit(solution)/shard_map/ppermute | solution.py:623
  111.5 8.1 %collective-permute-start.13 = (bf16[672,128]{1,0:T(8,128)(2,1)S(1)}, bf16[672,128]{1,0:T(8,128)(2,1)S(1)}, u32[]{:S(2)}, u32[]{:S(2)}) collective-permute-start(bf16[672,128]{1,0:T(8,128)(2,1)S(1)} %get-tuple-element.210), channel_id=1, source_target_pairs={{0,8},{1,17},{2,10},{3,19},{4,12},{5,21},{6,14},{7,23},{8,0},{9,25... | collective-permute-start | bytes 516104 | tf_op jit(solution)/shard_map/ppermute | solution.py:652
  112.1 1.6 copy-start.6
  112.1 10.1 %collective-permute-start.12 = (bf16[832,128]{1,0:T(8,128)(2,1)S(1)}, bf16[832,128]{1,0:T(8,128)(2,1)S(1)}, u32[]{:S(2)}, u32[]{:S(2)}) collective-permute-start(bf16[832,128]{1,0:T(8,128)(2,1)S(1)} %get-tuple-element.208.refs_10_), channel_id=1, source_target_pairs={{0,2},{1,5},{2,0},{3,7},{4,6},{5,1},{6,4},{7,3},{8,10},{9,13},{10,... | collective-permute-start | bytes 638984 | tf_op jit(solution)/shard_map/ppermute | solution.py:652
  113.7 5.0 %copy-start.3 = (bf16[2304,128]{1,0:T(8,128)(2,1)S(1)}, bf16[2304,128]{1,0:T(8,128)(2,1)}, u32[]{:S(2)}) copy-start(bf16[2304,128]{1,0:T(8,128)(2,1)} %get-tuple-element.144) | copy-start | bytes 1769476
  118.9 7.7 %collective-permute-start.11 = (bf16[1152,128]{1,0:T(8,128)(2,1)S(1)}, bf16[1152,128]{1,0:T(8,128)(2,1)S(1)}, u32[]{:S(2)}, u32[]{:S(2)}) collective-permute-start(bf16[1152,128]{1,0:T(8,128)(2,1)S(1)} %get-tuple-element.205), channel_id=1, source_target_pairs={{0,2},{1,5},{2,0},{3,7},{4,6},{5,1},{6,4},{7,3},{8,10},{9,13},{10,... | collective-permute-start | bytes 884744 | tf_op jit(solution)/shard_map/ppermute | solution.py:652
  119.6 8.7 %collective-permute-start.16 = (bf16[336,128]{1,0:T(8,128)(2,1)S(1)}, bf16[336,128]{1,0:T(8,128)(2,1)S(1)}, u32[]{:S(2)}, u32[]{:S(2)}) collective-permute-start(bf16[336,128]{1,0:T(8,128)(2,1)S(1)} %get-tuple-element.216), channel_id=1, source_target_pairs={{0,16},{1,3},{2,18},{3,1},{4,20},{5,7},{6,22},{7,5},{8,24},{9,11},... | collective-permute-start | bytes 258056 | tf_op jit(solution)/shard_map/ppermute | solution.py:652
  122.3 8.7 %collective-permute-start.15 = (bf16[416,128]{1,0:T(8,128)(2,1)S(1)}, bf16[416,128]{1,0:T(8,128)(2,1)S(1)}, u32[]{:S(2)}, u32[]{:S(2)}) collective-permute-start(bf16[416,128]{1,0:T(8,128)(2,1)S(1)} %get-tuple-element.214), channel_id=1, source_target_pairs={{0,16},{1,17},{2,18},{3,19},{4,20},{5,21},{6,22},{7,23},{8,24},{9,... | collective-permute-start | bytes 319496 | tf_op jit(solution)/shard_map/ppermute | solution.py:652
  126.7 5.2 %collective-permute-start.14 = (bf16[576,128]{1,0:T(8,128)(2,1)S(1)}, bf16[576,128]{1,0:T(8,128)(2,1)S(1)}, u32[]{:S(2)}, u32[]{:S(2)}) collective-permute-start(bf16[576,128]{1,0:T(8,128)(2,1)S(1)} %get-tuple-element.211), channel_id=1, source_target_pairs={{0,4},{1,3},{2,6},{3,1},{4,0},{5,7},{6,2},{7,5},{8,12},{9,11},{10,... | collective-permute-start | bytes 442376 | tf_op jit(solution)/shard_map/ppermute | solution.py:652
  128.3 8.0 %collective-permute-start.19 = (bf16[336,128]{1,0:T(8,128)(2,1)S(1)}, bf16[336,128]{1,0:T(8,128)(2,1)S(1)}, u32[]{:S(2)}, u32[]{:S(2)}) collective-permute-start(bf16[336,128]{1,0:T(8,128)(2,1)S(1)} %add_convert_fusion.22), channel_id=1, source_target_pairs={{0,16},{1,3},{2,18},{3,1},{4,20},{5,7},{6,22},{7,5},{8,24},{9,11},... | collective-permute-start | bytes 258056 | tf_op jit(solution)/shard_map/ppermute | solution.py:652
  131.1 9.7 %collective-permute-start.18 = (bf16[416,128]{1,0:T(8,128)(2,1)S(1)}, bf16[416,128]{1,0:T(8,128)(2,1)S(1)}, u32[]{:S(2)}, u32[]{:S(2)}) collective-permute-start(bf16[416,128]{1,0:T(8,128)(2,1)S(1)} %add_convert_fusion.19), channel_id=1, source_target_pairs={{0,16},{1,17},{2,18},{3,19},{4,20},{5,21},{6,22},{7,23},{8,24},{9,... | collective-permute-start | bytes 319496 | tf_op jit(solution)/shard_map/ppermute | solution.py:652
  131.9 9.0 %collective-permute-start.17 = (bf16[576,128]{1,0:T(8,128)(2,1)S(1)}, bf16[576,128]{1,0:T(8,128)(2,1)S(1)}, u32[]{:S(2)}, u32[]{:S(2)}) collective-permute-start(bf16[576,128]{1,0:T(8,128)(2,1)S(1)} %add_convert_fusion.16), channel_id=1, source_target_pairs={{0,8},{1,9},{2,10},{3,11},{4,12},{5,13},{6,14},{7,15},{8,0},{9,1},... | collective-permute-start | bytes 442376 | tf_op jit(solution)/shard_map/ppermute | solution.py:652
  136.4 8.5 %collective-permute-start.22 = (bf16[672,128]{1,0:T(8,128)(2,1)S(1)}, bf16[672,128]{1,0:T(8,128)(2,1)S(1)}, u32[]{:S(2)}, u32[]{:S(2)}) collective-permute-start(bf16[672,128]{1,0:T(8,128)(2,1)S(1)} %maximum_select_fusion.9), channel_id=1, source_target_pairs={{0,8},{1,17},{2,10},{3,19},{4,12},{5,21},{6,14},{7,23},{8,0},{9,25... | collective-permute-start | bytes 516104 | tf_op jit(solution)/shard_map/ppermute | solution.py:652
  140.9 5.9 %collective-permute-start.21 = (bf16[832,128]{1,0:T(8,128)(2,1)S(1)}, bf16[832,128]{1,0:T(8,128)(2,1)S(1)}, u32[]{:S(2)}, u32[]{:S(2)}) collective-permute-start(bf16[832,128]{1,0:T(8,128)(2,1)S(1)} %maximum_select_fusion.8), channel_id=1, source_target_pairs={{0,2},{1,5},{2,0},{3,7},{4,6},{5,1},{6,4},{7,3},{8,10},{9,13},{10,... | collective-permute-start | bytes 638984 | tf_op jit(solution)/shard_map/ppermute | solution.py:652
  141.0 6.4 %collective-permute-start.20 = (bf16[576,128]{1,0:T(8,128)(2,1)S(1)}, bf16[576,128]{1,0:T(8,128)(2,1)S(1)}, u32[]{:S(2)}, u32[]{:S(2)}) collective-permute-start(bf16[576,128]{1,0:T(8,128)(2,1)S(1)} %add_convert_fusion.15), channel_id=1, source_target_pairs={{0,16},{1,17},{2,18},{3,19},{4,20},{5,21},{6,22},{7,23},{8,24},{9,... | collective-permute-start | bytes 442376 | tf_op jit(solution)/shard_map/ppermute | solution.py:652
  147.5 5.2 %collective-permute-start.23 = (bf16[576,128]{1,0:T(8,128)(2,1)S(1)}, bf16[576,128]{1,0:T(8,128)(2,1)S(1)}, u32[]{:S(2)}, u32[]{:S(2)}) collective-permute-start(bf16[576,128]{1,0:T(8,128)(2,1)S(1)} %add_convert_fusion.14), channel_id=1, source_target_pairs={{0,4},{1,3},{2,6},{3,1},{4,0},{5,7},{6,2},{7,5},{8,12},{9,11},{10,... | collective-permute-start | bytes 442376 | tf_op jit(solution)/shard_map/ppermute | solution.py:652
  148.3 10.1 %collective-permute-start.26 = (bf16[1344,128]{1,0:T(8,128)(2,1)S(1)}, bf16[1344,128]{1,0:T(8,128)(2,1)S(1)}, u32[]{:S(2)}, u32[]{:S(2)}) collective-permute-start(bf16[1344,128]{1,0:T(8,128)(2,1)S(1)} %maximum_select_fusion.6), channel_id=1, source_target_pairs={{0,4},{1,9},{2,6},{3,11},{4,0},{5,13},{6,2},{7,15},{8,12},{9,1},{1... | collective-permute-start | bytes 1032200 | tf_op jit(solution)/shard_map/ppermute | solution.py:652
  149.6 13.6 %collective-permute-start.9 = (bf16[576,512]{1,0:T(8,128)(2,1)}, bf16[576,512]{1,0:T(8,128)(2,1)}, u32[]{:S(2)}, u32[]{:S(2)}) collective-permute-start(bf16[576,512]{1,0:T(8,128)(2,1)} %get-tuple-element.140), channel_id=1, source_target_pairs={{0,1},{1,0},{2,3},{3,2},{4,5},{5,4},{6,7},{7,6},{8,9},{9,8},{10,11... | collective-permute-start | bytes 1769480 | tf_op jit(solution)/shard_map/ppermute | solution.py:623
  149.6 13.6 %collective-permute-start.8 = (bf16[576,512]{1,0:T(8,128)(2,1)}, bf16[576,512]{1,0:T(8,128)(2,1)}, u32[]{:S(2)}, u32[]{:S(2)}) collective-permute-start(bf16[576,512]{1,0:T(8,128)(2,1)} %input_backward.2), channel_id=1, source_target_pairs={{0,1},{1,0},{2,3},{3,2},{4,5},{5,4},{6,7},{7,6},{8,9},{9,8},{10,11... | collective-permute-start | bytes 1769480 | tf_op jit(solution)/shard_map/ppermute | solution.py:623
  150.1 11.6 %collective-permute-start.25 = (bf16[1664,128]{1,0:T(8,128)(2,1)S(1)}, bf16[1664,128]{1,0:T(8,128)(2,1)S(1)}, u32[]{:S(2)}, u32[]{:S(2)}) collective-permute-start(bf16[1664,128]{1,0:T(8,128)(2,1)S(1)} %maximum_select_fusion.5), channel_id=1, source_target_pairs={{0,8},{1,3},{2,10},{3,1},{4,12},{5,7},{6,14},{7,5},{8,0},{9,11},{1... | collective-permute-start | bytes 1277960 | tf_op jit(solution)/shard_map/ppermute | solution.py:652
  152.8 10.1 %collective-permute-start.24 = (bf16[1152,128]{1,0:T(8,128)(2,1)S(1)}, bf16[1152,128]{1,0:T(8,128)(2,1)S(1)}, u32[]{:S(2)}, u32[]{:S(2)}) collective-permute-start(bf16[1152,128]{1,0:T(8,128)(2,1)S(1)} %maximum_select_fusion.7), channel_id=1, source_target_pairs={{0,2},{1,5},{2,0},{3,7},{4,6},{5,1},{6,4},{7,3},{8,10},{9,13},{10,... | collective-permute-start | bytes 884744 | tf_op jit(solution)/shard_map/ppermute | solution.py:652
  158.6 12.0 %collective-permute-start.28 = (bf16[2688,128]{1,0:T(8,128)(2,1)S(1)}, bf16[2688,128]{1,0:T(8,128)(2,1)S(1)}, u32[]{:S(2)}, u32[]{:S(2)}) collective-permute-start(bf16[2688,128]{1,0:T(8,128)(2,1)S(1)} %maximum_select_fusion.3), channel_id=1, source_target_pairs={{0,2},{1,5},{2,0},{3,7},{4,6},{5,1},{6,4},{7,3},{8,10},{9,13},{10,... | collective-permute-start | bytes 2064392 | tf_op jit(solution)/shard_map/ppermute | solution.py:652
  162.0 14.1 %collective-permute-start.29 = (bf16[3328,128]{1,0:T(8,128)(2,1)S(1)}, bf16[3328,128]{1,0:T(8,128)(2,1)S(1)}, u32[]{:S(2)}, u32[]{:S(2)}) collective-permute-start(bf16[3328,128]{1,0:T(8,128)(2,1)S(1)} %maximum_select_fusion.2), channel_id=1, source_target_pairs={{0,4},{1,9},{2,6},{3,11},{4,0},{5,13},{6,2},{7,15},{8,12},{9,1},{1... | collective-permute-start | bytes 2555912 | tf_op jit(solution)/shard_map/ppermute | solution.py:652
  163.1 0.8 copy-start.4
  163.1 9.0 %collective-permute-start.27 = (bf16[2304,128]{1,0:T(8,128)(2,1)S(1)}, bf16[2304,128]{1,0:T(8,128)(2,1)}, u32[]{:S(2)}, u32[]{:S(2)}) collective-permute-start(bf16[2304,128]{1,0:T(8,128)(2,1)S(1)} %maximum_select_fusion.4.refs_13_.refs_1_), channel_id=1, source_target_pairs={{0,1},{1,0},{2,3},{3,2},{4,5},{5,4},{6,7},{7,6},{8,9},{9,8},{10,11... | collective-permute-start | bytes 1769480 | tf_op jit(solution)/shard_map/ppermute | solution.py:623
  172.1 4.6 %collective-permute-start.31 = (bf16[5376,128]{1,0:T(8,128)(2,1)}, bf16[5376,128]{1,0:T(8,128)(2,1)}, u32[]{:S(2)}, u32[]{:S(2)}) collective-permute-start(bf16[5376,128]{1,0:T(8,128)(2,1)} %maximum_select_fusion.1.refs_5_.own_hbm), channel_id=1, source_target_pairs={{0,1},{1,0},{2,3},{3,2},{4,5},{5,4},{6,7},{7,6},{8,9},{9,8},{10,11... | collective-permute-start | bytes 4128776 | tf_op jit(solution)/shard_map/ppermute | solution.py:623
  176.5 4.6 %copy-start.1 = (bf16[6656,128]{1,0:T(8,128)(2,1)}, bf16[6656,128]{1,0:T(8,128)(2,1)S(1)}, u32[]{:S(2)}) copy-start(bf16[6656,128]{1,0:T(8,128)(2,1)S(1)} %maximum_select_fusion.own_hbm) | copy-start | bytes 5111812
  176.5 4.6 %collective-permute-start.30 = (bf16[6656,128]{1,0:T(8,128)(2,1)S(1)}, bf16[6656,128]{1,0:T(8,128)(2,1)S(1)}, u32[]{:S(2)}, u32[]{:S(2)}) collective-permute-start(bf16[6656,128]{1,0:T(8,128)(2,1)S(1)} %maximum_select_fusion.own_hbm), channel_id=1, source_target_pairs={{0,1},{1,0},{2,3},{3,2},{4,5},{5,4},{6,7},{7,6},{8,9},{9,8},{10,11... | collective-permute-start | bytes 5111816 | tf_op jit(solution)/shard_map/ppermute | solution.py:623
  181.2 1.2 copy-start.7
